TPU v7x, 512 devices: a whole 4x8x8 slice. The times are simulated.
512 devices in a mesh: group: 16 (over y, core), owner: 32 (over z, x).
Axes of the slice: x: 4, y: 8, z: 8, core: 2. Of those that a mesh axis runs over, the one named last changes fastest.
Arguments:
- embeddings: bfloat16 [65536, 1024], P('owner'), may hold values from -250 to 250
- cluster_of: int32 [65536], P('owner'), may hold values from 0 to 31, as said below
- cluster_owner: int32 [32], replicated, may hold values from 0 to 31, as said below
- slot_of: int32 [65536], P('owner'), may hold values from 0 to 2047, as said below
- pairs: int32 [32, 16, 49, 2], P('owner', 'group'), may hold values from -1 to 47, as said below
Outputs:
- similarity_max: float32 [32, 2048], P('owner', 'group')
Inputs may be any that keep to these rules, and one draw needn't show every extreme that they name: `cluster_owner`: each owner owns exactly one cluster. `cluster_of`: the rows of one index of owner go to one owner in 96 rows, to another in 32 rows and to each other owner in 64 rows; every owner receives exactly 2048 rows. `slot_of`: rows with the same owner have distinct slots. `pairs`: an entry (i, j) names block i of the owner's 16 blocks (slot order) and block j of the owner's wide rows: j < 16 is the previous owner's block j, 16 <= j < 32 its own block j - 16 with i <= j - 16, higher j the next owner's block j - 2 * 16 (owners cyclic). Valid entries stand first in each list, the rest are -1 in both places. No pair is listed twice among one owner's lists. Owner o lists (i, 32 + j) exactly when owner o + 1 lists (j, i). In every owner, a quarter of the indices of group hold 49 valid entries each, and the others share the remaining ones as evenly as possible.
All inputs are finite; a program needn't handle non-finite values.
Results may differ from a plain program's by a relative error of at most 0.00049.
Values may be sent and summed in bfloat16 or wider, within the bound.
No kernel may reach another device: no remote copies, remote signals or barrier semaphores. Data moves between devices by JAX's collectives and lax.ppermute only.
A program may use at most 128 MiB of HBM per device.

v0:
```python
import jax
import jax.numpy as jnp
from jax import lax
from jax.sharding import PartitionSpec as P

BLOCK = 128


batch_width = 8


def with_halo(block, sides, width):
    for axis, dim in sides:
        count = lax.axis_size(axis)
        forward = [(i, i + 1) for i in range(count - 1)]
        forward.append((count - 1, 0))
        backward = [(target, source) for source, target in forward]
        low = lax.ppermute(
            lax.slice_in_dim(block, block.shape[dim] - width, None, axis=dim), axis, forward
        )
        high = lax.ppermute(lax.slice_in_dim(block, 0, width, axis=dim), axis, backward)
        block = jnp.concatenate([low, block, high], axis=dim)
    return block


def tile_batch(maxima, entry_set, live, left_blocks, right_blocks, offset, block_count, col_limit):
    first_block = jnp.where(live, entry_set[:, 0], 0)
    second = jnp.where(live, entry_set[:, 1], offset)
    middle = second - block_count
    inside = jnp.logical_and(live, jnp.logical_and(middle >= 0, middle < col_limit))
    left_rows = left_blocks[first_block]
    right_rows = right_blocks[second - offset]
    scores = lax.dot_general(
        left_rows, right_rows, (((2,), (2,)), ((0,), (0,))), preferred_element_type=jnp.float32
    )
    diagonal = jnp.arange(BLOCK)[:, None] == jnp.arange(BLOCK)[None, :]
    same_block = jnp.logical_and(inside, middle == first_block)
    scores = jnp.where(
        jnp.logical_and(diagonal[None, :, :], same_block[:, None, None]), -2.0, scores
    )
    row_best = jnp.where(live[:, None], jnp.max(scores, axis=2), -2.0)
    col_best = jnp.where(inside[:, None], jnp.max(scores, axis=1), -2.0)
    maxima = maxima.at[first_block].max(row_best)
    return maxima.at[jnp.clip(middle, 0, col_limit - 1)].max(col_best)


def walk_entries(pairs, batch_update, initial):
    entries = pairs.reshape(-1, 2)
    list_len = entries.shape[0]
    padded_len = (list_len + batch_width - 1) // batch_width * batch_width
    entries = jnp.concatenate(
        [entries, jnp.full((padded_len - list_len, 2), -1, jnp.int32)], axis=0
    )
    valid_count = jnp.sum((entries[:, 0] >= 0).astype(jnp.int32))
    turns = (valid_count + batch_width - 1) // batch_width

    def visit_batch(turn, current_max):
        entry_set = lax.dynamic_slice_in_dim(entries, turn * batch_width, batch_width, 0)
        return batch_update(current_max, entry_set, entry_set[:, 0] >= 0)

    return lax.fori_loop(0, turns, visit_batch, initial)


def merge_groups(maxima, share_size):
    merged = lax.pmax(maxima, "group")
    return lax.dynamic_slice_in_dim(merged, lax.axis_index("group") * share_size, share_size, 1)


def on_device(embeddings, cluster_of, cluster_owner, slot_of, pairs):
    owner_count = lax.axis_size("owner")
    group_count = lax.axis_size("group")
    row_count = embeddings.shape[0]
    feat_width = embeddings.shape[1]
    block_count = row_count // BLOCK
    share_size = row_count // group_count
    capacity = 3 * row_count // (2 * owner_count)
    matches = cluster_of[:, None] == jnp.arange(cluster_owner.shape[0], dtype=jnp.int32)[None, :]
    target = jnp.sum(jnp.where(matches, cluster_owner[None, :], 0), axis=1)
    onehot = (target[:, None] == jnp.arange(owner_count, dtype=jnp.int32)[None, :]).astype(
        jnp.int32
    )
    position = jnp.sum((jnp.cumsum(onehot, axis=0) - onehot) * onehot, axis=1)
    outgoing = (
        jnp.zeros((owner_count, capacity, feat_width), jnp.bfloat16)
        .at[target, position]
        .set(embeddings)
    )
    out_slots = jnp.full((owner_count, capacity), -1, jnp.int32).at[target, position].set(slot_of)
    arrived, arrived_slots = (
        lax.all_to_all(outgoing, "owner", split_axis=0, concat_axis=0, tiled=True),
        lax.all_to_all(out_slots, "owner", split_axis=0, concat_axis=0, tiled=True),
    )
    flat_slots = arrived_slots.reshape(-1)
    safe_slot = jnp.where(flat_slots >= 0, flat_slots, row_count)
    placed = (
        jnp.zeros((row_count, feat_width), jnp.bfloat16)
        .at[safe_slot]
        .set(arrived.reshape(-1, feat_width), mode="drop")
    )
    floats = placed.astype(jnp.float32)
    unit_rows = (
        floats * lax.rsqrt(jnp.sum(floats * floats, axis=1, keepdims=True) + 1e-06)
    ).astype(jnp.bfloat16)
    left_blocks = unit_rows.reshape(block_count, BLOCK, feat_width)
    wide_rows = with_halo(unit_rows, (("owner", 0),), row_count)
    right_blocks = wide_rows.reshape(3 * block_count, BLOCK, feat_width)

    def batch_update(current_max, entry_set, live):
        return tile_batch(
            current_max, entry_set, live, left_blocks, right_blocks, 0, block_count, block_count
        )

    initial = jnp.full((block_count, BLOCK), -2.0, jnp.float32)
    maxima = walk_entries(pairs, batch_update, initial)
    result = merge_groups(maxima.reshape(1, row_count), share_size)
    return result


def solution(mesh):
    placed = (P("owner", None), P("owner"), P(), P("owner"), P("owner", "group", None, None))
    return jax.shard_map(
        on_device, mesh=mesh, in_specs=placed, out_specs=P("owner", "group"), check_vma=False
    )
```

profile of v0, /device:TPU:1, one launch (start us, length us, event | category | flops | bytes accessed | tf_op | source)
XLA Modules:
  0.0 450.6 jit_solution(186034596983611543)
XLA Ops:
  0.9 9.1 %reduce-window.6 = s32[32,16,128]{2,1,0:T(8,128)S(1)} reduce-window(s32[32,16,128]{2,1,0:T(8,128)S(1)} %fusion.22, s32[]{:T(128)} %constant.88.clone.1), window={size=1x1x128 pad=0_0x0_0x127_0}, to_apply=%region_2.3 | reduce-window | flops 8323072 | bytes 524292 | tf_op jit(solution)/shard_map/reduce-window
  12.3 8.2 %scatter_custom_fusion.3 = s32[3072]{0:T(1024)S(1)} fusion(s32[2048]{0:T(1024)S(1)} %broadcast_select_fusion, s32[2048]{0:T(1024)} %param.10, s32[]{:T(128)} %constant.90.clone.1), kind=kCustom, calls=%fused_computation.61 | custom fusion | bytes 12800
  21.2 13.7 %all-to-all-start = ((s32[32,1,96]{2,1,0:T(1,128)}), s32[32,1,96]{2,1,0:T(1,128)S(1)}, u32[]{:S(2)}, u32[]{:S(2)}) async-start(s32[32,1,96]{2,1,0:T(1,128)} %all_to_all.9), calls=%async_computation | async-start | bytes 32768 | tf_op jit(solution)/shard_map/all_to_all | solution.py:91
  35.0 14.2 %scatter_custom_fusion.4 = bf16[3072,1024]{1,0:T(8,128)(2,1)} fusion(s32[2048]{0:T(1024)S(1)} %broadcast_select_fusion, bf16[2048,1024]{1,0:T(8,128)(2,1)} %param.7, bf16[]{:T(256)} %constant.94.clone.1), kind=kCustom, calls=%fused_computation.39 | custom fusion | bytes 6291968
  49.2 9.3 %all-to-all-start.1 = ((bf16[32,96,1024]{2,1,0:T(8,128)(2,1)}), bf16[32,96,1024]{2,1,0:T(8,128)(2,1)}, u32[]{:S(2)}, u32[]{:S(2)}) async-start(bf16[32,96,1024]{2,1,0:T(8,128)(2,1)} %bitcast.61), calls=%async_computation.1 | async-start | bytes 12582912 | tf_op jit(solution)/shard_map/all_to_all | solution.py:90
  59.9 134.7 %all-to-all-done.1 = bf16[32,96,1024]{2,1,0:T(8,128)(2,1)} async-done(((bf16[32,96,1024]{2,1,0:T(8,128)(2,1)}), bf16[32,96,1024]{2,1,0:T(8,128)(2,1)}, u32[]{:S(2)}, u32[]{:S(2)}) %all-to-all-start.1) | async-done | bytes 6291488 | tf_op jit(solution)/shard_map/all_to_all | solution.py:90
  194.5 17.6 %scatter_custom_fusion.2 = bf16[2048,1024]{1,0:T(8,128)(2,1)} fusion(s32[3072]{0:T(1024)S(1)} %bitcast.69, bf16[3072,1024]{1,0:T(8,128)(2,1)} %bitcast.16, bf16[]{:T(256)} %constant.94.clone.1), kind=kCustom, calls=%fused_computation.41 | custom fusion | bytes 4194816 | tf_op jit(solution)/shard_map/scatter | solution.py:98
  212.1 3.2 fusion.13
  215.5 2.7 fusion.14
  218.2 6.4 %collective-permute-start = (bf16[2048,1024]{1,0:T(8,128)(2,1)}, bf16[2048,1024]{1,0:T(8,128)(2,1)}, u32[]{:S(2)}, u32[]{:S(2)}) collective-permute-start(bf16[2048,1024]{1,0:T(8,128)(2,1)} %fusion.14), channel_id=1, source_target_pairs={{0,1},{1,2},{2,3},{3,4},{4,5},{5,6},{6,7},{7,8},{8,9},{9,10},{10,1... | collective-permute-start | bytes 12582920 | tf_op jit(solution)/shard_map/ppermute | solution.py:18
  224.6 7.0 %collective-permute-start.1 = (bf16[2048,1024]{1,0:T(8,128)(2,1)}, bf16[2048,1024]{1,0:T(8,128)(2,1)}, u32[]{:S(2)}, u32[]{:S(2)}) collective-permute-start(bf16[2048,1024]{1,0:T(8,128)(2,1)} %fusion.14), channel_id=1, source_target_pairs={{1,0},{2,1},{3,2},{4,3},{5,4},{6,5},{7,6},{8,7},{9,8},{10,9},{11,1... | collective-permute-start | bytes 12582920 | tf_op jit(solution)/shard_map/ppermute | solution.py:21
  233.0 86.4 %collective-permute-done = bf16[2048,1024]{1,0:T(8,128)(2,1)} collective-permute-done((bf16[2048,1024]{1,0:T(8,128)(2,1)}, bf16[2048,1024]{1,0:T(8,128)(2,1)}, u32[]{:S(2)}, u32[]{:S(2)}) %collective-permute-start) | collective-permute-done | bytes 4194336 | tf_op jit(solution)/shard_map/ppermute | solution.py:18
  320.3 11.5 %pad_maximum_fusion = bf16[6144,1024]{1,0:T(8,128)(2,1)} fusion(bf16[2048,1024]{1,0:T(8,128)(2,1)} %collective-permute-done.1, bf16[2048,1024]{1,0:T(8,128)(2,1)} %fusion.14, bf16[2048,1024]{1,0:T(8,128)(2,1)} %collective-permute-done), kind=kLoop, calls=%fused_computation.34 | loop fusion | flops 37748736 | bytes 25165824 | tf_op jit(solution)/shard_map/concatenate | solution.py:22
  331.8 40.3 %while.12 = (s32[]{:T(128)}, f32[16,128]{1,0:T(8,128)S(1)}, s32[]{:T(128)}, s32[56,2]{0,1:T(2,128)S(1)}, bf16[16,128,1024]{2,1,0:T(8,128)(2,1)}, /*index=5*/bf16...) while((s32[]{:T(128)}, f32[16,128]{1,0:T(8,128)S(1)}, ...), condition=%wide.region_14.15_spmd, body=%wide.region_9.14_spmd.sunk | while | flops 268980480 | bytes 12658439 | solution.py:61
  331.9 5.3 %gather_fusion.1 = bf16[8,128,1024]{2,1,0:T(8,128)(2,1)S(1)} fusion(bf16[48,128,1024]{2,1,0:T(8,128)(2,1)} %get-tuple-element.186, s32[1024]{0:T(1024)S(1)} %pad_clamp_fusion.5), kind=kCustom, calls=%fused_computation.1.clone.1 | custom fusion | bytes 4194336 | tf_op jit(solution)/shard_map/while/body/gather | solution.py:32
  337.2 4.2 gather_fusion
  341.4 2.4 fusion.42
  345.3 5.3 %gather_fusion.1 = bf16[8,128,1024]{2,1,0:T(8,128)(2,1)S(1)} fusion(bf16[48,128,1024]{2,1,0:T(8,128)(2,1)} %get-tuple-element.186, s32[1024]{0:T(1024)S(1)} %pad_clamp_fusion.5), kind=kCustom, calls=%fused_computation.1.clone.1 | custom fusion | bytes 4194336 | tf_op jit(solution)/shard_map/while/body/gather | solution.py:32
  350.6 4.2 gather_fusion
  354.9 2.4 fusion.42
  358.8 5.3 %gather_fusion.1 = bf16[8,128,1024]{2,1,0:T(8,128)(2,1)S(1)} fusion(bf16[48,128,1024]{2,1,0:T(8,128)(2,1)} %get-tuple-element.186, s32[1024]{0:T(1024)S(1)} %pad_clamp_fusion.5), kind=kCustom, calls=%fused_computation.1.clone.1 | custom fusion | bytes 4194336 | tf_op jit(solution)/shard_map/while/body/gather | solution.py:32
  364.1 4.2 gather_fusion
  368.3 2.4 fusion.42
  372.1 78.0 %pmax.7 = f32[1,2048]{1,0:T(1,128)S(1)} all-reduce(f32[1,2048]{1,0:T(1,128)S(1)} %bitcast.68), channel_id=1, replica_groups=mesh['group'=16,'owner'=32] {'group'}, use_global_device_ids=true, to_apply=%region_15.16 | all-reduce | flops 2048 | bytes 16384 | tf_op jit(solution)/shard_map/pmax | solution.py:65
  (57 shorter events, 12.0 us)
Async XLA Ops:
  21.2 27.9 %all-to-all-start = ((s32[32,1,96]{2,1,0:T(1,128)}), s32[32,1,96]{2,1,0:T(1,128)S(1)}, u32[]{:S(2)}, u32[]{:S(2)}) async-start(s32[32,1,96]{2,1,0:T(1,128)} %all_to_all.9), calls=%async_computation | async-start | bytes 32768 | tf_op jit(solution)/shard_map/all_to_all | solution.py:91
  49.2 145.3 %all-to-all-start.1 = ((bf16[32,96,1024]{2,1,0:T(8,128)(2,1)}), bf16[32,96,1024]{2,1,0:T(8,128)(2,1)}, u32[]{:S(2)}, u32[]{:S(2)}) async-start(bf16[32,96,1024]{2,1,0:T(8,128)(2,1)} %bitcast.61), calls=%async_computation.1 | async-start | bytes 12582912 | tf_op jit(solution)/shard_map/all_to_all | solution.py:90
  212.1 3.4 copy-start
  215.5 16.1 %copy-start.1 = (s32[1,1,49,2]{2,3,1,0:T(2,128)S(1)}, s32[1,1,49,2]{2,3,1,0:T(2,128)}, u32[]{:S(2)}) copy-start(s32[1,1,49,2]{2,3,1,0:T(2,128)} %param.11) | copy-start | bytes 1180
  218.2 101.1 %collective-permute-start = (bf16[2048,1024]{1,0:T(8,128)(2,1)}, bf16[2048,1024]{1,0:T(8,128)(2,1)}, u32[]{:S(2)}, u32[]{:S(2)}) collective-permute-start(bf16[2048,1024]{1,0:T(8,128)(2,1)} %fusion.14), channel_id=1, source_target_pairs={{0,1},{1,2},{2,3},{3,4},{4,5},{5,6},{6,7},{7,8},{8,9},{9,10},{10,1... | collective-permute-start | bytes 12582920 | tf_op jit(solution)/shard_map/ppermute | solution.py:18
  224.6 95.6 %collective-permute-start.1 = (bf16[2048,1024]{1,0:T(8,128)(2,1)}, bf16[2048,1024]{1,0:T(8,128)(2,1)}, u32[]{:S(2)}, u32[]{:S(2)}) collective-permute-start(bf16[2048,1024]{1,0:T(8,128)(2,1)} %fusion.14), channel_id=1, source_target_pairs={{1,0},{2,1},{3,2},{4,3},{5,4},{6,5},{7,6},{8,7},{9,8},{10,9},{11,1... | collective-permute-start | bytes 12582920 | tf_op jit(solution)/shard_map/ppermute | solution.py:21
where the time goes:
time: 454 us; the launch traced here: 451 us
  waiting for transfers between devices  222 us (49%)
  blocking collectives  78 us (17%)
  local copies, waits for them, and re-layouts  71.1 us (16%)
  starting transfers between devices  36.4 us (8%)
  other arithmetic  35 us (8%)
  matrix products  7.13 us (2%)
    all_to_all x1, waiting for transfers between devices, on_device(): lax.all_to_all(outgoing, 'owner', split_axis=0, concat_axis=0, tiled=True)  135 us
    ppermute x1, waiting for transfers between devices, with_halo(): lax.ppermute(lax.slice_in_dim(block, block.shape[dim] - width, None, axis...  86.4 us
    pmax x1, blocking collectives, merge_groups(): merged = lax.pmax(maxima, 'group')  78 us
    unnamed x6, local copies, waits for them, and re-layouts  22.7 us
    scatter x1, local copies, waits for them, and re-layouts, on_device(): placed = jnp.zeros((row_count, feat_width), jnp.bfloat16).at[safe_slot].s...  17.6 us
    gather x3, local copies, waits for them, and re-layouts, tile_batch(): right_rows = right_blocks[second - offset]  15.8 us
    all_to_all x1, starting transfers between devices, on_device(): lax.all_to_all(out_slots, 'owner', split_axis=0, concat_axis=0, tiled=True)  13.7 us
    gather x3, local copies, waits for them, and re-layouts, tile_batch(): left_rows = left_blocks[first_block]  12.7 us
  transfers between devices with their start and end apart: 4, of which 3 were waited for; matrix products, arithmetic and copies ran while one was open for 4% of the time, Pallas kernels for 0%

commit v1 on v0

v1 whole, which is shorter than its diff:
```python
import jax
import jax.numpy as jnp
from jax import lax
from jax.experimental import pallas as pl
from jax.experimental.pallas import tpu as pltpu
from jax.sharding import PartitionSpec as P

BLOCK = 128
LANES = 128
META = 8
PAY_META = 16
BF16 = jnp.bfloat16
F32 = jnp.float32
I32 = jnp.int32


def iota(shape, dim):
    return lax.broadcasted_iota(I32, shape, dim)


def ones_where(mask):
    return jnp.where(mask, 1.0, 0.0).astype(BF16)


def mm(a, b):
    return jnp.dot(a, b, preferred_element_type=F32)


def mm_nt(a, b):
    return lax.dot_general(a, b, (((1,), (1,)), ((), ())), preferred_element_type=F32)


def mm_tn(a, b):
    return lax.dot_general(a, b, (((0,), (0,)), ((), ())), preferred_element_type=F32)


def send_kernel(n_owner, n_group, cap, pieces, me_ref, cluster_ref, owner_ref, slot_ref, emb_ref, out_ref, emb, wide, sems):
    rows, feat = emb.shape
    chunks = feat // LANES
    step = rows // pieces
    copies = [
        pltpu.make_async_copy(emb_ref.at[pl.ds(i * step, step)], emb.at[pl.ds(i * step, step)], sems.at[i])
        for i in range(pieces)
    ]
    for copy in copies:
        copy.start()
    me = me_ref[0]
    picked = ones_where(iota((n_owner, rows), 0) == cluster_ref[...])
    table = ones_where(iota((n_owner, n_owner), 0) == owner_ref[...])
    to = mm(table, picked).astype(BF16)
    parts = rows // LANES
    stacked = jnp.concatenate([to[:, i * LANES : (i + 1) * LANES] for i in range(parts)], axis=0)
    before = mm(stacked, ones_where(iota((LANES, LANES), 0) < iota((LANES, LANES), 1)))
    totals = mm(stacked, jnp.ones((LANES, LANES), BF16))
    running = jnp.zeros((n_owner, LANES), F32)
    lane_owner = iota((n_owner, LANES), 0).astype(F32)
    place, target = [], []
    for i in range(parts):
        here = stacked[i * n_owner : (i + 1) * n_owner].astype(F32)
        spot = before[i * n_owner : (i + 1) * n_owner] + running
        place.append(jnp.sum(here * spot, axis=0, keepdims=True))
        target.append(jnp.sum(here * lane_owner, axis=0, keepdims=True))
        running = running + totals[i * n_owner : (i + 1) * n_owner]
    place = jnp.concatenate(place, axis=1).astype(I32)
    target = jnp.concatenate(target, axis=1).astype(I32)
    mine = (place & (n_group - 1)) == me
    entry = place // n_group
    goal = jnp.where(mine, target * cap + entry, -1)
    slot = slot_ref[...]
    high = (slot // BLOCK + 1).astype(F32)
    low = (slot & (BLOCK - 1)).astype(F32)
    at_entry = jnp.logical_and(iota((LANES, rows), 0) == entry, mine)
    meta_high = mm_nt(to, jnp.where(at_entry, high, 0.0).astype(BF16)).astype(BF16)
    meta_low = mm_nt(to, jnp.where(at_entry, low, 0.0).astype(BF16)).astype(BF16)
    line = iota((n_owner * META, n_owner), 0)
    peer = iota((n_owner * META, n_owner), 1)
    meta = mm(ones_where(line == peer * META), meta_high) + mm(ones_where(line == peer * META + 1), meta_low)
    out_ref[:, cap * chunks :, :] = meta.reshape(n_owner, META, LANES).astype(BF16)
    select = ones_where(iota((n_owner * cap, rows), 0) == goal)
    total = None
    for i, copy in enumerate(copies):
        copy.wait()
        part = mm(select[:, i * step : (i + 1) * step], emb[pl.ds(i * step, step), :])
        total = part if total is None else total + part
    for k in range(chunks):
        wide[pl.ds(k, n_owner * cap, chunks), :] = total[:, k * LANES : (k + 1) * LANES]
    out_ref[:, : cap * chunks, :] = wide[...].reshape(n_owner, cap * chunks, LANES).astype(BF16)


def receive_kernel(n_owner, cap, feat, in_ref, first_ref, second_ref, out_ref, wide):
    chunks = feat // LANES
    lines = n_owner * cap
    wide[...] = in_ref[:, : cap * chunks, :].astype(F32).reshape(lines * chunks, LANES)
    meta = in_ref[:, cap * chunks :, :].astype(F32).reshape(n_owner * META, LANES).astype(BF16)
    line = iota((lines, n_owner * META), 0)
    source = iota((lines, n_owner * META), 1)
    at_lane = iota((lines, LANES), 1) == lax.rem(iota((lines, LANES), 0), cap)
    high = mm(ones_where(source == line // cap * META), meta)
    low = mm(ones_where(source == line // cap * META + 1), meta)
    ones = jnp.ones((LANES, LANES), BF16)
    high = mm(jnp.where(at_lane, high, 0.0).astype(BF16), ones)
    low = mm(jnp.where(at_lane, low, 0.0).astype(BF16), ones)
    valid = ones_where(high > 0.5)
    earlier = ones_where(iota((lines, lines), 1) < iota((lines, lines), 0))
    place = mm(earlier, valid)
    put = jnp.logical_and(place == iota((lines, BLOCK), 1).astype(F32), high > 0.5)
    put_one = ones_where(put)
    parts = []
    square = None
    for k in range(chunks):
        part = mm_tn(put_one, wide[pl.ds(k, lines, chunks), :].astype(BF16))
        parts.append(part)
        here = part * part
        square = here if square is None else square + here
    scale = lax.rsqrt(jnp.sum(square, axis=1, keepdims=True) + 1e-06)
    for k in range(chunks):
        out_ref[pl.ds(k * BLOCK, BLOCK), :] = (parts[k] * scale).astype(BF16)
    blocks = jnp.sum(jnp.where(put, high, 0.0), axis=0, keepdims=True) - 1.0
    inner = jnp.sum(jnp.where(put, low, 0.0), axis=0, keepdims=True)
    row = iota((PAY_META, LANES), 0)
    numbers = jnp.where(row == 0, blocks, jnp.where(row == 1, inner, 0.0))
    numbers = jnp.where(row == 2, first_ref[...].astype(F32), numbers)
    numbers = jnp.where(row == 3, second_ref[...].astype(F32), numbers)
    out_ref[pl.ds(chunks * BLOCK, PAY_META), :] = numbers.astype(BF16)


def rows_of(ref, start, chunks):
    return jnp.concatenate(
        [ref[pl.ds(start + k * BLOCK, BLOCK), :] for k in range(chunks)], axis=1
    )


def score_kernel(n_group, feat, me_ref, all_ref, own_ref, low_ref, high_ref, out_ref):
    chunks = feat // LANES
    size = feat + PAY_META
    blocks = n_group
    me = me_ref[0]
    numbers = [all_ref[pl.ds(b * size + feat, PAY_META), :].astype(F32) for b in range(blocks)]

    def numbers_row(i):
        return jnp.concatenate([n[i : i + 1, :] for n in numbers], axis=1).astype(I32)

    block_of, inner_of = numbers_row(0), numbers_row(1)
    first, second = numbers_row(2), numbers_row(3)
    total = blocks * LANES
    first_rows = iota((blocks, total), 0)
    wide_rows = iota((3 * blocks, total), 0)
    paired = mm_nt(ones_where(wide_rows == second), ones_where(first_rows == first))
    paired += mm_nt(ones_where(wide_rows == first + blocks), ones_where(first_rows == second - blocks))
    penalty = jnp.where(paired > 0.5, 0.0, -4.0).astype(BF16)
    sources = [low_ref, own_ref, high_ref]
    marks = [r[pl.ds(feat, PAY_META), :].astype(F32)[0:1, :].astype(I32) + n * blocks for n, r in enumerate(sources)]
    marks = jnp.concatenate(marks, axis=1)
    source_one = ones_where(iota((3 * blocks, 3 * BLOCK), 0) == marks)
    bias = mm_tn(source_one, penalty).astype(BF16)
    left = jnp.concatenate([rows_of(r, 0, chunks) for r in sources], axis=0)
    best = []
    pair = 2 * BLOCK
    for b in range(blocks // 2):
        right = jnp.concatenate([rows_of(all_ref, (2 * b + h) * size, chunks) for h in range(2)], axis=0)
        here = ones_where(iota((blocks, pair), 0) == block_of[:, b * pair : (b + 1) * pair])
        scores = mm_nt(left, right) + mm(bias, here)
        own = scores[BLOCK : 2 * BLOCK]
        same = iota((BLOCK, pair), 1) + b * pair == iota((BLOCK, pair), 0) + me * BLOCK
        own = jnp.where(same, -2.0, own)
        top = jnp.maximum(jnp.maximum(scores[:BLOCK], own), scores[2 * BLOCK :])
        best.append(jnp.max(top, axis=0, keepdims=True))
    best = jnp.maximum(jnp.concatenate(best, axis=1), -2.0)
    spread = iota((blocks, total), 0) == block_of
    inner = ones_where(iota((BLOCK, total), 0) == inner_of)
    result = jnp.zeros((blocks, BLOCK), F32)
    rest = best
    for _ in range(3):
        piece = rest.astype(BF16).astype(F32)
        rest = rest - piece
        result += mm_nt(jnp.where(spread, piece, 0.0).astype(BF16), inner)
    out_ref[...] = result


def vmem():
    return pl.BlockSpec(memory_space=pltpu.VMEM)


def smem():
    return pl.BlockSpec(memory_space=pltpu.SMEM)


PARAMS = pltpu.CompilerParams(vmem_limit_bytes=48 * 1024 * 1024)


def on_device(embeddings, cluster_of, cluster_owner, slot_of, pairs):
    n_owner = lax.axis_size("owner")
    n_group = lax.axis_size("group")
    rows, feat = embeddings.shape
    chunks = feat // LANES
    cap = 3 * rows // (2 * n_owner * n_group)
    pieces = 4
    me = lax.axis_index("group").astype(I32).reshape(1)
    lane_rows = cap * chunks + META
    outgoing = pl.pallas_call(
        lambda *refs: send_kernel(n_owner, n_group, cap, pieces, *refs),
        out_shape=jax.ShapeDtypeStruct((n_owner, lane_rows, LANES), BF16),
        in_specs=[smem(), vmem(), vmem(), vmem(), pl.BlockSpec(memory_space=pl.ANY)],
        out_specs=vmem(),
        scratch_shapes=[
            pltpu.VMEM((rows, feat), BF16),
            pltpu.VMEM((n_owner * cap * chunks, LANES), F32),
            pltpu.SemaphoreType.DMA((pieces,)),
        ],
        compiler_params=PARAMS,
        name="send_rows",
    )(me, cluster_of.reshape(1, rows), cluster_owner.reshape(1, n_owner), slot_of.reshape(1, rows), embeddings)
    arrived = lax.all_to_all(outgoing, "owner", split_axis=0, concat_axis=0, tiled=True)
    entries = pairs.reshape(-1, 2)
    listed = jnp.pad(entries.T, ((0, 0), (0, LANES - entries.shape[0])), constant_values=-1)
    payload = pl.pallas_call(
        lambda *refs: receive_kernel(n_owner, cap, feat, *refs),
        out_shape=jax.ShapeDtypeStruct((feat + PAY_META, LANES), BF16),
        in_specs=[vmem(), vmem(), vmem()],
        out_specs=vmem(),
        scratch_shapes=[pltpu.VMEM((n_owner * cap * chunks, LANES), F32)],
        compiler_params=PARAMS,
        name="unit_rows",
    )(arrived, listed[0:1], listed[1:2])
    forward = [(i, (i + 1) % n_owner) for i in range(n_owner)]
    backward = [(b, a) for a, b in forward]
    gathered = lax.all_gather(payload, "group", axis=0, tiled=True)
    low = lax.ppermute(payload, "owner", forward)
    high = lax.ppermute(payload, "owner", backward)
    table = pl.pallas_call(
        lambda *refs: score_kernel(n_group, feat, *refs),
        out_shape=jax.ShapeDtypeStruct((n_group, BLOCK), F32),
        in_specs=[smem(), vmem(), vmem(), vmem(), vmem()],
        out_specs=vmem(),
        compiler_params=PARAMS,
        name="score_rows",
    )(me, gathered, payload, low, high)
    shares = lax.all_to_all(table, "group", split_axis=0, concat_axis=0, tiled=True)
    return jnp.max(shares, axis=0, keepdims=True)


def solution(mesh):
    placed = (P("owner", None), P("owner"), P(), P("owner"), P("owner", "group", None, None))
    return jax.shard_map(
        on_device, mesh=mesh, in_specs=placed, out_specs=P("owner", "group"), check_vma=False
    )
```

time: 454 us -> 114 us (0.25)
  waiting for transfers between devices: 222 us -> 49.3 us
  blocking collectives: 78 us -> 11.5 us
  local copies, waits for them, and re-layouts: 71.1 us -> 6.47 us
  other arithmetic: 35 us -> 0.54 us
  starting transfers between devices: 36.4 us -> 22.4 us
  between operations: 0.85 us -> 13.5 us
  Pallas kernels: 0 us -> 9.64 us
  matrix products: 7.13 us -> 0 us
    all_to_all x1, waiting for transfers between devices: 135 us -> 14.3 us  [on_device(): lax.all_to_all(outgoing, 'owner', split_axis=0, concat_axis=0, tiled=True)]
    ppermute x2, waiting for transfers between devices: 87.3 us -> 3.65 us  [the longest x1 2.07 us: on_device(): low = lax.ppermute(payload, 'owner', forward)]
    pmax x1 -> x0, blocking collectives: 78 us -> none  [merge_groups(): merged = lax.pmax(maxima, 'group')]
    all_gather x0 -> x1, waiting for transfers between devices: none -> 31.3 us  [on_device(): gathered = lax.all_gather(payload, 'group', axis=0, tiled=True)]
    gather x6 -> x0, local copies, waits for them, and re-layouts: 28.4 us -> none  [the longest x3 15.8 us: tile_batch(): right_rows = right_blocks[second - offset]]
    scatter x1 -> x0, local copies, waits for them, and re-layouts: 17.6 us -> none  [on_device(): placed = jnp.zeros((row_count, feat_width), jnp.bfloat16).at[safe_slot].s...]
    unnamed x6 -> x12, local copies, waits for them, and re-layouts: 22.7 us -> 6.46 us
    all_to_all x1 -> x0, starting transfers between devices: 13.7 us -> none  [on_device(): lax.all_to_all(out_slots, 'owner', split_axis=0, concat_axis=0, tiled=True)]
  transfers between devices with their start and end apart: 4 -> 4, of which waited for: 3 -> 4; matrix products, arithmetic and copies ran while one was open for 4% -> 0% of each run, Pallas kernels for 0% -> 0%
where the time goes in v1:
time: 114 us; the launch traced here: 113 us
  waiting for transfers between devices  49.3 us (43%)
  starting transfers between devices  22.4 us (20%)
  between operations  13.5 us (12%)
  blocking collectives  11.5 us (10%)
  Pallas kernels  9.64 us (8%)
  local copies, waits for them, and re-layouts  6.47 us (6%)
    all_gather x1, waiting for transfers between devices, on_device(): gathered = lax.all_gather(payload, 'group', axis=0, tiled=True)  31.3 us
    all_to_all x1, waiting for transfers between devices, on_device(): lax.all_to_all(outgoing, 'owner', split_axis=0, concat_axis=0, tiled=True)  14.3 us
    all_to_all x1, starting transfers between devices, on_device(): lax.all_to_all(outgoing, 'owner', split_axis=0, concat_axis=0, tiled=True)  13.7 us
    all_to_all x1, blocking collectives, on_device(): lax.all_to_all(table, 'group', split_axis=0, concat_axis=0, tiled=True)  11.5 us
    unnamed x12, local copies, waits for them, and re-layouts  6.46 us
    ppermute x1, starting transfers between devices, on_device(): high = lax.ppermute(payload, 'owner', backward)  5.26 us
    pallas_call x1, Pallas kernels, on_device(): pl.pallas_call(lambda *refs: score_kernel(n_group, feat, *refs), out_shap...  4.52 us
    pallas_call x1, Pallas kernels, on_device(): pl.pallas_call(lambda *refs: send_kernel(n_owner, n_group, cap, pieces, *...  3.48 us
  transfers between devices with their start and end apart: 4, of which 4 were waited for; matrix products, arithmetic and copies ran while one was open for 0% of the time, Pallas kernels for 0%

profile of v1, /device:TPU:1, one launch (start us, length us, event | category | flops | bytes accessed | tf_op | source)
XLA Modules:
  0.0 113.2 jit_solution(7899948948773590347)
XLA Ops:
  6.5 0.0 copy-start.5
  6.5 0.0 copy-start.1
  6.5 2.2 %copy-done.1 = bf16[2048,1024]{1,0:T(8,128)(2,1)S(1)} copy-done((bf16[2048,1024]{1,0:T(8,128)(2,1)S(1)}, bf16[2048,1024]{1,0:T(8,128)(2,1)}, u32[]{:S(2)}) %copy-start.1) | copy-done | bytes 4194328
  8.7 0.7 copy-done.2
  9.4 0.0 copy-start.3
  9.4 0.7 copy-done.3
  10.1 0.0 copy-start.4
  10.1 0.7 copy-done.4
  10.8 3.5 %send_rows.1 = bf16[32,56,128]{2,1,0:T(8,128)(2,1)} custom-call(s32[1]{0:T(128)} %bitcast.refs_0_, s32[1,2048]{1,0:T(1,128)S(1)} %bitcast.12, s32[1,32]{1,0:T(1,128)S(1)} %bitcast.14, s32[1,2048]{1,0:T(1,128)S(1)} %bitcast.13, bf16[2048,1024]{1,0:T(8,128)(2,1)S(1)} %copy-done.1), custom_call_target="tpu_custom_call" | custom-call | tf_op jit(solution)/shard_map/send_rows/pallas_call | solution.py:200
  14.3 13.7 %all-to-all-start = ((bf16[32,56,128]{2,1,0:T(8,128)(2,1)}), bf16[32,56,128]{2,1,0:T(8,128)(2,1)S(1)}, u32[]{:S(2)}, u32[]{:S(2)}) async-start(bf16[32,56,128]{2,1,0:T(8,128)(2,1)} %send_rows.1), calls=%async_computation | async-start | bytes 917504 | tf_op jit(solution)/shard_map/all_to_all | solution.py:213
  28.0 0.0 all-gather.2.cloned.1.call-start
  28.1 0.0 copy-done.5
  28.1 14.3 %all-to-all-done.refs_0_ = bf16[32,56,128]{2,1,0:T(8,128)(2,1)S(1)} async-done(((bf16[32,56,128]{2,1,0:T(8,128)(2,1)}), bf16[32,56,128]{2,1,0:T(8,128)(2,1)S(1)}, u32[]{:S(2)}, u32[]{:S(2)}) %all-to-all-start) | async-done | bytes 458784 | tf_op jit(solution)/shard_map/all_to_all | solution.py:213
  42.4 1.6 %unit_rows.1.refs_2_ = bf16[1040,128]{1,0:T(8,128)(2,1)} custom-call(bf16[32,56,128]{2,1,0:T(8,128)(2,1)S(1)} %all-to-all-done.refs_0_, s32[1,128]{1,0:T(1,128)S(1)} %get-tuple-element.6.refs_1_, s32[1,128]{1,0:T(1,128)S(1)} %get-tuple-element.5.refs_2_), custom_call_target="tpu_custom_call" | custom-call | tf_op jit(solution)/shard_map/unit_rows/pallas_call | solution.py:216
  44.1 0.0 all-gather.2.cloned.1.call-update
  44.1 3.3 %collective-permute-start = (bf16[1040,128]{1,0:T(8,128)(2,1)}, bf16[1040,128]{1,0:T(8,128)(2,1)S(1)}, u32[]{:S(2)}, u32[]{:S(2)}) collective-permute-start(bf16[1040,128]{1,0:T(8,128)(2,1)} %unit_rows.1.refs_2_), channel_id=1, source_target_pairs={{0,1},{1,2},{2,3},{3,4},{4,5},{5,6},{6,7},{7,8},{8,9},{9,10},{10,1... | collective-permute-start | bytes 798728 | tf_op jit(solution)/shard_map/ppermute | solution.py:228
  47.4 5.3 %collective-permute-start.1 = (bf16[1040,128]{1,0:T(8,128)(2,1)}, bf16[1040,128]{1,0:T(8,128)(2,1)S(1)}, u32[]{:S(2)}, u32[]{:S(2)}) collective-permute-start(bf16[1040,128]{1,0:T(8,128)(2,1)} %unit_rows.1.refs_2_), channel_id=1, source_target_pairs={{1,0},{2,1},{3,2},{4,3},{5,4},{6,5},{7,6},{8,7},{9,8},{10,9},{11,1... | collective-permute-start | bytes 798728 | tf_op jit(solution)/shard_map/ppermute | solution.py:229
  52.7 2.1 %collective-permute-done.refs_3_ = bf16[1040,128]{1,0:T(8,128)(2,1)S(1)} collective-permute-done((bf16[1040,128]{1,0:T(8,128)(2,1)}, bf16[1040,128]{1,0:T(8,128)(2,1)S(1)}, u32[]{:S(2)}, u32[]{:S(2)}) %collective-permute-start) | collective-permute-done | bytes 266272 | tf_op jit(solution)/shard_map/ppermute | solution.py:228
  54.8 1.6 %collective-permute-done.1.refs_4_ = bf16[1040,128]{1,0:T(8,128)(2,1)S(1)} collective-permute-done((bf16[1040,128]{1,0:T(8,128)(2,1)}, bf16[1040,128]{1,0:T(8,128)(2,1)S(1)}, u32[]{:S(2)}, u32[]{:S(2)}) %collective-permute-start.1) | collective-permute-done | bytes 266272 | tf_op jit(solution)/shard_map/ppermute | solution.py:229
  56.4 31.3 %all-gather.2.cloned.1.call-done.refs_1_ = bf16[16640,128]{1,0:T(8,128)(2,1)} async-done(((bf16[1040,128]{1,0:T(8,128)(2,1)}), bf16[16640,128]{1,0:T(8,128)(2,1)}) %all-gather.2.cloned.1.call-update) | async-done | bytes 4259856 | tf_op jit(solution)/shard_map/all_gather | solution.py:227
  87.6 2.2 %copy-done = bf16[16640,128]{1,0:T(8,128)(2,1)S(1)} copy-done((bf16[16640,128]{1,0:T(8,128)(2,1)S(1)}, bf16[16640,128]{1,0:T(8,128)(2,1)}, u32[]{:S(2)}) %copy-start) | copy-done | bytes 4259864
  89.8 4.5 %score_rows.1 = f32[16,128]{1,0:T(8,128)S(1)} custom-call(s32[1]{0:T(128)} %bitcast.refs_0_, bf16[16640,128]{1,0:T(8,128)(2,1)S(1)} %copy-done, bf16[1040,128]{1,0:T(8,128)(2,1)} %unit_rows.1.refs_2_, bf16[1040,128]{1,0:T(8,128)(2,1)S(1)} %collective-permute-done.refs_3_, bf16[1040,128]{1,0:T(8,128)(2,1)S(1)} %collective-permute-done.1.refs_4_), custom_call_target="tpu_custom_call" | custom-call | tf_op jit(solution)/shard_map/score_rows/pallas_call | solution.py:230
  94.4 11.5 %all_to_all.14 = f32[16,1,128]{2,1,0:T(1,128)S(1)} all-to-all(f32[16,1,128]{2,1,0:T(1,128)S(1)} %bitcast.11), channel_id=1, replica_groups=mesh['group'=16,'owner'=32] {'group'}, dimensions={0} | all-to-all | bytes 16384 | tf_op jit(solution)/shard_map/all_to_all | solution.py:238
  105.8 0.5 reduce_max.9
  (3 shorter events, 0.0 us)
Async XLA Ops:
  6.5 21.5 %copy-start.5 = (s32[1,1,49,2]{2,3,1,0:T(2,128)S(1)}, s32[1,1,49,2]{2,3,1,0:T(2,128)}, u32[]{:S(2)}) copy-start(s32[1,1,49,2]{2,3,1,0:T(2,128)} %param.9) | copy-start | bytes 1180
  6.5 2.2 %copy-start.1 = (bf16[2048,1024]{1,0:T(8,128)(2,1)S(1)}, bf16[2048,1024]{1,0:T(8,128)(2,1)}, u32[]{:S(2)}) copy-start(bf16[2048,1024]{1,0:T(8,128)(2,1)} %refs_4_.1) | copy-start | bytes 12582916
  8.7 0.7 copy-start.2
  9.4 0.7 copy-start.3
  10.1 0.7 copy-start.4
  14.3 28.2 %all-to-all-start = ((bf16[32,56,128]{2,1,0:T(8,128)(2,1)}), bf16[32,56,128]{2,1,0:T(8,128)(2,1)S(1)}, u32[]{:S(2)}, u32[]{:S(2)}) async-start(bf16[32,56,128]{2,1,0:T(8,128)(2,1)} %send_rows.1), calls=%async_computation | async-start | bytes 917504 | tf_op jit(solution)/shard_map/all_to_all | solution.py:213
  28.0 59.6 %all-gather.2.cloned.1.call-start = ((), (), s32[]{:S(2)}) async-start(), calls=%async_computation.2 | async-start | bytes 4526080 | tf_op jit(solution)/shard_map/all_gather | solution.py:227
  44.1 10.7 %collective-permute-start = (bf16[1040,128]{1,0:T(8,128)(2,1)}, bf16[1040,128]{1,0:T(8,128)(2,1)S(1)}, u32[]{:S(2)}, u32[]{:S(2)}) collective-permute-start(bf16[1040,128]{1,0:T(8,128)(2,1)} %unit_rows.1.refs_2_), channel_id=1, source_target_pairs={{0,1},{1,2},{2,3},{3,4},{4,5},{5,6},{6,7},{7,8},{8,9},{9,10},{10,1... | collective-permute-start | bytes 798728 | tf_op jit(solution)/shard_map/ppermute | solution.py:228
  47.4 8.9 %collective-permute-start.1 = (bf16[1040,128]{1,0:T(8,128)(2,1)}, bf16[1040,128]{1,0:T(8,128)(2,1)S(1)}, u32[]{:S(2)}, u32[]{:S(2)}) collective-permute-start(bf16[1040,128]{1,0:T(8,128)(2,1)} %unit_rows.1.refs_2_), channel_id=1, source_target_pairs={{1,0},{2,1},{3,2},{4,3},{5,4},{6,5},{7,6},{8,7},{9,8},{10,9},{11,1... | collective-permute-start | bytes 798728 | tf_op jit(solution)/shard_map/ppermute | solution.py:229
  87.6 2.2 %copy-start = (bf16[16640,128]{1,0:T(8,128)(2,1)S(1)}, bf16[16640,128]{1,0:T(8,128)(2,1)}, u32[]{:S(2)}) copy-start(bf16[16640,128]{1,0:T(8,128)(2,1)} %all-gather.2.cloned.1.call-done.refs_1_) | copy-start | bytes 12779524
Sparse Core Ops, SparseCore 0:
  44.2 43.3 all-gather.1

commit v2 on v1

v2 whole, which is shorter than its diff:
```python
import jax
import jax.numpy as jnp
from jax import lax
from jax.experimental import pallas as pl
from jax.experimental.pallas import tpu as pltpu
from jax.sharding import PartitionSpec as P

BLOCK = 128
LANES = 128
META = 8
PAY_META = 16
UNITS = 2
BF16 = jnp.bfloat16
F32 = jnp.float32
I32 = jnp.int32


def iota(shape, dim):
    return lax.broadcasted_iota(I32, shape, dim)


def ones_where(mask):
    return jnp.where(mask, 1.0, 0.0).astype(BF16)


def mm(a, b):
    return jnp.dot(a, b, preferred_element_type=F32)


def mm_nt(a, b):
    return lax.dot_general(a, b, (((1,), (1,)), ((), ())), preferred_element_type=F32)


def mm_tn(a, b):
    return lax.dot_general(a, b, (((0,), (0,)), ((), ())), preferred_element_type=F32)


def send_kernel(n_owner, n_group, cap, shift, pieces, cluster_hbm, owner_hbm, slot_hbm, emb_ref, out_ref, emb, wide, cluster_ref, owner_ref, slot_ref, sems):
    rows, feat = emb.shape
    chunks = feat // LANES
    step = rows // pieces
    small = [
        pltpu.make_async_copy(source, goal, sems.at[pieces + i])
        for i, (source, goal) in enumerate(
            ((cluster_hbm, cluster_ref), (owner_hbm, owner_ref), (slot_hbm, slot_ref))
        )
    ]
    copies = [
        pltpu.make_async_copy(emb_ref.at[pl.ds(i * step, step)], emb.at[pl.ds(i * step, step)], sems.at[i])
        for i in range(pieces)
    ]
    for copy in small + copies:
        copy.start()
    for copy in small:
        copy.wait()
    me = lax.axis_index("group")
    picked = ones_where(iota((n_owner, rows), 0) == cluster_ref[...])
    table = ones_where(iota((n_owner, n_owner), 0) == owner_ref[...])
    to = mm(table, picked).astype(BF16)
    parts = rows // LANES
    stacked = jnp.concatenate([to[:, i * LANES : (i + 1) * LANES] for i in range(parts)], axis=0)
    before = mm(stacked, ones_where(iota((LANES, LANES), 0) < iota((LANES, LANES), 1)))
    totals = mm(stacked, jnp.ones((LANES, LANES), BF16))
    running = jnp.zeros((n_owner, LANES), F32)
    lane_owner = iota((n_owner, LANES), 0).astype(F32)
    place, target = [], []
    for i in range(parts):
        here = stacked[i * n_owner : (i + 1) * n_owner].astype(F32)
        spot = before[i * n_owner : (i + 1) * n_owner] + running
        place.append(jnp.sum(here * spot, axis=0, keepdims=True))
        target.append(jnp.sum(here * lane_owner, axis=0, keepdims=True))
        running = running + totals[i * n_owner : (i + 1) * n_owner]
    place = jnp.concatenate(place, axis=1).astype(I32)
    target = jnp.concatenate(target, axis=1).astype(I32)
    share = place & (n_group - 1)
    entry = place // n_group
    entry = jnp.where(share == me, entry, jnp.where(share == ((me + shift) & (n_group - 1)), entry + cap, -1))
    mine = entry >= 0
    lines = UNITS * cap
    goal = jnp.where(mine, target * lines + entry, -1)
    slot = slot_ref[...]
    high = (slot // BLOCK + 1).astype(F32)
    low = (slot & (BLOCK - 1)).astype(F32)
    at_entry = iota((LANES, rows), 0) == entry
    meta_high = mm_nt(to, jnp.where(at_entry, high, 0.0).astype(BF16)).astype(BF16)
    meta_low = mm_nt(to, jnp.where(at_entry, low, 0.0).astype(BF16)).astype(BF16)
    line = iota((n_owner * META, n_owner), 0)
    peer = iota((n_owner * META, n_owner), 1)
    meta = mm(ones_where(line == peer * META), meta_high) + mm(ones_where(line == peer * META + 1), meta_low)
    out_ref[:, lines * chunks :, :] = meta.reshape(n_owner, META, LANES).astype(BF16)
    select = ones_where(iota((n_owner * lines, rows), 0) == goal)
    total = None
    for i, copy in enumerate(copies):
        copy.wait()
        part = mm(select[:, i * step : (i + 1) * step], emb[pl.ds(i * step, step), :])
        total = part if total is None else total + part
    for k in range(chunks):
        wide[pl.ds(k, n_owner * lines, chunks), :] = total[:, k * LANES : (k + 1) * LANES]
    out_ref[:, : lines * chunks, :] = wide[...].reshape(n_owner, lines * chunks, LANES).astype(BF16)


def receive_kernel(n_owner, cap, feat, in_ref, near_ref, up_ref, down_ref, both_ref, first_ref, wide):
    chunks = feat // LANES
    per_peer = UNITS * cap
    lines = n_owner * per_peer
    size = feat + PAY_META
    wide[...] = in_ref[:, : per_peer * chunks, :].astype(F32).reshape(lines * chunks, LANES)
    meta = in_ref[:, per_peer * chunks :, :].astype(F32).reshape(n_owner * META, LANES).astype(BF16)
    line = iota((lines, n_owner * META), 0)
    source = iota((lines, n_owner * META), 1)
    at_lane = iota((lines, LANES), 1) == lax.rem(iota((lines, LANES), 0), per_peer)
    high = mm(ones_where(source == line // per_peer * META), meta)
    low = mm(ones_where(source == line // per_peer * META + 1), meta)
    ones = jnp.ones((LANES, LANES), BF16)
    high = mm(jnp.where(at_lane, high, 0.0).astype(BF16), ones)
    low = mm(jnp.where(at_lane, low, 0.0).astype(BF16), ones)
    valid = ones_where(high > 0.5)
    later, sooner = iota((lines, lines), 0), iota((lines, lines), 1)
    same = lax.rem(later, per_peer) // cap == lax.rem(sooner, per_peer) // cap
    place = mm(ones_where(jnp.logical_and(sooner < later, same)), valid)
    unit = lax.rem(iota((lines, BLOCK), 0), per_peer) // cap
    here = jnp.logical_and(place == iota((lines, BLOCK), 1).astype(F32), high > 0.5)
    puts = [jnp.logical_and(here, unit == n) for n in range(UNITS)]
    put_one = ones_where(jnp.concatenate(puts, axis=1))
    parts = []
    square = None
    for k in range(chunks):
        part = mm_tn(put_one, wide[pl.ds(k, lines, chunks), :].astype(BF16))
        parts.append(part)
        here = part * part
        square = here if square is None else square + here
    scale = lax.rsqrt(jnp.sum(square, axis=1, keepdims=True) + 1e-06)
    for k in range(chunks):
        piece = (parts[k] * scale).astype(BF16)
        for n in range(UNITS):
            both_ref[pl.ds(n * size + k * BLOCK, BLOCK), :] = piece[n * BLOCK : (n + 1) * BLOCK]
        first_ref[pl.ds(k * BLOCK, BLOCK), :] = piece[:BLOCK]
    row = iota((PAY_META, LANES), 0)
    for n in range(UNITS):
        blocks = jnp.sum(jnp.where(puts[n], high, 0.0), axis=0, keepdims=True) - 1.0
        inner = jnp.sum(jnp.where(puts[n], low, 0.0), axis=0, keepdims=True)
        numbers = jnp.where(row == 0, blocks, jnp.where(row == 1, inner, 0.0)).astype(BF16)
        both_ref[pl.ds(n * size + feat, PAY_META), :] = numbers
        if n == 0:
            first_ref[pl.ds(feat, PAY_META), :] = numbers
    lists = jnp.concatenate([near_ref[0:6, :], up_ref[0:6, :], down_ref[2:6, :]], axis=0)
    both_ref[pl.ds(UNITS * size, PAY_META), :] = lists.astype(BF16)


def rows_of(ref, start, feat):
    return jnp.concatenate([ref[pl.ds(start + k * BLOCK, BLOCK), :] for k in range(feat // LANES)], axis=1)


def numbers_of(ref, start, feat):
    return ref[pl.ds(start + feat, PAY_META), :].astype(F32)[0:2, :].astype(I32)


def stack_rows(places, feat):
    return jnp.concatenate([rows_of(ref, start, feat) for ref, start in places], axis=0)


def stack_numbers(places, feat):
    return jnp.concatenate([numbers_of(ref, start, feat) for ref, start in places], axis=1)


def best_of(left, bias, places, feat, blocks, same=None):
    right = stack_rows(places, feat)
    width = right.shape[0]
    here = ones_where(iota((blocks, width), 0) == stack_numbers(places, feat)[0:1, :])
    scores = mm_nt(left, right) + mm(bias, here)
    if same is not None:
        scores = jnp.where(same, -2.0, scores)
    return jnp.max(scores, axis=0, keepdims=True)


def bias_of(penalty, marks):
    picked = ones_where(iota((penalty.shape[0], marks.shape[1]), 0) == marks)
    return mm_tn(picked, penalty).astype(BF16)


def slot_table(best, numbers, blocks):
    total = best.shape[1]
    best = jnp.maximum(best, -2.0)
    spread = iota((blocks, total), 0) == numbers[0:1, :]
    inner = ones_where(iota((BLOCK, total), 0) == numbers[1:2, :])
    filled = mm_nt(ones_where(spread), inner)
    result = jnp.zeros((blocks, BLOCK), F32)
    rest = best
    for _ in range(3):
        piece = rest.astype(BF16).astype(F32)
        rest = rest - piece
        result += mm_nt(jnp.where(spread, piece, 0.0).astype(BF16), inner)
    return jnp.where(filled > 0.5, result, -2.0)


def first_score_kernel(blocks, feat, own_ref, twin_ref, back_ref, next_ref, low_ref, high_ref, out_ref, bias_ref):
    size = feat + PAY_META
    lists = [r[pl.ds(UNITS * size, PAY_META), :].astype(F32) for r in (own_ref, twin_ref)]
    count = PAY_META // 2

    def list_row(i):
        return jnp.concatenate([n[2 * b + i : 2 * b + i + 1, :] for n in lists for b in range(count)], axis=1).astype(I32)

    first, second = list_row(0), list_row(1)
    total = 2 * count * LANES
    first_rows = iota((blocks, total), 0)
    wide_rows = iota((3 * blocks, total), 0)
    paired = mm_nt(ones_where(wide_rows == second), ones_where(first_rows == first))
    paired += mm_nt(ones_where(wide_rows == first + blocks), ones_where(first_rows == second - blocks))
    penalty = jnp.where(paired > 0.5, 0.0, -4.0).astype(BF16)
    across = [(low_ref, 0), (low_ref, size), (high_ref, 0), (high_ref, size)]
    marks = stack_numbers(across, feat)[0:1, :]
    marks += jnp.where(iota(marks.shape, 1) < 2 * BLOCK, 0, 2 * blocks)
    across_bias = bias_of(penalty, marks)
    bias_ref[...] = across_bias
    across_rows = stack_rows(across, feat)
    inside = [(back_ref, 0), (next_ref, 0), (own_ref, 0), (twin_ref, 0), (own_ref, size), (twin_ref, size)]
    inside_bias = bias_of(penalty, stack_numbers(inside, feat)[0:1, :] + blocks)
    inside_rows = stack_rows(inside, feat)
    row, lane = iota((6 * BLOCK, 2 * BLOCK), 0), iota((6 * BLOCK, 2 * BLOCK), 1)
    same = row == lane + jnp.where(lane < BLOCK, 2 * BLOCK, 3 * BLOCK)
    groups = [
        ([(own_ref, 0), (own_ref, size)], 0, 6, same),
        ([(twin_ref, 0), (twin_ref, size)], 0, 3, None),
        ([(back_ref, 0), (next_ref, 0)], 2, 6, None),
    ]
    best, numbers = [], []
    for places, low, high, equal in groups:
        part = slice(low * BLOCK, high * BLOCK)
        one = best_of(across_rows, across_bias, places, feat, blocks)
        two = best_of(inside_rows[part], inside_bias[part], places, feat, blocks, equal)
        best.append(jnp.maximum(one, two))
        numbers.append(stack_numbers(places, feat))
    out_ref[...] = slot_table(jnp.concatenate(best, axis=1), jnp.concatenate(numbers, axis=1), blocks)


def second_score_kernel(blocks, feat, table_ref, bias_ref, low_ref, high_ref, back_ref, back_twin_ref, next_twin_ref, out_ref):
    size = feat + PAY_META
    across_rows = stack_rows([(low_ref, 0), (low_ref, size), (high_ref, 0), (high_ref, size)], feat)
    across_bias = bias_ref[...]
    best, numbers = [], []
    for places in ([(back_ref, size), (back_twin_ref, size)], [(back_twin_ref, 0), (next_twin_ref, 0)]):
        best.append(best_of(across_rows, across_bias, places, feat, blocks))
        numbers.append(stack_numbers(places, feat))
    table = slot_table(jnp.concatenate(best, axis=1), jnp.concatenate(numbers, axis=1), blocks)
    out_ref[...] = jnp.maximum(table_ref[...], table)


def vmem():
    return pl.BlockSpec(memory_space=pltpu.VMEM)


def anywhere():
    return pl.BlockSpec(memory_space=pl.ANY)


PARAMS = pltpu.CompilerParams(vmem_limit_bytes=48 * 1024 * 1024)


def cost(flops, nbytes):
    return pl.CostEstimate(flops=flops, bytes_accessed=nbytes, transcendentals=0)


def on_device(embeddings, cluster_of, cluster_owner, slot_of, pairs):
    n_owner = lax.axis_size("owner")
    n_group = lax.axis_size("group")
    rows, feat = embeddings.shape
    chunks = feat // LANES
    cap = 3 * rows // (2 * n_owner * n_group)
    lines = UNITS * cap
    pieces = 4
    size = feat + PAY_META
    outgoing = pl.pallas_call(
        lambda *refs: send_kernel(n_owner, n_group, cap, 6, pieces, *refs),
        out_shape=jax.ShapeDtypeStruct((n_owner, lines * chunks + META, LANES), BF16),
        in_specs=[anywhere()] * 4,
        out_specs=vmem(),
        scratch_shapes=[
            pltpu.VMEM((rows, feat), BF16),
            pltpu.VMEM((n_owner * lines * chunks, LANES), F32),
            pltpu.VMEM((1, rows), I32),
            pltpu.VMEM((1, n_owner), I32),
            pltpu.VMEM((1, rows), I32),
            pltpu.SemaphoreType.DMA((pieces + 3,)),
        ],
        compiler_params=PARAMS,
        name="send_rows",
    )(cluster_of.reshape(1, rows), cluster_owner.reshape(1, n_owner), slot_of.reshape(1, rows), embeddings)
    arrived = lax.all_to_all(outgoing, "owner", split_axis=0, concat_axis=0, tiled=True)
    swap = [(i, i ^ 1) for i in range(n_group)]

    def along_y(x, hops):
        return lax.ppermute(x, "group", [(i, (i + 2 * hops) % n_group) for i in range(n_group)])

    def along_owner(x, hops):
        return lax.ppermute(x, "owner", [(i, (i + hops) % n_owner) for i in range(n_owner)])

    entries = pairs.reshape(-1, 2)
    listed = jnp.pad(entries.T, ((0, 6), (0, LANES - entries.shape[0])), constant_values=-1).astype(F32)
    before, after = along_y(listed, 1), along_y(listed, -1)
    near = jnp.concatenate([before[0:2], listed[0:2], after[0:2], listed[6:8]], axis=0)
    down, up = along_y(near, 3), along_y(near, -3)
    both, first = pl.pallas_call(
        lambda *refs: receive_kernel(n_owner, cap, feat, *refs),
        out_shape=[
            jax.ShapeDtypeStruct((UNITS * size + PAY_META, LANES), BF16),
            jax.ShapeDtypeStruct((size, LANES), BF16),
        ],
        in_specs=[vmem()] * 4,
        out_specs=[vmem()] * 2,
        scratch_shapes=[pltpu.VMEM((n_owner * lines * chunks, LANES), F32)],
        compiler_params=PARAMS,
        name="unit_rows",
    )(arrived, near, up, down)
    low, high = along_owner(both, 1), along_owner(both, -1)
    back, following = along_y(both, 1), along_y(first, -1)
    twin = lax.ppermute(both, "group", swap)
    low, high, back, following, twin = lax.optimization_barrier((low, high, back, following, twin))
    back_twin, next_twin = lax.ppermute(back, "group", swap), lax.ppermute(following, "group", swap)
    table, bias = pl.pallas_call(
        lambda *refs: first_score_kernel(n_group, feat, *refs),
        out_shape=[
            jax.ShapeDtypeStruct((n_group, BLOCK), F32),
            jax.ShapeDtypeStruct((4 * BLOCK, n_group), BF16),
        ],
        in_specs=[vmem()] * 6,
        out_specs=[vmem()] * 2,
        compiler_params=PARAMS,
        cost_estimate=cost(3 * 10**9, 4 * 10**6),
        name="score_rows",
    )(both, twin, back, following, low, high)
    table = pl.pallas_call(
        lambda *refs: second_score_kernel(n_group, feat, *refs),
        out_shape=jax.ShapeDtypeStruct((n_group, BLOCK), F32),
        in_specs=[vmem()] * 7,
        out_specs=vmem(),
        compiler_params=PARAMS,
        cost_estimate=cost(5 * 10**8, 2 * 10**6),
        name="score_rest",
    )(table, bias, low, high, back, back_twin, next_twin)
    shares = lax.all_to_all(table, "group", split_axis=0, concat_axis=0, tiled=True)
    return jnp.max(shares, axis=0, keepdims=True)


def solution(mesh):
    placed = (P("owner", None), P("owner"), P(), P("owner"), P("owner", "group", None, None))
    return jax.shard_map(
        on_device, mesh=mesh, in_specs=placed, out_specs=P("owner", "group"), check_vma=False
    )
```

time: 114 us -> 102 us (0.89)
  starting transfers between devices: 22.4 us -> 53.3 us
  waiting for transfers between devices: 49.3 us -> 21.2 us
  between operations: 13.5 us -> 0.17 us
  local copies, waits for them, and re-layouts: 6.47 us -> 4.26 us
    all_gather x1 -> x0, waiting for transfers between devices: 31.3 us -> none  [on_device(): gathered = lax.all_gather(payload, 'group', axis=0, tiled=True)]
    ppermute x2 -> x11, starting transfers between devices: 8.6 us -> 39.5 us  [the longest x6 20.5 us: along_y(): lax.ppermute(x, 'group', [(i, (i + 2 * hops) % n_group) for i in range(n_...]
    ppermute x2 -> x11, waiting for transfers between devices: 3.65 us -> 19.2 us  [the longest x6 12 us: along_y(): lax.ppermute(x, 'group', [(i, (i + 2 * hops) % n_group) for i in range(n_...]
    all_to_all x1, waiting for transfers between devices: 14.3 us -> 2.07 us  [on_device(): lax.all_to_all(outgoing, 'owner', split_axis=0, concat_axis=0, tiled=True)]
    unnamed x12 -> x10, local copies, waits for them, and re-layouts: 6.46 us -> 4.25 us
    pallas_call x2 -> x3, Pallas kernels: 8 us -> 8.97 us  [the longest x1 4.7 us: on_device(): pl.pallas_call(lambda *refs: send_kernel(n_owner, n_group, cap, 6, pieces...]
  transfers between devices with their start and end apart: 4 -> 12, of which waited for: 4 -> 6; matrix products, arithmetic and copies ran while one was open for 0% -> 0% of each run, Pallas kernels for 0% -> 3%
where the time goes in v2:
time: 102 us
  starting transfers between devices  53.3 us (52%)
  waiting for transfers between devices  21.2 us (21%)
  blocking collectives  11.7 us (11%)
  Pallas kernels  10.4 us (10%)
  local copies, waits for them, and re-layouts  4.26 us (4%)
    ppermute x6, starting transfers between devices, along_y(): lax.ppermute(x, 'group', [(i, (i + 2 * hops) % n_group) for i in range(n_...  20.5 us
    all_to_all x1, starting transfers between devices, on_device(): lax.all_to_all(outgoing, 'owner', split_axis=0, concat_axis=0, tiled=True)  13.7 us
    ppermute x6, waiting for transfers between devices, along_y(): lax.ppermute(x, 'group', [(i, (i + 2 * hops) % n_group) for i in range(n_...  12 us
    all_to_all x1, blocking collectives, on_device(): lax.all_to_all(table, 'group', split_axis=0, concat_axis=0, tiled=True)  11.7 us
    ppermute x2, starting transfers between devices, along_owner(): lax.ppermute(x, 'owner', [(i, (i + hops) % n_owner) for i in range(n_owne...  8.75 us
    ppermute x2, waiting for transfers between devices, along_owner(): lax.ppermute(x, 'owner', [(i, (i + hops) % n_owner) for i in range(n_owne...  7.18 us
    ppermute x1, starting transfers between devices, on_device(): twin = lax.ppermute(both, 'group', swap)  5.02 us
    pallas_call x1, Pallas kernels, on_device(): pl.pallas_call(lambda *refs: send_kernel(n_owner, n_group, cap, 6, pieces...  4.7 us
  transfers between devices with their start and end apart: 12, of which 6 were waited for; matrix products, arithmetic and copies ran while one was open for 0% of the time, Pallas kernels for 3%

profile of v2, /device:TPU:1, one launch (start us, length us, event | category | flops | bytes accessed | tf_op | source)
XLA Modules:
  0.0 101.7 jit_solution(11361375536837852208)
XLA Ops:
  0.0 2.2 %copy-done = bf16[2048,1024]{1,0:T(8,128)(2,1)S(1)} copy-done((bf16[2048,1024]{1,0:T(8,128)(2,1)S(1)}, bf16[2048,1024]{1,0:T(8,128)(2,1)}, u32[]{:S(2)}) %copy-start) | copy-done | bytes 4194328
  2.2 0.7 copy-done.1
  4.3 4.7 %send_rows.1 = bf16[32,104,128]{2,1,0:T(8,128)(2,1)} custom-call(s32[1,2048]{1,0:T(1,128)S(1)} %bitcast.11, s32[1,32]{1,0:T(1,128)S(1)} %bitcast.13, s32[1,2048]{1,0:T(1,128)S(1)} %bitcast.12, bf16[2048,1024]{1,0:T(8,128)(2,1)S(1)} %copy-done), custom_call_target="tpu_custom_call" | custom-call | tf_op jit(solution)/shard_map/send_rows/pallas_call | solution.py:273
  9.0 13.7 %all-to-all-start = ((bf16[32,104,128]{2,1,0:T(8,128)(2,1)}), bf16[32,104,128]{2,1,0:T(8,128)(2,1)S(1)}, u32[]{:S(2)}, u32[]{:S(2)}) async-start(bf16[32,104,128]{2,1,0:T(8,128)(2,1)} %send_rows.1), calls=%async_computation | async-start | bytes 1703936 | tf_op jit(solution)/shard_map/all_to_all | solution.py:289
  22.7 5.1 %collective-permute-start.1 = (f32[8,128]{1,0:T(8,128)S(1)}, f32[8,128]{1,0:T(8,128)S(1)}, u32[]{:S(2)}, u32[]{:S(2)}) collective-permute-start(f32[8,128]{1,0:T(8,128)S(1)} %pad_convert_fusion), channel_id=1, source_target_pairs={{0,448},{32,480},{64,0},{96,32},{128,64},{160,96},{192,128},{224,1... | collective-permute-start | bytes 12296 | tf_op jit(solution)/shard_map/ppermute | solution.py:293
  27.8 1.9 %collective-permute-start = (f32[8,128]{1,0:T(8,128)S(1)}, f32[8,128]{1,0:T(8,128)S(1)}, u32[]{:S(2)}, u32[]{:S(2)}) collective-permute-start(f32[8,128]{1,0:T(8,128)S(1)} %pad_convert_fusion), channel_id=1, source_target_pairs={{0,64},{32,96},{64,128},{96,160},{128,192},{160,224},{192,256},{22... | collective-permute-start | bytes 12296 | tf_op jit(solution)/shard_map/ppermute | solution.py:293
  29.8 3.9 %collective-permute-done = f32[8,128]{1,0:T(8,128)S(1)} collective-permute-done((f32[8,128]{1,0:T(8,128)S(1)}, f32[8,128]{1,0:T(8,128)S(1)}, u32[]{:S(2)}, u32[]{:S(2)}) %collective-permute-start) | collective-permute-done | bytes 4128 | tf_op jit(solution)/shard_map/ppermute | solution.py:293
  33.7 1.9 %collective-permute-start.3 = (f32[8,128]{1,0:T(8,128)S(1)}, f32[8,128]{1,0:T(8,128)S(1)}, u32[]{:S(2)}, u32[]{:S(2)}) collective-permute-start(f32[8,128]{1,0:T(8,128)S(1)} %pad_maximum_fusion.refs_1_), channel_id=1, source_target_pairs={{0,192},{32,224},{64,256},{96,288},{128,320},{160,352},{192,384},{... | collective-permute-start | bytes 12296 | tf_op jit(solution)/shard_map/ppermute | solution.py:293
  35.6 6.4 %collective-permute-start.2 = (f32[8,128]{1,0:T(8,128)S(1)}, f32[8,128]{1,0:T(8,128)S(1)}, u32[]{:S(2)}, u32[]{:S(2)}) collective-permute-start(f32[8,128]{1,0:T(8,128)S(1)} %pad_maximum_fusion.refs_1_), channel_id=1, source_target_pairs={{0,320},{32,352},{64,384},{96,416},{128,448},{160,480},{192,0},{22... | collective-permute-start | bytes 12296 | tf_op jit(solution)/shard_map/ppermute | solution.py:293
  42.0 0.7 collective-permute-done.2.refs_2_
  42.7 2.1 %all-to-all-done.refs_0_ = bf16[32,104,128]{2,1,0:T(8,128)(2,1)S(1)} async-done(((bf16[32,104,128]{2,1,0:T(8,128)(2,1)}), bf16[32,104,128]{2,1,0:T(8,128)(2,1)S(1)}, u32[]{:S(2)}, u32[]{:S(2)}) %all-to-all-start) | async-done | bytes 852000 | tf_op jit(solution)/shard_map/all_to_all | solution.py:289
  44.8 1.5 %unit_rows.1 = (bf16[2096,128]{1,0:T(8,128)(2,1)S(1)}, bf16[1040,128]{1,0:T(8,128)(2,1)S(1)}) custom-call(bf16[32,104,128]{2,1,0:T(8,128)(2,1)S(1)} %all-to-all-done.refs_0_, f32[8,128]{1,0:T(8,128)S(1)} %pad_maximum_fusion.refs_1_, f32[8,128]{1,0:T(8,128)S(1)} %collective-permute-done.2.refs_2_, f32[8,128]{1,0:T(8,128)S(1)} %collective-permute-done.3.refs_3_), custom_call_target="tpu_custom_call" | custom-call | tf_op jit(solution)/shard_map/unit_rows/pallas_call | solution.py:303
  46.3 5.0 %collective-permute-start.8 = (bf16[2096,128]{1,0:T(8,128)(2,1)S(1)}, bf16[2096,128]{1,0:T(8,128)(2,1)S(1)}, u32[]{:S(2)}, u32[]{:S(2)}) collective-permute-start(bf16[2096,128]{1,0:T(8,128)(2,1)S(1)} %get-tuple-element.14.refs_0_), channel_id=1, source_target_pairs={{0,32},{32,0},{64,96},{96,64},{128,160},{160,128},{192,224},{224,1... | collective-permute-start | bytes 1609736 | tf_op jit(solution)/shard_map/ppermute | solution.py:317
  51.3 3.3 %collective-permute-start.6 = (bf16[2096,128]{1,0:T(8,128)(2,1)S(1)}, bf16[2096,128]{1,0:T(8,128)(2,1)S(1)}, u32[]{:S(2)}, u32[]{:S(2)}) collective-permute-start(bf16[2096,128]{1,0:T(8,128)(2,1)S(1)} %get-tuple-element.14.refs_0_), channel_id=1, source_target_pairs={{0,64},{32,96},{64,128},{96,160},{128,192},{160,224},{192,256},{22... | collective-permute-start | bytes 1609736 | tf_op jit(solution)/shard_map/ppermute | solution.py:293
  54.6 6.8 %collective-permute-start.5 = (bf16[2096,128]{1,0:T(8,128)(2,1)S(1)}, bf16[2096,128]{1,0:T(8,128)(2,1)S(1)}, u32[]{:S(2)}, u32[]{:S(2)}) collective-permute-start(bf16[2096,128]{1,0:T(8,128)(2,1)S(1)} %get-tuple-element.14.refs_0_), channel_id=1, source_target_pairs={{0,31},{1,0},{2,1},{3,2},{4,3},{5,4},{6,5},{7,6},{8,7},{9,8},{10,9... | collective-permute-start | bytes 1609736 | tf_op jit(solution)/shard_map/ppermute | solution.py:296
  61.4 1.9 %collective-permute-start.4 = (bf16[2096,128]{1,0:T(8,128)(2,1)S(1)}, bf16[2096,128]{1,0:T(8,128)(2,1)S(1)}, u32[]{:S(2)}, u32[]{:S(2)}) collective-permute-start(bf16[2096,128]{1,0:T(8,128)(2,1)S(1)} %get-tuple-element.14.refs_0_), channel_id=1, source_target_pairs={{0,1},{1,2},{2,3},{3,4},{4,5},{5,6},{6,7},{7,8},{8,9},{9,10},{10,1... | collective-permute-start | bytes 1609736 | tf_op jit(solution)/shard_map/ppermute | solution.py:296
  63.4 1.9 %collective-permute-start.7 = (bf16[1040,128]{1,0:T(8,128)(2,1)S(1)}, bf16[1040,128]{1,0:T(8,128)(2,1)S(1)}, u32[]{:S(2)}, u32[]{:S(2)}) collective-permute-start(bf16[1040,128]{1,0:T(8,128)(2,1)S(1)} %get-tuple-element.15), channel_id=1, source_target_pairs={{0,448},{32,480},{64,0},{96,32},{128,64},{160,96},{192,128},{224,1... | collective-permute-start | bytes 798728 | tf_op jit(solution)/shard_map/ppermute | solution.py:293
  65.3 7.3 %collective-permute-done.7.refs_3_ = bf16[1040,128]{1,0:T(8,128)(2,1)S(1)} collective-permute-done((bf16[1040,128]{1,0:T(8,128)(2,1)S(1)}, bf16[1040,128]{1,0:T(8,128)(2,1)S(1)}, u32[]{:S(2)}, u32[]{:S(2)}) %collective-permute-start.7) | collective-permute-done | bytes 266272 | tf_op jit(solution)/shard_map/ppermute | solution.py:293
  72.7 7.1 %collective-permute-done.4.refs_4_.refs_2_ = bf16[2096,128]{1,0:T(8,128)(2,1)S(1)} collective-permute-done((bf16[2096,128]{1,0:T(8,128)(2,1)S(1)}, bf16[2096,128]{1,0:T(8,128)(2,1)S(1)}, u32[]{:S(2)}, u32[]{:S(2)}) %collective-permute-start.4) | collective-permute-done | bytes 536608 | tf_op jit(solution)/shard_map/ppermute | solution.py:296
  79.8 3.3 %collective-permute-start.9 = (bf16[2096,128]{1,0:T(8,128)(2,1)S(1)}, bf16[2096,128]{1,0:T(8,128)(2,1)S(1)}, u32[]{:S(2)}, u32[]{:S(2)}) collective-permute-start(bf16[2096,128]{1,0:T(8,128)(2,1)S(1)} %collective-permute-done.6.refs_2_.refs_4_), channel_id=1, source_target_pairs={{0,32},{32,0},{64,96},{96,64},{128,160},{160,128},{192,224},{224,1... | collective-permute-start | bytes 1609736 | tf_op jit(solution)/shard_map/ppermute | solution.py:319
  83.2 1.9 %collective-permute-start.10 = (bf16[1040,128]{1,0:T(8,128)(2,1)S(1)}, bf16[1040,128]{1,0:T(8,128)(2,1)S(1)}, u32[]{:S(2)}, u32[]{:S(2)}) collective-permute-start(bf16[1040,128]{1,0:T(8,128)(2,1)S(1)} %collective-permute-done.7.refs_3_), channel_id=1, source_target_pairs={{0,32},{32,0},{64,96},{96,64},{128,160},{160,128},{192,224},{224,1... | collective-permute-start | bytes 798728 | tf_op jit(solution)/shard_map/ppermute | solution.py:319
  85.1 3.1 %score_rows.1 = (f32[16,128]{1,0:T(8,128)S(1)}, bf16[512,16]{1,0:T(8,128)(2,1)S(1)}) custom-call(bf16[2096,128]{1,0:T(8,128)(2,1)S(1)} %get-tuple-element.14.refs_0_, bf16[2096,128]{1,0:T(8,128)(2,1)S(1)} %collective-permute-done.8.refs_1_, bf16[2096,128]{1,0:T(8,128)(2,1)S(1)} %collective-permute-done.6.refs_2_.refs_4_, ...), custom_call_target="tpu_custom_call" | custom-call | flops 3000000000 | bytes 4000000 | tf_op jit(solution)/shard_map/score_rows/pallas_call | solution.py:320
  88.2 1.2 %score_rest.1 = f32[16,128]{1,0:T(8,128)S(1)} custom-call(f32[16,128]{1,0:T(8,128)S(1)} %get-tuple-element.21.refs_0_, bf16[512,16]{1,0:T(8,128)(2,1)S(1)} %get-tuple-element.22.refs_1_, bf16[2096,128]{1,0:T(8,128)(2,1)S(1)} %collective-permute-done.4.refs_4_.refs_2_, bf16[2096,128]{1,0:T(8,128)(2,1)S(1)} %collective-permute-done.5.refs_5_.refs_3_, ...), custom_call_target="tpu_custom_call" | custom-call | flops 500000000 | bytes 2000000 | tf_op jit(solution)/shard_map/score_rest/pallas_call | solution.py:332
  89.4 11.7 %all_to_all.14 = f32[16,1,128]{2,1,0:T(1,128)S(1)} all-to-all(f32[16,1,128]{2,1,0:T(1,128)S(1)} %bitcast.10), channel_id=1, replica_groups=mesh['group'=16,'owner'=32] {'group'}, dimensions={0} | all-to-all | bytes 16384 | tf_op jit(solution)/shard_map/all_to_all | solution.py:341
  (21 shorter events, 2.0 us)
Async XLA Ops:
  0.0 22.7 %copy-start.4 = (s32[1,1,49,2]{2,3,1,0:T(2,128)S(1)}, s32[1,1,49,2]{2,3,1,0:T(2,128)}, u32[]{:S(2)}) copy-start(s32[1,1,49,2]{2,3,1,0:T(2,128)} %param.9) | copy-start | bytes 1180
  0.0 2.2 %copy-start = (bf16[2048,1024]{1,0:T(8,128)(2,1)S(1)}, bf16[2048,1024]{1,0:T(8,128)(2,1)}, u32[]{:S(2)}) copy-start(bf16[2048,1024]{1,0:T(8,128)(2,1)} %refs_3_.1) | copy-start | bytes 12582916
  2.2 0.7 copy-start.1
  2.9 0.7 copy-start.2
  3.6 0.7 copy-start.3
  9.0 35.8 %all-to-all-start = ((bf16[32,104,128]{2,1,0:T(8,128)(2,1)}), bf16[32,104,128]{2,1,0:T(8,128)(2,1)S(1)}, u32[]{:S(2)}, u32[]{:S(2)}) async-start(bf16[32,104,128]{2,1,0:T(8,128)(2,1)} %send_rows.1), calls=%async_computation | async-start | bytes 1703936 | tf_op jit(solution)/shard_map/all_to_all | solution.py:289
  22.7 7.0 %collective-permute-start.1 = (f32[8,128]{1,0:T(8,128)S(1)}, f32[8,128]{1,0:T(8,128)S(1)}, u32[]{:S(2)}, u32[]{:S(2)}) collective-permute-start(f32[8,128]{1,0:T(8,128)S(1)} %pad_convert_fusion), channel_id=1, source_target_pairs={{0,448},{32,480},{64,0},{96,32},{128,64},{160,96},{192,128},{224,1... | collective-permute-start | bytes 12296 | tf_op jit(solution)/shard_map/ppermute | solution.py:293
  27.8 5.9 %collective-permute-start = (f32[8,128]{1,0:T(8,128)S(1)}, f32[8,128]{1,0:T(8,128)S(1)}, u32[]{:S(2)}, u32[]{:S(2)}) collective-permute-start(f32[8,128]{1,0:T(8,128)S(1)} %pad_convert_fusion), channel_id=1, source_target_pairs={{0,64},{32,96},{64,128},{96,160},{128,192},{160,224},{192,256},{22... | collective-permute-start | bytes 12296 | tf_op jit(solution)/shard_map/ppermute | solution.py:293
  33.7 8.3 %collective-permute-start.3 = (f32[8,128]{1,0:T(8,128)S(1)}, f32[8,128]{1,0:T(8,128)S(1)}, u32[]{:S(2)}, u32[]{:S(2)}) collective-permute-start(f32[8,128]{1,0:T(8,128)S(1)} %pad_maximum_fusion.refs_1_), channel_id=1, source_target_pairs={{0,192},{32,224},{64,256},{96,288},{128,320},{160,352},{192,384},{... | collective-permute-start | bytes 12296 | tf_op jit(solution)/shard_map/ppermute | solution.py:293
  35.6 7.1 %collective-permute-start.2 = (f32[8,128]{1,0:T(8,128)S(1)}, f32[8,128]{1,0:T(8,128)S(1)}, u32[]{:S(2)}, u32[]{:S(2)}) collective-permute-start(f32[8,128]{1,0:T(8,128)S(1)} %pad_maximum_fusion.refs_1_), channel_id=1, source_target_pairs={{0,320},{32,352},{64,384},{96,416},{128,448},{160,480},{192,0},{22... | collective-permute-start | bytes 12296 | tf_op jit(solution)/shard_map/ppermute | solution.py:293
  46.3 26.4 %collective-permute-start.8 = (bf16[2096,128]{1,0:T(8,128)(2,1)S(1)}, bf16[2096,128]{1,0:T(8,128)(2,1)S(1)}, u32[]{:S(2)}, u32[]{:S(2)}) collective-permute-start(bf16[2096,128]{1,0:T(8,128)(2,1)S(1)} %get-tuple-element.14.refs_0_), channel_id=1, source_target_pairs={{0,32},{32,0},{64,96},{96,64},{128,160},{160,128},{192,224},{224,1... | collective-permute-start | bytes 1609736 | tf_op jit(solution)/shard_map/ppermute | solution.py:317
  51.3 21.3 %collective-permute-start.6 = (bf16[2096,128]{1,0:T(8,128)(2,1)S(1)}, bf16[2096,128]{1,0:T(8,128)(2,1)S(1)}, u32[]{:S(2)}, u32[]{:S(2)}) collective-permute-start(bf16[2096,128]{1,0:T(8,128)(2,1)S(1)} %get-tuple-element.14.refs_0_), channel_id=1, source_target_pairs={{0,64},{32,96},{64,128},{96,160},{128,192},{160,224},{192,256},{22... | collective-permute-start | bytes 1609736 | tf_op jit(solution)/shard_map/ppermute | solution.py:293
  54.6 18.1 %collective-permute-start.5 = (bf16[2096,128]{1,0:T(8,128)(2,1)S(1)}, bf16[2096,128]{1,0:T(8,128)(2,1)S(1)}, u32[]{:S(2)}, u32[]{:S(2)}) collective-permute-start(bf16[2096,128]{1,0:T(8,128)(2,1)S(1)} %get-tuple-element.14.refs_0_), channel_id=1, source_target_pairs={{0,31},{1,0},{2,1},{3,2},{4,3},{5,4},{6,5},{7,6},{8,7},{9,8},{10,9... | collective-permute-start | bytes 1609736 | tf_op jit(solution)/shard_map/ppermute | solution.py:296
  61.4 18.4 %collective-permute-start.4 = (bf16[2096,128]{1,0:T(8,128)(2,1)S(1)}, bf16[2096,128]{1,0:T(8,128)(2,1)S(1)}, u32[]{:S(2)}, u32[]{:S(2)}) collective-permute-start(bf16[2096,128]{1,0:T(8,128)(2,1)S(1)} %get-tuple-element.14.refs_0_), channel_id=1, source_target_pairs={{0,1},{1,2},{2,3},{3,4},{4,5},{5,6},{6,7},{7,8},{8,9},{9,10},{10,1... | collective-permute-start | bytes 1609736 | tf_op jit(solution)/shard_map/ppermute | solution.py:296
  63.4 9.3 %collective-permute-start.7 = (bf16[1040,128]{1,0:T(8,128)(2,1)S(1)}, bf16[1040,128]{1,0:T(8,128)(2,1)S(1)}, u32[]{:S(2)}, u32[]{:S(2)}) collective-permute-start(bf16[1040,128]{1,0:T(8,128)(2,1)S(1)} %get-tuple-element.15), channel_id=1, source_target_pairs={{0,448},{32,480},{64,0},{96,32},{128,64},{160,96},{192,128},{224,1... | collective-permute-start | bytes 798728 | tf_op jit(solution)/shard_map/ppermute | solution.py:293
  79.8 8.4 %collective-permute-start.9 = (bf16[2096,128]{1,0:T(8,128)(2,1)S(1)}, bf16[2096,128]{1,0:T(8,128)(2,1)S(1)}, u32[]{:S(2)}, u32[]{:S(2)}) collective-permute-start(bf16[2096,128]{1,0:T(8,128)(2,1)S(1)} %collective-permute-done.6.refs_2_.refs_4_), channel_id=1, source_target_pairs={{0,32},{32,0},{64,96},{96,64},{128,160},{160,128},{192,224},{224,1... | collective-permute-start | bytes 1609736 | tf_op jit(solution)/shard_map/ppermute | solution.py:319
  83.2 5.0 %collective-permute-start.10 = (bf16[1040,128]{1,0:T(8,128)(2,1)S(1)}, bf16[1040,128]{1,0:T(8,128)(2,1)S(1)}, u32[]{:S(2)}, u32[]{:S(2)}) collective-permute-start(bf16[1040,128]{1,0:T(8,128)(2,1)S(1)} %collective-permute-done.7.refs_3_), channel_id=1, source_target_pairs={{0,32},{32,0},{64,96},{96,64},{128,160},{160,128},{192,224},{224,1... | collective-permute-start | bytes 798728 | tf_op jit(solution)/shard_map/ppermute | solution.py:319

commit v3 on v2

--- a/solution.py
+++ b/solution.py
@@ -234,12 +234,12 @@
     out_ref[...] = slot_table(jnp.concatenate(best, axis=1), jnp.concatenate(numbers, axis=1), blocks)
 
 
-def second_score_kernel(blocks, feat, table_ref, bias_ref, low_ref, high_ref, back_ref, back_twin_ref, next_twin_ref, out_ref):
+def second_score_kernel(blocks, feat, table_ref, bias_ref, low_ref, high_ref, back_ref, late_ref, out_ref):
     size = feat + PAY_META
     across_rows = stack_rows([(low_ref, 0), (low_ref, size), (high_ref, 0), (high_ref, size)], feat)
     across_bias = bias_ref[...]
     best, numbers = [], []
-    for places in ([(back_ref, size), (back_twin_ref, size)], [(back_twin_ref, 0), (next_twin_ref, 0)]):
+    for places in ([(back_ref, size), (late_ref, size)], [(late_ref, 0), (late_ref, 2 * size)]):
         best.append(best_of(across_rows, across_bias, places, feat, blocks))
         numbers.append(stack_numbers(places, feat))
     table = slot_table(jnp.concatenate(best, axis=1), jnp.concatenate(numbers, axis=1), blocks)
@@ -250,8 +250,8 @@
     return pl.BlockSpec(memory_space=pltpu.VMEM)
 
 
-def anywhere():
-    return pl.BlockSpec(memory_space=pl.ANY)
+def far():
+    return pl.BlockSpec(memory_space=pltpu.HBM)
 
 
 PARAMS = pltpu.CompilerParams(vmem_limit_bytes=48 * 1024 * 1024)
@@ -273,7 +273,7 @@
     outgoing = pl.pallas_call(
         lambda *refs: send_kernel(n_owner, n_group, cap, 6, pieces, *refs),
         out_shape=jax.ShapeDtypeStruct((n_owner, lines * chunks + META, LANES), BF16),
-        in_specs=[anywhere()] * 4,
+        in_specs=[far()] * 4,
         out_specs=vmem(),
         scratch_shapes=[
             pltpu.VMEM((rows, feat), BF16),
@@ -285,7 +285,12 @@
         ],
         compiler_params=PARAMS,
         name="send_rows",
-    )(cluster_of.reshape(1, rows), cluster_owner.reshape(1, n_owner), slot_of.reshape(1, rows), embeddings)
+    )(
+        *[
+            pltpu.with_memory_space_constraint(x, pltpu.HBM)
+            for x in (cluster_of.reshape(1, rows), cluster_owner.reshape(1, n_owner), slot_of.reshape(1, rows), embeddings)
+        ]
+    )
     arrived = lax.all_to_all(outgoing, "owner", split_axis=0, concat_axis=0, tiled=True)
     swap = [(i, i ^ 1) for i in range(n_group)]
 
@@ -312,11 +317,11 @@
         compiler_params=PARAMS,
         name="unit_rows",
     )(arrived, near, up, down)
-    low, high = along_owner(both, 1), along_owner(both, -1)
-    back, following = along_y(both, 1), along_y(first, -1)
     twin = lax.ppermute(both, "group", swap)
-    low, high, back, following, twin = lax.optimization_barrier((low, high, back, following, twin))
-    back_twin, next_twin = lax.ppermute(back, "group", swap), lax.ppermute(following, "group", swap)
+    following, back = along_y(first, -1), along_y(both, 1)
+    high, low = along_owner(both, -1), along_owner(both, 1)
+    twin, following, back, high, low = lax.optimization_barrier((twin, following, back, high, low))
+    late = lax.ppermute(jnp.concatenate([back[: 2 * size], following], axis=0), "group", swap)
     table, bias = pl.pallas_call(
         lambda *refs: first_score_kernel(n_group, feat, *refs),
         out_shape=[
@@ -332,12 +337,12 @@
     table = pl.pallas_call(
         lambda *refs: second_score_kernel(n_group, feat, *refs),
         out_shape=jax.ShapeDtypeStruct((n_group, BLOCK), F32),
-        in_specs=[vmem()] * 7,
+        in_specs=[vmem()] * 6,
         out_specs=vmem(),
         compiler_params=PARAMS,
         cost_estimate=cost(5 * 10**8, 2 * 10**6),
         name="score_rest",
-    )(table, bias, low, high, back, back_twin, next_twin)
+    )(table, bias, low, high, back, late)
     shares = lax.all_to_all(table, "group", split_axis=0, concat_axis=0, tiled=True)
     return jnp.max(shares, axis=0, keepdims=True)
 

time: 102 us -> 92.5 us (0.907)
  waiting for transfers between devices: 21.2 us -> 13.1 us
  local copies, waits for them, and re-layouts: 4.26 us -> 0.05 us
  blocking collectives: 11.7 us -> 14.2 us
    ppermute x2, waiting for transfers between devices: 7.18 us -> 0.01 us  [along_owner(): lax.ppermute(x, 'owner', [(i, (i + hops) % n_owner) for i in range(n_owne...]
    unnamed x10 -> x2, local copies, waits for them, and re-layouts: 4.25 us -> 0.01 us
    ppermute x2 -> x1, starting transfers between devices: 5.25 us -> 2.7 us  [on_device(): lax.ppermute(jnp.concatenate([back[:2 * size], following], axis=0), 'grou...]
    all_to_all x1, blocking collectives: 11.7 us -> 14.2 us  [on_device(): lax.all_to_all(table, 'group', split_axis=0, concat_axis=0, tiled=True)]
    ppermute x6, starting transfers between devices: 20.5 us -> 22 us  [along_y(): lax.ppermute(x, 'group', [(i, (i + 2 * hops) % n_group) for i in range(n_...]
  transfers between devices with their start and end apart: 12 -> 11, of which waited for: 6 -> 4; matrix products, arithmetic and copies ran while one was open for 0% -> 0% of each run, Pallas kernels for 3% -> 3%
where the time goes in v3:
time: 92.5 us; the launch traced here: 92 us
  starting transfers between devices  52.9 us (57%)
  blocking collectives  14.2 us (15%)
  waiting for transfers between devices  13.1 us (14%)
  Pallas kernels  10.9 us (12%)
    ppermute x6, starting transfers between devices, along_y(): lax.ppermute(x, 'group', [(i, (i + 2 * hops) % n_group) for i in range(n_...  22 us
    all_to_all x1, blocking collectives, on_device(): lax.all_to_all(table, 'group', split_axis=0, concat_axis=0, tiled=True)  14.2 us
    all_to_all x1, starting transfers between devices, on_device(): lax.all_to_all(outgoing, 'owner', split_axis=0, concat_axis=0, tiled=True)  13.7 us
    ppermute x6, waiting for transfers between devices, along_y(): lax.ppermute(x, 'group', [(i, (i + 2 * hops) % n_group) for i in range(n_...  11.1 us
    ppermute x2, starting transfers between devices, along_owner(): lax.ppermute(x, 'owner', [(i, (i + hops) % n_owner) for i in range(n_owne...  8.6 us
    ppermute x1, starting transfers between devices, on_device(): twin = lax.ppermute(both, 'group', swap)  5.96 us
    pallas_call x1, Pallas kernels, on_device(): pl.pallas_call(lambda *refs: send_kernel(n_owner, n_group, cap, 6, pieces...  5.16 us
    pallas_call x1, Pallas kernels, on_device(): pl.pallas_call(lambda *refs: first_score_kernel(n_group, feat, *refs), ou...  3.1 us
  transfers between devices with their start and end apart: 11, of which 4 were waited for; matrix products, arithmetic and copies ran while one was open for 0% of the time, Pallas kernels for 3%

profile of v3, /device:TPU:1, one launch (start us, length us, event | category | flops | bytes accessed | tf_op | source)
XLA Modules:
  0.0 92.0 jit_solution(5812218369693664943)
XLA Ops:
  0.0 5.2 %send_rows.1 = bf16[32,104,128]{2,1,0:T(8,128)(2,1)} custom-call(s32[1,2048]{1,0:T(1,128)} %bitcast.11, s32[1,32]{1,0:T(1,128)} %bitcast.14, s32[1,2048]{1,0:T(1,128)} %bitcast.12, bf16[2048,1024]{1,0:T(8,128)(2,1)} %refs_3_.1), custom_call_target="tpu_custom_call" | custom-call | tf_op jit(solution)/shard_map/send_rows/pallas_call | solution.py:273
  5.2 0.0 copy-start
  5.2 13.7 %all-to-all-start = ((bf16[32,104,128]{2,1,0:T(8,128)(2,1)}), bf16[32,104,128]{2,1,0:T(8,128)(2,1)S(1)}, u32[]{:S(2)}, u32[]{:S(2)}) async-start(bf16[32,104,128]{2,1,0:T(8,128)(2,1)} %send_rows.1), calls=%async_computation | async-start | bytes 1703936 | tf_op jit(solution)/shard_map/all_to_all | solution.py:294
  18.9 5.1 %collective-permute-start.1 = (f32[8,128]{1,0:T(8,128)S(1)}, f32[8,128]{1,0:T(8,128)S(1)}, u32[]{:S(2)}, u32[]{:S(2)}) collective-permute-start(f32[8,128]{1,0:T(8,128)S(1)} %pad_convert_fusion), channel_id=1, source_target_pairs={{0,448},{32,480},{64,0},{96,32},{128,64},{160,96},{192,128},{224,1... | collective-permute-start | bytes 12296 | tf_op jit(solution)/shard_map/ppermute | solution.py:298
  24.0 1.9 %collective-permute-start = (f32[8,128]{1,0:T(8,128)S(1)}, f32[8,128]{1,0:T(8,128)S(1)}, u32[]{:S(2)}, u32[]{:S(2)}) collective-permute-start(f32[8,128]{1,0:T(8,128)S(1)} %pad_convert_fusion), channel_id=1, source_target_pairs={{0,64},{32,96},{64,128},{96,160},{128,192},{160,224},{192,256},{22... | collective-permute-start | bytes 12296 | tf_op jit(solution)/shard_map/ppermute | solution.py:298
  26.0 3.9 %collective-permute-done = f32[8,128]{1,0:T(8,128)S(1)} collective-permute-done((f32[8,128]{1,0:T(8,128)S(1)}, f32[8,128]{1,0:T(8,128)S(1)}, u32[]{:S(2)}, u32[]{:S(2)}) %collective-permute-start) | collective-permute-done | bytes 4128 | tf_op jit(solution)/shard_map/ppermute | solution.py:298
  29.9 1.9 %collective-permute-start.3 = (f32[8,128]{1,0:T(8,128)S(1)}, f32[8,128]{1,0:T(8,128)S(1)}, u32[]{:S(2)}, u32[]{:S(2)}) collective-permute-start(f32[8,128]{1,0:T(8,128)S(1)} %pad_maximum_fusion.1.refs_1_), channel_id=1, source_target_pairs={{0,192},{32,224},{64,256},{96,288},{128,320},{160,352},{192,384},{... | collective-permute-start | bytes 12296 | tf_op jit(solution)/shard_map/ppermute | solution.py:298
  31.8 6.4 %collective-permute-start.2 = (f32[8,128]{1,0:T(8,128)S(1)}, f32[8,128]{1,0:T(8,128)S(1)}, u32[]{:S(2)}, u32[]{:S(2)}) collective-permute-start(f32[8,128]{1,0:T(8,128)S(1)} %pad_maximum_fusion.1.refs_1_), channel_id=1, source_target_pairs={{0,320},{32,352},{64,384},{96,416},{128,448},{160,480},{192,0},{22... | collective-permute-start | bytes 12296 | tf_op jit(solution)/shard_map/ppermute | solution.py:298
  38.2 0.0 collective-permute-done.3.refs_3_
  38.2 0.7 collective-permute-done.2.refs_2_
  38.9 2.1 %all-to-all-done.refs_0_ = bf16[32,104,128]{2,1,0:T(8,128)(2,1)S(1)} async-done(((bf16[32,104,128]{2,1,0:T(8,128)(2,1)}), bf16[32,104,128]{2,1,0:T(8,128)(2,1)S(1)}, u32[]{:S(2)}, u32[]{:S(2)}) %all-to-all-start) | async-done | bytes 852000 | tf_op jit(solution)/shard_map/all_to_all | solution.py:294
  41.0 1.5 %unit_rows.1 = (bf16[2096,128]{1,0:T(8,128)(2,1)S(1)}, bf16[1040,128]{1,0:T(8,128)(2,1)S(1)}) custom-call(bf16[32,104,128]{2,1,0:T(8,128)(2,1)S(1)} %all-to-all-done.refs_0_, f32[8,128]{1,0:T(8,128)S(1)} %pad_maximum_fusion.1.refs_1_, f32[8,128]{1,0:T(8,128)S(1)} %collective-permute-done.2.refs_2_, f32[8,128]{1,0:T(8,128)S(1)} %collective-permute-done.3.refs_3_), custom_call_target="tpu_custom_call" | custom-call | tf_op jit(solution)/shard_map/unit_rows/pallas_call | solution.py:308
  42.5 3.7 %collective-permute-start.8 = (bf16[2096,128]{1,0:T(8,128)(2,1)S(1)}, bf16[2096,128]{1,0:T(8,128)(2,1)S(1)}, u32[]{:S(2)}, u32[]{:S(2)}) collective-permute-start(bf16[2096,128]{1,0:T(8,128)(2,1)S(1)} %get-tuple-element.14.refs_0_), channel_id=1, source_target_pairs={{0,1},{1,2},{2,3},{3,4},{4,5},{5,6},{6,7},{7,8},{8,9},{9,10},{10,1... | collective-permute-start | bytes 1609736 | tf_op jit(solution)/shard_map/ppermute | solution.py:301
  46.2 4.9 %collective-permute-start.7 = (bf16[2096,128]{1,0:T(8,128)(2,1)S(1)}, bf16[2096,128]{1,0:T(8,128)(2,1)S(1)}, u32[]{:S(2)}, u32[]{:S(2)}) collective-permute-start(bf16[2096,128]{1,0:T(8,128)(2,1)S(1)} %get-tuple-element.14.refs_0_), channel_id=1, source_target_pairs={{0,31},{1,0},{2,1},{3,2},{4,3},{5,4},{6,5},{7,6},{8,7},{9,8},{10,9... | collective-permute-start | bytes 1609736 | tf_op jit(solution)/shard_map/ppermute | solution.py:301
  51.1 3.2 %collective-permute-start.6 = (bf16[2096,128]{1,0:T(8,128)(2,1)S(1)}, bf16[2096,128]{1,0:T(8,128)(2,1)S(1)}, u32[]{:S(2)}, u32[]{:S(2)}) collective-permute-start(bf16[2096,128]{1,0:T(8,128)(2,1)S(1)} %get-tuple-element.14.refs_0_), channel_id=1, source_target_pairs={{0,64},{32,96},{64,128},{96,160},{128,192},{160,224},{192,256},{22... | collective-permute-start | bytes 1609736 | tf_op jit(solution)/shard_map/ppermute | solution.py:298
  54.3 6.0 %collective-permute-start.4 = (bf16[2096,128]{1,0:T(8,128)(2,1)S(1)}, bf16[2096,128]{1,0:T(8,128)(2,1)S(1)}, u32[]{:S(2)}, u32[]{:S(2)}) collective-permute-start(bf16[2096,128]{1,0:T(8,128)(2,1)S(1)} %get-tuple-element.14.refs_0_), channel_id=1, source_target_pairs={{0,32},{32,0},{64,96},{96,64},{128,160},{160,128},{192,224},{224,1... | collective-permute-start | bytes 1609736 | tf_op jit(solution)/shard_map/ppermute | solution.py:320
  60.3 3.5 %collective-permute-start.5 = (bf16[1040,128]{1,0:T(8,128)(2,1)S(1)}, bf16[1040,128]{1,0:T(8,128)(2,1)S(1)}, u32[]{:S(2)}, u32[]{:S(2)}) collective-permute-start(bf16[1040,128]{1,0:T(8,128)(2,1)S(1)} %get-tuple-element.15), channel_id=1, source_target_pairs={{0,448},{32,480},{64,0},{96,32},{128,64},{160,96},{192,128},{224,1... | collective-permute-start | bytes 798728 | tf_op jit(solution)/shard_map/ppermute | solution.py:298
  63.7 6.4 %collective-permute-done.5.refs_3_ = bf16[1040,128]{1,0:T(8,128)(2,1)S(1)} collective-permute-done((bf16[1040,128]{1,0:T(8,128)(2,1)S(1)}, bf16[1040,128]{1,0:T(8,128)(2,1)S(1)}, u32[]{:S(2)}, u32[]{:S(2)}) %collective-permute-start.5) | collective-permute-done | bytes 266272 | tf_op jit(solution)/shard_map/ppermute | solution.py:298
  70.2 0.1 pad_maximum_fusion
  70.3 2.7 %collective-permute-start.9 = (bf16[3120,128]{1,0:T(8,128)(2,1)S(1)}, bf16[3120,128]{1,0:T(8,128)(2,1)S(1)}, u32[]{:S(2)}, u32[]{:S(2)}) collective-permute-start(bf16[3120,128]{1,0:T(8,128)(2,1)S(1)} %pad_maximum_fusion), channel_id=1, source_target_pairs={{0,32},{32,0},{64,96},{96,64},{128,160},{160,128},{192,224},{224,1... | collective-permute-start | bytes 2396168 | tf_op jit(solution)/shard_map/ppermute | solution.py:324
  73.0 3.1 %score_rows.1 = (f32[16,128]{1,0:T(8,128)S(1)}, bf16[512,16]{1,0:T(8,128)(2,1)S(1)}) custom-call(bf16[2096,128]{1,0:T(8,128)(2,1)S(1)} %get-tuple-element.14.refs_0_, bf16[2096,128]{1,0:T(8,128)(2,1)S(1)} %collective-permute-done.4.refs_1_, bf16[2096,128]{1,0:T(8,128)(2,1)S(1)} %collective-permute-done.6.refs_2_.refs_4_, ...), custom_call_target="tpu_custom_call" | custom-call | flops 3000000000 | bytes 4000000 | tf_op jit(solution)/shard_map/score_rows/pallas_call | solution.py:325
  76.1 1.2 %score_rest.1 = f32[16,128]{1,0:T(8,128)S(1)} custom-call(f32[16,128]{1,0:T(8,128)S(1)} %get-tuple-element.21.refs_0_, bf16[512,16]{1,0:T(8,128)(2,1)S(1)} %get-tuple-element.22.refs_1_, bf16[2096,128]{1,0:T(8,128)(2,1)S(1)} %collective-permute-done.8.refs_4_.refs_2_, bf16[2096,128]{1,0:T(8,128)(2,1)S(1)} %collective-permute-done.7.refs_5_.refs_3_, ...), custom_call_target="tpu_custom_call" | custom-call | flops 500000000 | bytes 2000000 | tf_op jit(solution)/shard_map/score_rest/pallas_call | solution.py:337
  77.3 14.2 %all_to_all.14 = f32[16,1,128]{2,1,0:T(1,128)S(1)} all-to-all(f32[16,1,128]{2,1,0:T(1,128)S(1)} %bitcast.10), channel_id=1, replica_groups=mesh['group'=16,'owner'=32] {'group'}, dimensions={0} | all-to-all | bytes 16384 | tf_op jit(solution)/shard_map/all_to_all | solution.py:346
  91.4 0.5 reduce_max.9
  (13 shorter events, 0.1 us)
Async XLA Ops:
  5.2 13.7 %copy-start = (s32[1,1,49,2]{2,3,1,0:T(2,128)S(1)}, s32[1,1,49,2]{2,3,1,0:T(2,128)}, u32[]{:S(2)}) copy-start(s32[1,1,49,2]{2,3,1,0:T(2,128)} %param.9) | copy-start | bytes 1180
  5.2 35.8 %all-to-all-start = ((bf16[32,104,128]{2,1,0:T(8,128)(2,1)}), bf16[32,104,128]{2,1,0:T(8,128)(2,1)S(1)}, u32[]{:S(2)}, u32[]{:S(2)}) async-start(bf16[32,104,128]{2,1,0:T(8,128)(2,1)} %send_rows.1), calls=%async_computation | async-start | bytes 1703936 | tf_op jit(solution)/shard_map/all_to_all | solution.py:294
  18.9 7.1 %collective-permute-start.1 = (f32[8,128]{1,0:T(8,128)S(1)}, f32[8,128]{1,0:T(8,128)S(1)}, u32[]{:S(2)}, u32[]{:S(2)}) collective-permute-start(f32[8,128]{1,0:T(8,128)S(1)} %pad_convert_fusion), channel_id=1, source_target_pairs={{0,448},{32,480},{64,0},{96,32},{128,64},{160,96},{192,128},{224,1... | collective-permute-start | bytes 12296 | tf_op jit(solution)/shard_map/ppermute | solution.py:298
  24.0 5.9 %collective-permute-start = (f32[8,128]{1,0:T(8,128)S(1)}, f32[8,128]{1,0:T(8,128)S(1)}, u32[]{:S(2)}, u32[]{:S(2)}) collective-permute-start(f32[8,128]{1,0:T(8,128)S(1)} %pad_convert_fusion), channel_id=1, source_target_pairs={{0,64},{32,96},{64,128},{96,160},{128,192},{160,224},{192,256},{22... | collective-permute-start | bytes 12296 | tf_op jit(solution)/shard_map/ppermute | solution.py:298
  29.9 8.3 %collective-permute-start.3 = (f32[8,128]{1,0:T(8,128)S(1)}, f32[8,128]{1,0:T(8,128)S(1)}, u32[]{:S(2)}, u32[]{:S(2)}) collective-permute-start(f32[8,128]{1,0:T(8,128)S(1)} %pad_maximum_fusion.1.refs_1_), channel_id=1, source_target_pairs={{0,192},{32,224},{64,256},{96,288},{128,320},{160,352},{192,384},{... | collective-permute-start | bytes 12296 | tf_op jit(solution)/shard_map/ppermute | solution.py:298
  31.8 7.1 %collective-permute-start.2 = (f32[8,128]{1,0:T(8,128)S(1)}, f32[8,128]{1,0:T(8,128)S(1)}, u32[]{:S(2)}, u32[]{:S(2)}) collective-permute-start(f32[8,128]{1,0:T(8,128)S(1)} %pad_maximum_fusion.1.refs_1_), channel_id=1, source_target_pairs={{0,320},{32,352},{64,384},{96,416},{128,448},{160,480},{192,0},{22... | collective-permute-start | bytes 12296 | tf_op jit(solution)/shard_map/ppermute | solution.py:298
  42.5 27.7 %collective-permute-start.8 = (bf16[2096,128]{1,0:T(8,128)(2,1)S(1)}, bf16[2096,128]{1,0:T(8,128)(2,1)S(1)}, u32[]{:S(2)}, u32[]{:S(2)}) collective-permute-start(bf16[2096,128]{1,0:T(8,128)(2,1)S(1)} %get-tuple-element.14.refs_0_), channel_id=1, source_target_pairs={{0,1},{1,2},{2,3},{3,4},{4,5},{5,6},{6,7},{7,8},{8,9},{9,10},{10,1... | collective-permute-start | bytes 1609736 | tf_op jit(solution)/shard_map/ppermute | solution.py:301
  46.2 24.0 %collective-permute-start.7 = (bf16[2096,128]{1,0:T(8,128)(2,1)S(1)}, bf16[2096,128]{1,0:T(8,128)(2,1)S(1)}, u32[]{:S(2)}, u32[]{:S(2)}) collective-permute-start(bf16[2096,128]{1,0:T(8,128)(2,1)S(1)} %get-tuple-element.14.refs_0_), channel_id=1, source_target_pairs={{0,31},{1,0},{2,1},{3,2},{4,3},{5,4},{6,5},{7,6},{8,7},{9,8},{10,9... | collective-permute-start | bytes 1609736 | tf_op jit(solution)/shard_map/ppermute | solution.py:301
  51.1 19.1 %collective-permute-start.6 = (bf16[2096,128]{1,0:T(8,128)(2,1)S(1)}, bf16[2096,128]{1,0:T(8,128)(2,1)S(1)}, u32[]{:S(2)}, u32[]{:S(2)}) collective-permute-start(bf16[2096,128]{1,0:T(8,128)(2,1)S(1)} %get-tuple-element.14.refs_0_), channel_id=1, source_target_pairs={{0,64},{32,96},{64,128},{96,160},{128,192},{160,224},{192,256},{22... | collective-permute-start | bytes 1609736 | tf_op jit(solution)/shard_map/ppermute | solution.py:298
  54.3 15.9 %collective-permute-start.4 = (bf16[2096,128]{1,0:T(8,128)(2,1)S(1)}, bf16[2096,128]{1,0:T(8,128)(2,1)S(1)}, u32[]{:S(2)}, u32[]{:S(2)}) collective-permute-start(bf16[2096,128]{1,0:T(8,128)(2,1)S(1)} %get-tuple-element.14.refs_0_), channel_id=1, source_target_pairs={{0,32},{32,0},{64,96},{96,64},{128,160},{160,128},{192,224},{224,1... | collective-permute-start | bytes 1609736 | tf_op jit(solution)/shard_map/ppermute | solution.py:320
  60.3 9.9 %collective-permute-start.5 = (bf16[1040,128]{1,0:T(8,128)(2,1)S(1)}, bf16[1040,128]{1,0:T(8,128)(2,1)S(1)}, u32[]{:S(2)}, u32[]{:S(2)}) collective-permute-start(bf16[1040,128]{1,0:T(8,128)(2,1)S(1)} %get-tuple-element.15), channel_id=1, source_target_pairs={{0,448},{32,480},{64,0},{96,32},{128,64},{160,96},{192,128},{224,1... | collective-permute-start | bytes 798728 | tf_op jit(solution)/shard_map/ppermute | solution.py:298
  70.3 5.8 %collective-permute-start.9 = (bf16[3120,128]{1,0:T(8,128)(2,1)S(1)}, bf16[3120,128]{1,0:T(8,128)(2,1)S(1)}, u32[]{:S(2)}, u32[]{:S(2)}) collective-permute-start(bf16[3120,128]{1,0:T(8,128)(2,1)S(1)} %pad_maximum_fusion), channel_id=1, source_target_pairs={{0,32},{32,0},{64,96},{96,64},{128,160},{160,128},{192,224},{224,1... | collective-permute-start | bytes 2396168 | tf_op jit(solution)/shard_map/ppermute | solution.py:324

commit v4 on v3

--- a/solution.py
+++ b/solution.py
@@ -243,7 +243,9 @@
         best.append(best_of(across_rows, across_bias, places, feat, blocks))
         numbers.append(stack_numbers(places, feat))
     table = slot_table(jnp.concatenate(best, axis=1), jnp.concatenate(numbers, axis=1), blocks)
-    out_ref[...] = jnp.maximum(table_ref[...], table)
+    table = jnp.maximum(table_ref[...], table)
+    for b in range(blocks):
+        out_ref[b] = jnp.broadcast_to(table[b : b + 1, :], (8, BLOCK))
 
 
 def vmem():
@@ -320,7 +322,7 @@
     twin = lax.ppermute(both, "group", swap)
     following, back = along_y(first, -1), along_y(both, 1)
     high, low = along_owner(both, -1), along_owner(both, 1)
-    twin, following, back, high, low = lax.optimization_barrier((twin, following, back, high, low))
+    following, back, high, low = lax.optimization_barrier((following, back, high, low))
     late = lax.ppermute(jnp.concatenate([back[: 2 * size], following], axis=0), "group", swap)
     table, bias = pl.pallas_call(
         lambda *refs: first_score_kernel(n_group, feat, *refs),
@@ -336,7 +338,7 @@
     )(both, twin, back, following, low, high)
     table = pl.pallas_call(
         lambda *refs: second_score_kernel(n_group, feat, *refs),
-        out_shape=jax.ShapeDtypeStruct((n_group, BLOCK), F32),
+        out_shape=jax.ShapeDtypeStruct((n_group, 8, BLOCK), F32),
         in_specs=[vmem()] * 6,
         out_specs=vmem(),
         compiler_params=PARAMS,
@@ -344,7 +346,7 @@
         name="score_rest",
     )(table, bias, low, high, back, late)
     shares = lax.all_to_all(table, "group", split_axis=0, concat_axis=0, tiled=True)
-    return jnp.max(shares, axis=0, keepdims=True)
+    return jnp.max(shares[:, :1], axis=0)
 
 
 def solution(mesh):

time: 92.5 us -> 89.7 us (0.970)
  starting transfers between devices: 52.9 us -> 56 us
  waiting for transfers between devices: 13.1 us -> 10 us
  blocking collectives: 14.2 us -> 11.4 us
    ppermute x1, starting transfers between devices: 2.7 us -> 7.05 us  [on_device(): lax.ppermute(jnp.concatenate([back[:2 * size], following], axis=0), 'grou...]
    ppermute x6, waiting for transfers between devices: 11.1 us -> 7.79 us  [along_y(): lax.ppermute(x, 'group', [(i, (i + 2 * hops) % n_group) for i in range(n_...]
    all_to_all x1, blocking collectives: 14.2 us -> 11.4 us  [on_device(): lax.all_to_all(table, 'group', split_axis=0, concat_axis=0, tiled=True)]
    ppermute x2, waiting for transfers between devices: 0.01 us -> 2.1 us  [along_owner(): lax.ppermute(x, 'owner', [(i, (i + hops) % n_owner) for i in range(n_owne...]
    all_to_all x1, waiting for transfers between devices: 2.06 us -> 0.11 us  [on_device(): lax.all_to_all(outgoing, 'owner', split_axis=0, concat_axis=0, tiled=True)]
    ppermute x2, starting transfers between devices: 8.6 us -> 7.32 us  [along_owner(): lax.ppermute(x, 'owner', [(i, (i + hops) % n_owner) for i in range(n_owne...]
where the time goes in v4:
time: 89.7 us; the launch traced here: 89.2 us
  starting transfers between devices  56 us (62%)
  blocking collectives  11.4 us (13%)
  Pallas kernels  10.9 us (12%)
  waiting for transfers between devices  10 us (11%)
    ppermute x6, starting transfers between devices, along_y(): lax.ppermute(x, 'group', [(i, (i + 2 * hops) % n_group) for i in range(n_...  21.4 us
    all_to_all x1, starting transfers between devices, on_device(): lax.all_to_all(outgoing, 'owner', split_axis=0, concat_axis=0, tiled=True)  13.7 us
    all_to_all x1, blocking collectives, on_device(): lax.all_to_all(table, 'group', split_axis=0, concat_axis=0, tiled=True)  11.4 us
    ppermute x6, waiting for transfers between devices, along_y(): lax.ppermute(x, 'group', [(i, (i + 2 * hops) % n_group) for i in range(n_...  7.79 us
    ppermute x2, starting transfers between devices, along_owner(): lax.ppermute(x, 'owner', [(i, (i + hops) % n_owner) for i in range(n_owne...  7.32 us
    ppermute x1, starting transfers between devices, on_device(): lax.ppermute(jnp.concatenate([back[:2 * size], following], axis=0), 'grou...  7.05 us
    ppermute x1, starting transfers between devices, on_device(): twin = lax.ppermute(both, 'group', swap)  6.55 us
    pallas_call x1, Pallas kernels, on_device(): pl.pallas_call(lambda *refs: send_kernel(n_owner, n_group, cap, 6, pieces...  5.16 us
  transfers between devices with their start and end apart: 11, of which 4 were waited for; matrix products, arithmetic and copies ran while one was open for 0% of the time, Pallas kernels for 3%

profile of v4, /device:TPU:1, one launch (start us, length us, event | category | flops | bytes accessed | tf_op | source)
XLA Modules:
  0.0 89.2 jit_solution(8117138110379702385)
XLA Ops:
  0.0 5.2 %send_rows.1 = bf16[32,104,128]{2,1,0:T(8,128)(2,1)} custom-call(s32[1,2048]{1,0:T(1,128)} %bitcast.7, s32[1,32]{1,0:T(1,128)} %bitcast.10, s32[1,2048]{1,0:T(1,128)} %bitcast.8, bf16[2048,1024]{1,0:T(8,128)(2,1)} %refs_3_.1), custom_call_target="tpu_custom_call" | custom-call | tf_op jit(solution)/shard_map/send_rows/pallas_call | solution.py:275
  5.2 0.0 copy-start
  5.2 13.7 %all-to-all-start = ((bf16[32,104,128]{2,1,0:T(8,128)(2,1)}), bf16[32,104,128]{2,1,0:T(8,128)(2,1)S(1)}, u32[]{:S(2)}, u32[]{:S(2)}) async-start(bf16[32,104,128]{2,1,0:T(8,128)(2,1)} %send_rows.1), calls=%async_computation | async-start | bytes 1703936 | tf_op jit(solution)/shard_map/all_to_all | solution.py:296
  18.9 5.1 %collective-permute-start.1 = (f32[8,128]{1,0:T(8,128)S(1)}, f32[8,128]{1,0:T(8,128)S(1)}, u32[]{:S(2)}, u32[]{:S(2)}) collective-permute-start(f32[8,128]{1,0:T(8,128)S(1)} %pad_convert_fusion), channel_id=1, source_target_pairs={{0,448},{32,480},{64,0},{96,32},{128,64},{160,96},{192,128},{224,1... | collective-permute-start | bytes 12296 | tf_op jit(solution)/shard_map/ppermute | solution.py:300
  24.0 1.9 %collective-permute-start = (f32[8,128]{1,0:T(8,128)S(1)}, f32[8,128]{1,0:T(8,128)S(1)}, u32[]{:S(2)}, u32[]{:S(2)}) collective-permute-start(f32[8,128]{1,0:T(8,128)S(1)} %pad_convert_fusion), channel_id=1, source_target_pairs={{0,64},{32,96},{64,128},{96,160},{128,192},{160,224},{192,256},{22... | collective-permute-start | bytes 12296 | tf_op jit(solution)/shard_map/ppermute | solution.py:300
  26.0 3.9 %collective-permute-done = f32[8,128]{1,0:T(8,128)S(1)} collective-permute-done((f32[8,128]{1,0:T(8,128)S(1)}, f32[8,128]{1,0:T(8,128)S(1)}, u32[]{:S(2)}, u32[]{:S(2)}) %collective-permute-start) | collective-permute-done | bytes 4128 | tf_op jit(solution)/shard_map/ppermute | solution.py:300
  29.9 3.3 %collective-permute-start.2 = (f32[8,128]{1,0:T(8,128)S(1)}, f32[8,128]{1,0:T(8,128)S(1)}, u32[]{:S(2)}, u32[]{:S(2)}) collective-permute-start(f32[8,128]{1,0:T(8,128)S(1)} %pad_maximum_fusion.1.refs_1_), channel_id=1, source_target_pairs={{0,320},{32,352},{64,384},{96,416},{128,448},{160,480},{192,0},{22... | collective-permute-start | bytes 12296 | tf_op jit(solution)/shard_map/ppermute | solution.py:300
  33.2 3.8 %collective-permute-start.3 = (f32[8,128]{1,0:T(8,128)S(1)}, f32[8,128]{1,0:T(8,128)S(1)}, u32[]{:S(2)}, u32[]{:S(2)}) collective-permute-start(f32[8,128]{1,0:T(8,128)S(1)} %pad_maximum_fusion.1.refs_1_), channel_id=1, source_target_pairs={{0,192},{32,224},{64,256},{96,288},{128,320},{160,352},{192,384},{... | collective-permute-start | bytes 12296 | tf_op jit(solution)/shard_map/ppermute | solution.py:300
  37.0 3.9 %collective-permute-done.3.refs_3_ = f32[8,128]{1,0:T(8,128)S(1)} collective-permute-done((f32[8,128]{1,0:T(8,128)S(1)}, f32[8,128]{1,0:T(8,128)S(1)}, u32[]{:S(2)}, u32[]{:S(2)}) %collective-permute-start.3) | collective-permute-done | bytes 4128 | tf_op jit(solution)/shard_map/ppermute | solution.py:300
  40.9 0.1 all-to-all-done.refs_0_
  41.0 1.5 %unit_rows.1 = (bf16[2096,128]{1,0:T(8,128)(2,1)S(1)}, bf16[1040,128]{1,0:T(8,128)(2,1)S(1)}) custom-call(bf16[32,104,128]{2,1,0:T(8,128)(2,1)S(1)} %all-to-all-done.refs_0_, f32[8,128]{1,0:T(8,128)S(1)} %pad_maximum_fusion.1.refs_1_, f32[8,128]{1,0:T(8,128)S(1)} %collective-permute-done.2.refs_2_, f32[8,128]{1,0:T(8,128)S(1)} %collective-permute-done.3.refs_3_), custom_call_target="tpu_custom_call" | custom-call | tf_op jit(solution)/shard_map/unit_rows/pallas_call | solution.py:310
  42.5 3.2 %collective-permute-start.6 = (bf16[2096,128]{1,0:T(8,128)(2,1)S(1)}, bf16[2096,128]{1,0:T(8,128)(2,1)S(1)}, u32[]{:S(2)}, u32[]{:S(2)}) collective-permute-start(bf16[2096,128]{1,0:T(8,128)(2,1)S(1)} %get-tuple-element.13.refs_0_), channel_id=1, source_target_pairs={{0,64},{32,96},{64,128},{96,160},{128,192},{160,224},{192,256},{22... | collective-permute-start | bytes 1609736 | tf_op jit(solution)/shard_map/ppermute | solution.py:300
  45.7 5.4 %collective-permute-start.7 = (bf16[2096,128]{1,0:T(8,128)(2,1)S(1)}, bf16[2096,128]{1,0:T(8,128)(2,1)S(1)}, u32[]{:S(2)}, u32[]{:S(2)}) collective-permute-start(bf16[2096,128]{1,0:T(8,128)(2,1)S(1)} %get-tuple-element.13.refs_0_), channel_id=1, source_target_pairs={{0,31},{1,0},{2,1},{3,2},{4,3},{5,4},{6,5},{7,6},{8,7},{9,8},{10,9... | collective-permute-start | bytes 1609736 | tf_op jit(solution)/shard_map/ppermute | solution.py:303
  51.1 1.9 %collective-permute-start.8 = (bf16[2096,128]{1,0:T(8,128)(2,1)S(1)}, bf16[2096,128]{1,0:T(8,128)(2,1)S(1)}, u32[]{:S(2)}, u32[]{:S(2)}) collective-permute-start(bf16[2096,128]{1,0:T(8,128)(2,1)S(1)} %get-tuple-element.13.refs_0_), channel_id=1, source_target_pairs={{0,1},{1,2},{2,3},{3,4},{4,5},{5,6},{6,7},{7,8},{8,9},{9,10},{10,1... | collective-permute-start | bytes 1609736 | tf_op jit(solution)/shard_map/ppermute | solution.py:303
  53.0 4.1 %collective-permute-start.5 = (bf16[1040,128]{1,0:T(8,128)(2,1)S(1)}, bf16[1040,128]{1,0:T(8,128)(2,1)S(1)}, u32[]{:S(2)}, u32[]{:S(2)}) collective-permute-start(bf16[1040,128]{1,0:T(8,128)(2,1)S(1)} %get-tuple-element.14), channel_id=1, source_target_pairs={{0,448},{32,480},{64,0},{96,32},{128,64},{160,96},{192,128},{224,1... | collective-permute-start | bytes 798728 | tf_op jit(solution)/shard_map/ppermute | solution.py:300
  57.1 6.5 %collective-permute-start.4 = (bf16[2096,128]{1,0:T(8,128)(2,1)S(1)}, bf16[2096,128]{1,0:T(8,128)(2,1)S(1)}, u32[]{:S(2)}, u32[]{:S(2)}) collective-permute-start(bf16[2096,128]{1,0:T(8,128)(2,1)S(1)} %get-tuple-element.13.refs_0_), channel_id=1, source_target_pairs={{0,32},{32,0},{64,96},{96,64},{128,160},{160,128},{192,224},{224,1... | collective-permute-start | bytes 1609736 | tf_op jit(solution)/shard_map/ppermute | solution.py:322
  63.6 0.0 collective-permute-done.5.refs_3_
  63.7 2.1 %collective-permute-done.8.refs_4_.refs_2_ = bf16[2096,128]{1,0:T(8,128)(2,1)S(1)} collective-permute-done((bf16[2096,128]{1,0:T(8,128)(2,1)S(1)}, bf16[2096,128]{1,0:T(8,128)(2,1)S(1)}, u32[]{:S(2)}, u32[]{:S(2)}) %collective-permute-start.8) | collective-permute-done | bytes 536608 | tf_op jit(solution)/shard_map/ppermute | solution.py:303
  65.8 0.1 pad_maximum_fusion
  65.9 7.1 %collective-permute-start.9 = (bf16[3120,128]{1,0:T(8,128)(2,1)S(1)}, bf16[3120,128]{1,0:T(8,128)(2,1)S(1)}, u32[]{:S(2)}, u32[]{:S(2)}) collective-permute-start(bf16[3120,128]{1,0:T(8,128)(2,1)S(1)} %pad_maximum_fusion), channel_id=1, source_target_pairs={{0,32},{32,0},{64,96},{96,64},{128,160},{160,128},{192,224},{224,1... | collective-permute-start | bytes 2396168 | tf_op jit(solution)/shard_map/ppermute | solution.py:326
  72.9 3.1 %score_rows.1 = (f32[16,128]{1,0:T(8,128)S(1)}, bf16[512,16]{1,0:T(8,128)(2,1)S(1)}) custom-call(bf16[2096,128]{1,0:T(8,128)(2,1)S(1)} %get-tuple-element.13.refs_0_, bf16[2096,128]{1,0:T(8,128)(2,1)S(1)} %collective-permute-done.4.refs_1_, bf16[2096,128]{1,0:T(8,128)(2,1)S(1)} %collective-permute-done.6.refs_2_.refs_4_, ...), custom_call_target="tpu_custom_call" | custom-call | flops 3000000000 | bytes 4000000 | tf_op jit(solution)/shard_map/score_rows/pallas_call | solution.py:327
  76.0 1.2 %score_rest.1 = f32[16,8,128]{2,1,0:T(8,128)S(1)} custom-call(f32[16,128]{1,0:T(8,128)S(1)} %get-tuple-element.19.refs_0_, bf16[512,16]{1,0:T(8,128)(2,1)S(1)} %get-tuple-element.20.refs_1_, bf16[2096,128]{1,0:T(8,128)(2,1)S(1)} %collective-permute-done.8.refs_4_.refs_2_, bf16[2096,128]{1,0:T(8,128)(2,1)S(1)} %collective-permute-done.7.refs_5_.refs_3_, ...), custom_call_target="tpu_custom_call" | custom-call | flops 500000000 | bytes 2000000 | tf_op jit(solution)/shard_map/score_rest/pallas_call | solution.py:339
  77.2 11.4 %all_to_all.10 = f32[16,8,128]{2,1,0:T(8,128)S(1)} all-to-all(f32[16,8,128]{2,1,0:T(8,128)S(1)} %score_rest.1), channel_id=1, replica_groups=mesh['group'=16,'owner'=32] {'group'}, dimensions={0} | all-to-all | bytes 131072 | tf_op jit(solution)/shard_map/all_to_all | solution.py:348
  88.6 0.5 slice_reduce_fusion
  (13 shorter events, 0.1 us)
Async XLA Ops:
  5.2 13.7 %copy-start = (s32[1,1,49,2]{2,3,1,0:T(2,128)S(1)}, s32[1,1,49,2]{2,3,1,0:T(2,128)}, u32[]{:S(2)}) copy-start(s32[1,1,49,2]{2,3,1,0:T(2,128)} %param.9) | copy-start | bytes 1180
  5.2 35.8 %all-to-all-start = ((bf16[32,104,128]{2,1,0:T(8,128)(2,1)}), bf16[32,104,128]{2,1,0:T(8,128)(2,1)S(1)}, u32[]{:S(2)}, u32[]{:S(2)}) async-start(bf16[32,104,128]{2,1,0:T(8,128)(2,1)} %send_rows.1), calls=%async_computation | async-start | bytes 1703936 | tf_op jit(solution)/shard_map/all_to_all | solution.py:296
  18.9 7.1 %collective-permute-start.1 = (f32[8,128]{1,0:T(8,128)S(1)}, f32[8,128]{1,0:T(8,128)S(1)}, u32[]{:S(2)}, u32[]{:S(2)}) collective-permute-start(f32[8,128]{1,0:T(8,128)S(1)} %pad_convert_fusion), channel_id=1, source_target_pairs={{0,448},{32,480},{64,0},{96,32},{128,64},{160,96},{192,128},{224,1... | collective-permute-start | bytes 12296 | tf_op jit(solution)/shard_map/ppermute | solution.py:300
  24.0 5.9 %collective-permute-start = (f32[8,128]{1,0:T(8,128)S(1)}, f32[8,128]{1,0:T(8,128)S(1)}, u32[]{:S(2)}, u32[]{:S(2)}) collective-permute-start(f32[8,128]{1,0:T(8,128)S(1)} %pad_convert_fusion), channel_id=1, source_target_pairs={{0,64},{32,96},{64,128},{96,160},{128,192},{160,224},{192,256},{22... | collective-permute-start | bytes 12296 | tf_op jit(solution)/shard_map/ppermute | solution.py:300
  29.9 7.1 %collective-permute-start.2 = (f32[8,128]{1,0:T(8,128)S(1)}, f32[8,128]{1,0:T(8,128)S(1)}, u32[]{:S(2)}, u32[]{:S(2)}) collective-permute-start(f32[8,128]{1,0:T(8,128)S(1)} %pad_maximum_fusion.1.refs_1_), channel_id=1, source_target_pairs={{0,320},{32,352},{64,384},{96,416},{128,448},{160,480},{192,0},{22... | collective-permute-start | bytes 12296 | tf_op jit(solution)/shard_map/ppermute | solution.py:300
  33.2 7.7 %collective-permute-start.3 = (f32[8,128]{1,0:T(8,128)S(1)}, f32[8,128]{1,0:T(8,128)S(1)}, u32[]{:S(2)}, u32[]{:S(2)}) collective-permute-start(f32[8,128]{1,0:T(8,128)S(1)} %pad_maximum_fusion.1.refs_1_), channel_id=1, source_target_pairs={{0,192},{32,224},{64,256},{96,288},{128,320},{160,352},{192,384},{... | collective-permute-start | bytes 12296 | tf_op jit(solution)/shard_map/ppermute | solution.py:300
  42.5 21.2 %collective-permute-start.6 = (bf16[2096,128]{1,0:T(8,128)(2,1)S(1)}, bf16[2096,128]{1,0:T(8,128)(2,1)S(1)}, u32[]{:S(2)}, u32[]{:S(2)}) collective-permute-start(bf16[2096,128]{1,0:T(8,128)(2,1)S(1)} %get-tuple-element.13.refs_0_), channel_id=1, source_target_pairs={{0,64},{32,96},{64,128},{96,160},{128,192},{160,224},{192,256},{22... | collective-permute-start | bytes 1609736 | tf_op jit(solution)/shard_map/ppermute | solution.py:300
  45.7 18.0 %collective-permute-start.7 = (bf16[2096,128]{1,0:T(8,128)(2,1)S(1)}, bf16[2096,128]{1,0:T(8,128)(2,1)S(1)}, u32[]{:S(2)}, u32[]{:S(2)}) collective-permute-start(bf16[2096,128]{1,0:T(8,128)(2,1)S(1)} %get-tuple-element.13.refs_0_), channel_id=1, source_target_pairs={{0,31},{1,0},{2,1},{3,2},{4,3},{5,4},{6,5},{7,6},{8,7},{9,8},{10,9... | collective-permute-start | bytes 1609736 | tf_op jit(solution)/shard_map/ppermute | solution.py:303
  51.1 14.7 %collective-permute-start.8 = (bf16[2096,128]{1,0:T(8,128)(2,1)S(1)}, bf16[2096,128]{1,0:T(8,128)(2,1)S(1)}, u32[]{:S(2)}, u32[]{:S(2)}) collective-permute-start(bf16[2096,128]{1,0:T(8,128)(2,1)S(1)} %get-tuple-element.13.refs_0_), channel_id=1, source_target_pairs={{0,1},{1,2},{2,3},{3,4},{4,5},{5,6},{6,7},{7,8},{8,9},{9,10},{10,1... | collective-permute-start | bytes 1609736 | tf_op jit(solution)/shard_map/ppermute | solution.py:303
  53.0 10.6 %collective-permute-start.5 = (bf16[1040,128]{1,0:T(8,128)(2,1)S(1)}, bf16[1040,128]{1,0:T(8,128)(2,1)S(1)}, u32[]{:S(2)}, u32[]{:S(2)}) collective-permute-start(bf16[1040,128]{1,0:T(8,128)(2,1)S(1)} %get-tuple-element.14), channel_id=1, source_target_pairs={{0,448},{32,480},{64,0},{96,32},{128,64},{160,96},{192,128},{224,1... | collective-permute-start | bytes 798728 | tf_op jit(solution)/shard_map/ppermute | solution.py:300
  57.1 15.8 %collective-permute-start.4 = (bf16[2096,128]{1,0:T(8,128)(2,1)S(1)}, bf16[2096,128]{1,0:T(8,128)(2,1)S(1)}, u32[]{:S(2)}, u32[]{:S(2)}) collective-permute-start(bf16[2096,128]{1,0:T(8,128)(2,1)S(1)} %get-tuple-element.13.refs_0_), channel_id=1, source_target_pairs={{0,32},{32,0},{64,96},{96,64},{128,160},{160,128},{192,224},{224,1... | collective-permute-start | bytes 1609736 | tf_op jit(solution)/shard_map/ppermute | solution.py:322
  65.9 10.2 %collective-permute-start.9 = (bf16[3120,128]{1,0:T(8,128)(2,1)S(1)}, bf16[3120,128]{1,0:T(8,128)(2,1)S(1)}, u32[]{:S(2)}, u32[]{:S(2)}) collective-permute-start(bf16[3120,128]{1,0:T(8,128)(2,1)S(1)} %pad_maximum_fusion), channel_id=1, source_target_pairs={{0,32},{32,0},{64,96},{96,64},{128,160},{160,128},{192,224},{224,1... | collective-permute-start | bytes 2396168 | tf_op jit(solution)/shard_map/ppermute | solution.py:326

commit v5 on v4

--- a/solution.py
+++ b/solution.py
@@ -81,25 +81,35 @@
     slot = slot_ref[...]
     high = (slot // BLOCK + 1).astype(F32)
     low = (slot & (BLOCK - 1)).astype(F32)
-    at_entry = iota((LANES, rows), 0) == entry
-    meta_high = mm_nt(to, jnp.where(at_entry, high, 0.0).astype(BF16)).astype(BF16)
-    meta_low = mm_nt(to, jnp.where(at_entry, low, 0.0).astype(BF16)).astype(BF16)
+    width = 16
+    row = iota((2 * width, rows), 0)
+    values = jnp.where((row & (width - 1)) == entry, jnp.where(row < width, high, low), 0.0).astype(BF16)
+    meta = mm_nt(to, values).astype(BF16)
     line = iota((n_owner * META, n_owner), 0)
     peer = iota((n_owner * META, n_owner), 1)
-    meta = mm(ones_where(line == peer * META), meta_high) + mm(ones_where(line == peer * META + 1), meta_low)
+    meta = mm(ones_where(line // META == peer), meta)
+    line = iota((n_owner * META, 2 * width), 0) & (META - 1)
+    meta = jnp.where(iota((n_owner * META, 2 * width), 1) // width == line, meta, 0.0).astype(BF16)
+    column = iota((2 * width, LANES), 0) & (width - 1)
+    meta = mm(meta, ones_where(column == iota((2 * width, LANES), 1)))
     out_ref[:, lines * chunks :, :] = meta.reshape(n_owner, META, LANES).astype(BF16)
     select = ones_where(iota((n_owner * lines, rows), 0) == goal)
     total = None
-    for i, copy in enumerate(copies):
+    for i, copy in enumerate(copies[:-1]):
         copy.wait()
         part = mm(select[:, i * step : (i + 1) * step], emb[pl.ds(i * step, step), :])
         total = part if total is None else total + part
-    for k in range(chunks):
-        wide[pl.ds(k, n_owner * lines, chunks), :] = total[:, k * LANES : (k + 1) * LANES]
+    copies[-1].wait()
+    last = rows - step
+    for k in range(0, chunks, 2):
+        part = total[:, k * LANES : (k + 2) * LANES]
+        part += mm(select[:, last:], emb[pl.ds(last, step), pl.ds(k * LANES, 2 * LANES)])
+        for h in range(2):
+            wide[pl.ds(k + h, n_owner * lines, chunks), :] = part[:, h * LANES : (h + 1) * LANES]
     out_ref[:, : lines * chunks, :] = wide[...].reshape(n_owner, lines * chunks, LANES).astype(BF16)
 
 
-def receive_kernel(n_owner, cap, feat, in_ref, near_ref, up_ref, down_ref, both_ref, first_ref, wide):
+def receive_kernel(n_owner, cap, feat, in_ref, here_ref, there_ref, both_ref, first_ref, wide):
     chunks = feat // LANES
     per_peer = UNITS * cap
     lines = n_owner * per_peer
@@ -143,7 +153,7 @@
         both_ref[pl.ds(n * size + feat, PAY_META), :] = numbers
         if n == 0:
             first_ref[pl.ds(feat, PAY_META), :] = numbers
-    lists = jnp.concatenate([near_ref[0:6, :], up_ref[0:6, :], down_ref[2:6, :]], axis=0)
+    lists = jnp.concatenate([here_ref[...], there_ref[...]], axis=0)
     both_ref[pl.ds(UNITS * size, PAY_META), :] = lists.astype(BF16)
 
 
@@ -193,7 +203,7 @@
     return jnp.where(filled > 0.5, result, -2.0)
 
 
-def first_score_kernel(blocks, feat, own_ref, twin_ref, back_ref, next_ref, low_ref, high_ref, out_ref, bias_ref):
+def first_score_kernel(blocks, feat, own_ref, twin_ref, back_ref, next_ref, left_ref, right_ref, out_ref, bias_ref):
     size = feat + PAY_META
     lists = [r[pl.ds(UNITS * size, PAY_META), :].astype(F32) for r in (own_ref, twin_ref)]
     count = PAY_META // 2
@@ -208,39 +218,41 @@
     paired = mm_nt(ones_where(wide_rows == second), ones_where(first_rows == first))
     paired += mm_nt(ones_where(wide_rows == first + blocks), ones_where(first_rows == second - blocks))
     penalty = jnp.where(paired > 0.5, 0.0, -4.0).astype(BF16)
-    across = [(low_ref, 0), (low_ref, size), (high_ref, 0), (high_ref, size)]
+    across = [(left_ref, 0), (right_ref, 0), (left_ref, size), (right_ref, size)]
     marks = stack_numbers(across, feat)[0:1, :]
-    marks += jnp.where(iota(marks.shape, 1) < 2 * BLOCK, 0, 2 * blocks)
+    odd = lax.axis_index("owner") & 1
+    marks += 2 * blocks * jnp.where((iota(marks.shape, 1) & BLOCK) == 0, 1 - odd, odd)
     across_bias = bias_of(penalty, marks)
     bias_ref[...] = across_bias
     across_rows = stack_rows(across, feat)
-    inside = [(back_ref, 0), (next_ref, 0), (own_ref, 0), (twin_ref, 0), (own_ref, size), (twin_ref, size)]
+    inside = [(next_ref, 0), (back_ref, 0), (own_ref, 0), (twin_ref, 0), (own_ref, size), (twin_ref, size)]
     inside_bias = bias_of(penalty, stack_numbers(inside, feat)[0:1, :] + blocks)
     inside_rows = stack_rows(inside, feat)
-    row, lane = iota((6 * BLOCK, 2 * BLOCK), 0), iota((6 * BLOCK, 2 * BLOCK), 1)
-    same = row == lane + jnp.where(lane < BLOCK, 2 * BLOCK, 3 * BLOCK)
+    row, lane = iota((5 * BLOCK, 2 * BLOCK), 0), iota((5 * BLOCK, 2 * BLOCK), 1)
     groups = [
-        ([(own_ref, 0), (own_ref, size)], 0, 6, same),
-        ([(twin_ref, 0), (twin_ref, size)], 0, 3, None),
-        ([(back_ref, 0), (next_ref, 0)], 2, 6, None),
+        ([(own_ref, 0), (twin_ref, 0)], 4, 1, 6, row == lane + BLOCK),
+        ([(own_ref, size), (twin_ref, size)], 2, 0, 3, None),
+        ([(back_ref, 0), (next_ref, 0)], 4, 2, 6, None),
     ]
     best, numbers = [], []
-    for places, low, high, equal in groups:
+    for places, count, low, high, equal in groups:
         part = slice(low * BLOCK, high * BLOCK)
-        one = best_of(across_rows, across_bias, places, feat, blocks)
+        outer = slice(0, count * BLOCK)
+        one = best_of(across_rows[outer], across_bias[outer], places, feat, blocks)
         two = best_of(inside_rows[part], inside_bias[part], places, feat, blocks, equal)
         best.append(jnp.maximum(one, two))
         numbers.append(stack_numbers(places, feat))
     out_ref[...] = slot_table(jnp.concatenate(best, axis=1), jnp.concatenate(numbers, axis=1), blocks)
 
 
-def second_score_kernel(blocks, feat, table_ref, bias_ref, low_ref, high_ref, back_ref, late_ref, out_ref):
+def second_score_kernel(blocks, feat, table_ref, bias_ref, left_ref, right_ref, back_ref, late_ref, out_ref):
     size = feat + PAY_META
-    across_rows = stack_rows([(low_ref, 0), (low_ref, size), (high_ref, 0), (high_ref, size)], feat)
+    across_rows = stack_rows([(left_ref, 0), (right_ref, 0), (left_ref, size), (right_ref, size)], feat)
     across_bias = bias_ref[...]
     best, numbers = [], []
-    for places in ([(back_ref, size), (late_ref, size)], [(late_ref, 0), (late_ref, 2 * size)]):
-        best.append(best_of(across_rows, across_bias, places, feat, blocks))
+    for places, count in (([(back_ref, size), (late_ref, size)], 2), ([(late_ref, 0), (late_ref, 2 * size)], 4)):
+        outer = slice(0, count * BLOCK)
+        best.append(best_of(across_rows[outer], across_bias[outer], places, feat, blocks))
         numbers.append(stack_numbers(places, feat))
     table = slot_table(jnp.concatenate(best, axis=1), jnp.concatenate(numbers, axis=1), blocks)
     table = jnp.maximum(table_ref[...], table)
@@ -296,33 +308,36 @@
     arrived = lax.all_to_all(outgoing, "owner", split_axis=0, concat_axis=0, tiled=True)
     swap = [(i, i ^ 1) for i in range(n_group)]
 
-    def along_y(x, hops):
-        return lax.ppermute(x, "group", [(i, (i + 2 * hops) % n_group) for i in range(n_group)])
-
-    def along_owner(x, hops):
-        return lax.ppermute(x, "owner", [(i, (i + hops) % n_owner) for i in range(n_owner)])
+    def along_y(x, partner):
+        return lax.ppermute(x, "group", [(i, 2 * (partner(i // 2) % (n_group // 2)) + i % 2) for i in range(n_group)])
+
+    def along_owner(x, partner):
+        return lax.ppermute(x, "owner", [(i, partner(i) % n_owner) for i in range(n_owner)])
 
     entries = pairs.reshape(-1, 2)
-    listed = jnp.pad(entries.T, ((0, 6), (0, LANES - entries.shape[0])), constant_values=-1).astype(F32)
-    before, after = along_y(listed, 1), along_y(listed, -1)
-    near = jnp.concatenate([before[0:2], listed[0:2], after[0:2], listed[6:8]], axis=0)
-    down, up = along_y(near, 3), along_y(near, -3)
+    here = jnp.pad(entries.T, ((0, 0), (0, LANES - entries.shape[0])), constant_values=-1).astype(F32)
+    blank = jnp.full((6, LANES), -1.0, F32)
+    there = along_y(jnp.concatenate([here, blank], axis=0), lambda y: y ^ 1)
+    here = jnp.concatenate([here, there[:2]], axis=0)
+    there = along_y(jnp.concatenate([here, blank[:4]], axis=0), lambda y: y ^ 2)
+    here = jnp.concatenate([here, there[:4]], axis=0)
+    there = along_y(here, lambda y: y ^ 4)
     both, first = pl.pallas_call(
         lambda *refs: receive_kernel(n_owner, cap, feat, *refs),
         out_shape=[
             jax.ShapeDtypeStruct((UNITS * size + PAY_META, LANES), BF16),
             jax.ShapeDtypeStruct((size, LANES), BF16),
         ],
-        in_specs=[vmem()] * 4,
+        in_specs=[vmem()] * 3,
         out_specs=[vmem()] * 2,
         scratch_shapes=[pltpu.VMEM((n_owner * lines * chunks, LANES), F32)],
         compiler_params=PARAMS,
         name="unit_rows",
-    )(arrived, near, up, down)
+    )(arrived, here, there)
     twin = lax.ppermute(both, "group", swap)
-    following, back = along_y(first, -1), along_y(both, 1)
-    high, low = along_owner(both, -1), along_owner(both, 1)
-    following, back, high, low = lax.optimization_barrier((following, back, high, low))
+    following, back = along_y(first, lambda y: y - 1), along_y(both, lambda y: y + 1)
+    left, right = along_owner(both, lambda o: o ^ 1), along_owner(both, lambda o: o + 2 * (o & 1) - 1)
+    following, right, back, left = lax.optimization_barrier((following, right, back, left))
     late = lax.ppermute(jnp.concatenate([back[: 2 * size], following], axis=0), "group", swap)
     table, bias = pl.pallas_call(
         lambda *refs: first_score_kernel(n_group, feat, *refs),
@@ -335,7 +350,7 @@
         compiler_params=PARAMS,
         cost_estimate=cost(3 * 10**9, 4 * 10**6),
         name="score_rows",
-    )(both, twin, back, following, low, high)
+    )(both, twin, back, following, left, right)
     table = pl.pallas_call(
         lambda *refs: second_score_kernel(n_group, feat, *refs),
         out_shape=jax.ShapeDtypeStruct((n_group, 8, BLOCK), F32),
@@ -344,7 +359,7 @@
         compiler_params=PARAMS,
         cost_estimate=cost(5 * 10**8, 2 * 10**6),
         name="score_rest",
-    )(table, bias, low, high, back, late)
+    )(table, bias, left, right, back, late)
     shares = lax.all_to_all(table, "group", split_axis=0, concat_axis=0, tiled=True)
     return jnp.max(shares[:, :1], axis=0)
 

time: 89.7 us -> 86.4 us (0.963)
  waiting for transfers between devices: 10 us -> 7.03 us
  blocking collectives: 11.4 us -> 13.9 us
  starting transfers between devices: 56 us -> 53.5 us
    ppermute x8 -> x7, waiting for transfers between devices: 9.89 us -> 3.8 us  [the longest x5 3.79 us: along_y(): lax.ppermute(x, 'group', [(i, 2 * (partner(i // 2) % (n_group // 2)) + i...]
    all_to_all x1, waiting for transfers between devices: 0.11 us -> 3.23 us  [on_device(): lax.all_to_all(outgoing, 'owner', split_axis=0, concat_axis=0, tiled=True)]
    all_to_all x1, blocking collectives: 11.4 us -> 13.9 us  [on_device(): lax.all_to_all(table, 'group', split_axis=0, concat_axis=0, tiled=True)]
    ppermute x1, starting transfers between devices: 6.55 us -> 5.25 us  [on_device(): twin = lax.ppermute(both, 'group', swap)]
    ppermute x1, starting transfers between devices: 7.05 us -> 5.91 us  [on_device(): lax.ppermute(jnp.concatenate([back[:2 * size], following], axis=0), 'grou...]
    ppermute x8 -> x7, starting transfers between devices: 28.7 us -> 28.6 us  [the longest x5 21.7 us: along_y(): lax.ppermute(x, 'group', [(i, 2 * (partner(i // 2) % (n_group // 2)) + i...]
  transfers between devices with their start and end apart: 11 -> 10, of which waited for: 4 -> 4; matrix products, arithmetic and copies ran while one was open for 0% -> 0% of each run, Pallas kernels for 3% -> 3%
where the time goes in v5:
time: 86.4 us; the launch traced here: 85.9 us
  starting transfers between devices  53.5 us (62%)
  blocking collectives  13.9 us (16%)
  Pallas kernels  10.4 us (12%)
  waiting for transfers between devices  7.03 us (8%)
    ppermute x5, starting transfers between devices, along_y(): lax.ppermute(x, 'group', [(i, 2 * (partner(i // 2) % (n_group // 2)) + i...  21.7 us
    all_to_all x1, blocking collectives, on_device(): lax.all_to_all(table, 'group', split_axis=0, concat_axis=0, tiled=True)  13.9 us
    all_to_all x1, starting transfers between devices, on_device(): lax.all_to_all(outgoing, 'owner', split_axis=0, concat_axis=0, tiled=True)  13.7 us
    ppermute x2, starting transfers between devices, along_owner(): lax.ppermute(x, 'owner', [(i, partner(i) % n_owner) for i in range(n_owne...  6.89 us
    ppermute x1, starting transfers between devices, on_device(): lax.ppermute(jnp.concatenate([back[:2 * size], following], axis=0), 'grou...  5.91 us
    ppermute x1, starting transfers between devices, on_device(): twin = lax.ppermute(both, 'group', swap)  5.25 us
    pallas_call x1, Pallas kernels, on_device(): pl.pallas_call(lambda *refs: send_kernel(n_owner, n_group, cap, 6, pieces...  4.9 us
    ppermute x5, waiting for transfers between devices, along_y(): lax.ppermute(x, 'group', [(i, 2 * (partner(i // 2) % (n_group // 2)) + i...  3.79 us
  transfers between devices with their start and end apart: 10, of which 4 were waited for; matrix products, arithmetic and copies ran while one was open for 0% of the time, Pallas kernels for 3%

profile of v5, /device:TPU:1, one launch (start us, length us, event | category | flops | bytes accessed | tf_op | source)
XLA Modules:
  0.0 85.9 jit_solution(17233932315530610387)
XLA Ops:
  0.0 4.9 %send_rows.1 = bf16[32,104,128]{2,1,0:T(8,128)(2,1)} custom-call(s32[1,2048]{1,0:T(1,128)} %bitcast.7, s32[1,32]{1,0:T(1,128)} %bitcast.10, s32[1,2048]{1,0:T(1,128)} %bitcast.8, bf16[2048,1024]{1,0:T(8,128)(2,1)} %refs_3_.1), custom_call_target="tpu_custom_call" | custom-call | tf_op jit(solution)/shard_map/send_rows/pallas_call | solution.py:287
  4.9 0.0 copy-start
  4.9 13.7 %all-to-all-start = ((bf16[32,104,128]{2,1,0:T(8,128)(2,1)}), bf16[32,104,128]{2,1,0:T(8,128)(2,1)S(1)}, u32[]{:S(2)}, u32[]{:S(2)}) async-start(bf16[32,104,128]{2,1,0:T(8,128)(2,1)} %send_rows.1), calls=%async_computation | async-start | bytes 1703936 | tf_op jit(solution)/shard_map/all_to_all | solution.py:308
  18.7 3.2 %collective-permute-start = (f32[8,128]{1,0:T(8,128)S(1)}, f32[8,128]{1,0:T(8,128)S(1)}, u32[]{:S(2)}, u32[]{:S(2)}) collective-permute-start(f32[8,128]{1,0:T(8,128)S(1)} %concatenate.15), channel_id=1, source_target_pairs={{0,64},{32,96},{64,0},{96,32},{128,192},{160,224},{192,128},{224,1... | collective-permute-start | bytes 12296 | tf_op jit(solution)/shard_map/ppermute | solution.py:312
  21.9 0.1 pad.13.clone
  22.0 1.3 %collective-permute-done = f32[8,128]{1,0:T(8,128)S(1)} collective-permute-done((f32[8,128]{1,0:T(8,128)S(1)}, f32[8,128]{1,0:T(8,128)S(1)}, u32[]{:S(2)}, u32[]{:S(2)}) %collective-permute-start) | collective-permute-done | bytes 4128 | tf_op jit(solution)/shard_map/ppermute | solution.py:312
  23.3 0.1 fusion
  23.4 4.2 %collective-permute-start.1 = (f32[8,128]{1,0:T(8,128)S(1)}, f32[8,128]{1,0:T(8,128)S(1)}, u32[]{:S(2)}, u32[]{:S(2)}) collective-permute-start(f32[8,128]{1,0:T(8,128)S(1)} %fusion), channel_id=1, source_target_pairs={{0,128},{32,160},{64,192},{96,224},{128,0},{160,32},{192,64},{224,... | collective-permute-start | bytes 12296 | tf_op jit(solution)/shard_map/ppermute | solution.py:312
  27.6 1.3 %collective-permute-done.1 = f32[8,128]{1,0:T(8,128)S(1)} collective-permute-done((f32[8,128]{1,0:T(8,128)S(1)}, f32[8,128]{1,0:T(8,128)S(1)}, u32[]{:S(2)}, u32[]{:S(2)}) %collective-permute-start.1) | collective-permute-done | bytes 4128 | tf_op jit(solution)/shard_map/ppermute | solution.py:312
  29.0 7.4 %collective-permute-start.2 = (f32[8,128]{1,0:T(8,128)S(1)}, f32[8,128]{1,0:T(8,128)S(1)}, u32[]{:S(2)}, u32[]{:S(2)}) collective-permute-start(f32[8,128]{1,0:T(8,128)S(1)} %pad_maximum_fusion.1.refs_1_), channel_id=1, source_target_pairs={{0,256},{32,288},{64,320},{96,352},{128,384},{160,416},{192,448},{... | collective-permute-start | bytes 12296 | tf_op jit(solution)/shard_map/ppermute | solution.py:312
  36.4 1.1 %collective-permute-done.2.refs_2_ = f32[8,128]{1,0:T(8,128)S(1)} collective-permute-done((f32[8,128]{1,0:T(8,128)S(1)}, f32[8,128]{1,0:T(8,128)S(1)}, u32[]{:S(2)}, u32[]{:S(2)}) %collective-permute-start.2) | collective-permute-done | bytes 4128 | tf_op jit(solution)/shard_map/ppermute | solution.py:312
  37.5 3.2 %all-to-all-done.refs_0_ = bf16[32,104,128]{2,1,0:T(8,128)(2,1)S(1)} async-done(((bf16[32,104,128]{2,1,0:T(8,128)(2,1)}), bf16[32,104,128]{2,1,0:T(8,128)(2,1)S(1)}, u32[]{:S(2)}, u32[]{:S(2)}) %all-to-all-start) | async-done | bytes 852000 | tf_op jit(solution)/shard_map/all_to_all | solution.py:308
  40.8 1.5 %unit_rows.1 = (bf16[2096,128]{1,0:T(8,128)(2,1)S(1)}, bf16[1040,128]{1,0:T(8,128)(2,1)S(1)}) custom-call(bf16[32,104,128]{2,1,0:T(8,128)(2,1)S(1)} %all-to-all-done.refs_0_, f32[8,128]{1,0:T(8,128)S(1)} %pad_maximum_fusion.1.refs_1_, f32[8,128]{1,0:T(8,128)S(1)} %collective-permute-done.2.refs_2_), custom_call_target="tpu_custom_call" | custom-call | tf_op jit(solution)/shard_map/unit_rows/pallas_call | solution.py:325
  42.2 3.5 %collective-permute-start.5 = (bf16[2096,128]{1,0:T(8,128)(2,1)S(1)}, bf16[2096,128]{1,0:T(8,128)(2,1)S(1)}, u32[]{:S(2)}, u32[]{:S(2)}) collective-permute-start(bf16[2096,128]{1,0:T(8,128)(2,1)S(1)} %get-tuple-element.13.refs_0_), channel_id=1, source_target_pairs={{0,31},{1,2},{2,1},{3,4},{4,3},{5,6},{6,5},{7,8},{8,7},{9,10},{10,... | collective-permute-start | bytes 1609736 | tf_op jit(solution)/shard_map/ppermute | solution.py:315
  45.7 3.0 %collective-permute-start.6 = (bf16[2096,128]{1,0:T(8,128)(2,1)S(1)}, bf16[2096,128]{1,0:T(8,128)(2,1)S(1)}, u32[]{:S(2)}, u32[]{:S(2)}) collective-permute-start(bf16[2096,128]{1,0:T(8,128)(2,1)S(1)} %get-tuple-element.13.refs_0_), channel_id=1, source_target_pairs={{0,64},{32,96},{64,128},{96,160},{128,192},{160,224},{192,256},{22... | collective-permute-start | bytes 1609736 | tf_op jit(solution)/shard_map/ppermute | solution.py:312
  48.8 3.4 %collective-permute-start.7 = (bf16[2096,128]{1,0:T(8,128)(2,1)S(1)}, bf16[2096,128]{1,0:T(8,128)(2,1)S(1)}, u32[]{:S(2)}, u32[]{:S(2)}) collective-permute-start(bf16[2096,128]{1,0:T(8,128)(2,1)S(1)} %get-tuple-element.13.refs_0_), channel_id=1, source_target_pairs={{0,1},{1,0},{2,3},{3,2},{4,5},{5,4},{6,7},{7,6},{8,9},{9,8},{10,11... | collective-permute-start | bytes 1609736 | tf_op jit(solution)/shard_map/ppermute | solution.py:315
  52.2 3.8 %collective-permute-start.4 = (bf16[1040,128]{1,0:T(8,128)(2,1)S(1)}, bf16[1040,128]{1,0:T(8,128)(2,1)S(1)}, u32[]{:S(2)}, u32[]{:S(2)}) collective-permute-start(bf16[1040,128]{1,0:T(8,128)(2,1)S(1)} %get-tuple-element.14), channel_id=1, source_target_pairs={{0,448},{32,480},{64,0},{96,32},{128,64},{160,96},{192,128},{224,1... | collective-permute-start | bytes 798728 | tf_op jit(solution)/shard_map/ppermute | solution.py:312
  56.0 5.2 %collective-permute-start.3 = (bf16[2096,128]{1,0:T(8,128)(2,1)S(1)}, bf16[2096,128]{1,0:T(8,128)(2,1)S(1)}, u32[]{:S(2)}, u32[]{:S(2)}) collective-permute-start(bf16[2096,128]{1,0:T(8,128)(2,1)S(1)} %get-tuple-element.13.refs_0_), channel_id=1, source_target_pairs={{0,32},{32,0},{64,96},{96,64},{128,160},{160,128},{192,224},{224,1... | collective-permute-start | bytes 1609736 | tf_op jit(solution)/shard_map/ppermute | solution.py:337
  61.3 0.1 pad_maximum_fusion
  61.4 5.9 %collective-permute-start.8 = (bf16[3120,128]{1,0:T(8,128)(2,1)S(1)}, bf16[3120,128]{1,0:T(8,128)(2,1)S(1)}, u32[]{:S(2)}, u32[]{:S(2)}) collective-permute-start(bf16[3120,128]{1,0:T(8,128)(2,1)S(1)} %pad_maximum_fusion), channel_id=1, source_target_pairs={{0,32},{32,0},{64,96},{96,64},{128,160},{160,128},{192,224},{224,1... | collective-permute-start | bytes 2396168 | tf_op jit(solution)/shard_map/ppermute | solution.py:341
  67.3 3.0 %score_rows.1 = (f32[16,128]{1,0:T(8,128)S(1)}, bf16[512,16]{1,0:T(8,128)(2,1)S(1)}) custom-call(bf16[2096,128]{1,0:T(8,128)(2,1)S(1)} %get-tuple-element.13.refs_0_, bf16[2096,128]{1,0:T(8,128)(2,1)S(1)} %collective-permute-done.3.refs_1_, bf16[2096,128]{1,0:T(8,128)(2,1)S(1)} %collective-permute-done.6.refs_2_.refs_4_, ...), custom_call_target="tpu_custom_call" | custom-call | flops 3000000000 | bytes 4000000 | tf_op jit(solution)/shard_map/score_rows/pallas_call | solution.py:342
  70.3 1.0 %score_rest.1 = f32[16,8,128]{2,1,0:T(8,128)S(1)} custom-call(f32[16,128]{1,0:T(8,128)S(1)} %get-tuple-element.19.refs_0_, bf16[512,16]{1,0:T(8,128)(2,1)S(1)} %get-tuple-element.20.refs_1_, bf16[2096,128]{1,0:T(8,128)(2,1)S(1)} %collective-permute-done.7.refs_4_.refs_2_, bf16[2096,128]{1,0:T(8,128)(2,1)S(1)} %collective-permute-done.5.refs_5_.refs_3_, ...), custom_call_target="tpu_custom_call" | custom-call | flops 500000000 | bytes 2000000 | tf_op jit(solution)/shard_map/score_rest/pallas_call | solution.py:354
  71.4 13.9 %all_to_all.10 = f32[16,8,128]{2,1,0:T(8,128)S(1)} all-to-all(f32[16,8,128]{2,1,0:T(8,128)S(1)} %score_rest.1), channel_id=1, replica_groups=mesh['group'=16,'owner'=32] {'group'}, dimensions={0} | all-to-all | bytes 131072 | tf_op jit(solution)/shard_map/all_to_all | solution.py:363
  85.3 0.5 slice_reduce_fusion
  (14 shorter events, 0.1 us)
Async XLA Ops:
  4.9 13.8 %copy-start = (s32[1,1,49,2]{2,3,1,0:T(2,128)S(1)}, s32[1,1,49,2]{2,3,1,0:T(2,128)}, u32[]{:S(2)}) copy-start(s32[1,1,49,2]{2,3,1,0:T(2,128)} %param.9) | copy-start | bytes 1180
  4.9 35.8 %all-to-all-start = ((bf16[32,104,128]{2,1,0:T(8,128)(2,1)}), bf16[32,104,128]{2,1,0:T(8,128)(2,1)S(1)}, u32[]{:S(2)}, u32[]{:S(2)}) async-start(bf16[32,104,128]{2,1,0:T(8,128)(2,1)} %send_rows.1), calls=%async_computation | async-start | bytes 1703936 | tf_op jit(solution)/shard_map/all_to_all | solution.py:308
  18.7 4.6 %collective-permute-start = (f32[8,128]{1,0:T(8,128)S(1)}, f32[8,128]{1,0:T(8,128)S(1)}, u32[]{:S(2)}, u32[]{:S(2)}) collective-permute-start(f32[8,128]{1,0:T(8,128)S(1)} %concatenate.15), channel_id=1, source_target_pairs={{0,64},{32,96},{64,0},{96,32},{128,192},{160,224},{192,128},{224,1... | collective-permute-start | bytes 12296 | tf_op jit(solution)/shard_map/ppermute | solution.py:312
  23.4 5.5 %collective-permute-start.1 = (f32[8,128]{1,0:T(8,128)S(1)}, f32[8,128]{1,0:T(8,128)S(1)}, u32[]{:S(2)}, u32[]{:S(2)}) collective-permute-start(f32[8,128]{1,0:T(8,128)S(1)} %fusion), channel_id=1, source_target_pairs={{0,128},{32,160},{64,192},{96,224},{128,0},{160,32},{192,64},{224,... | collective-permute-start | bytes 12296 | tf_op jit(solution)/shard_map/ppermute | solution.py:312
  29.0 8.6 %collective-permute-start.2 = (f32[8,128]{1,0:T(8,128)S(1)}, f32[8,128]{1,0:T(8,128)S(1)}, u32[]{:S(2)}, u32[]{:S(2)}) collective-permute-start(f32[8,128]{1,0:T(8,128)S(1)} %pad_maximum_fusion.1.refs_1_), channel_id=1, source_target_pairs={{0,256},{32,288},{64,320},{96,352},{128,384},{160,416},{192,448},{... | collective-permute-start | bytes 12296 | tf_op jit(solution)/shard_map/ppermute | solution.py:312
  42.2 19.0 %collective-permute-start.5 = (bf16[2096,128]{1,0:T(8,128)(2,1)S(1)}, bf16[2096,128]{1,0:T(8,128)(2,1)S(1)}, u32[]{:S(2)}, u32[]{:S(2)}) collective-permute-start(bf16[2096,128]{1,0:T(8,128)(2,1)S(1)} %get-tuple-element.13.refs_0_), channel_id=1, source_target_pairs={{0,31},{1,2},{2,1},{3,4},{4,3},{5,6},{6,5},{7,8},{8,7},{9,10},{10,... | collective-permute-start | bytes 1609736 | tf_op jit(solution)/shard_map/ppermute | solution.py:315
  45.7 15.5 %collective-permute-start.6 = (bf16[2096,128]{1,0:T(8,128)(2,1)S(1)}, bf16[2096,128]{1,0:T(8,128)(2,1)S(1)}, u32[]{:S(2)}, u32[]{:S(2)}) collective-permute-start(bf16[2096,128]{1,0:T(8,128)(2,1)S(1)} %get-tuple-element.13.refs_0_), channel_id=1, source_target_pairs={{0,64},{32,96},{64,128},{96,160},{128,192},{160,224},{192,256},{22... | collective-permute-start | bytes 1609736 | tf_op jit(solution)/shard_map/ppermute | solution.py:312
  48.8 12.5 %collective-permute-start.7 = (bf16[2096,128]{1,0:T(8,128)(2,1)S(1)}, bf16[2096,128]{1,0:T(8,128)(2,1)S(1)}, u32[]{:S(2)}, u32[]{:S(2)}) collective-permute-start(bf16[2096,128]{1,0:T(8,128)(2,1)S(1)} %get-tuple-element.13.refs_0_), channel_id=1, source_target_pairs={{0,1},{1,0},{2,3},{3,2},{4,5},{5,4},{6,7},{7,6},{8,9},{9,8},{10,11... | collective-permute-start | bytes 1609736 | tf_op jit(solution)/shard_map/ppermute | solution.py:315
  52.2 9.1 %collective-permute-start.4 = (bf16[1040,128]{1,0:T(8,128)(2,1)S(1)}, bf16[1040,128]{1,0:T(8,128)(2,1)S(1)}, u32[]{:S(2)}, u32[]{:S(2)}) collective-permute-start(bf16[1040,128]{1,0:T(8,128)(2,1)S(1)} %get-tuple-element.14), channel_id=1, source_target_pairs={{0,448},{32,480},{64,0},{96,32},{128,64},{160,96},{192,128},{224,1... | collective-permute-start | bytes 798728 | tf_op jit(solution)/shard_map/ppermute | solution.py:312
  56.0 11.3 %collective-permute-start.3 = (bf16[2096,128]{1,0:T(8,128)(2,1)S(1)}, bf16[2096,128]{1,0:T(8,128)(2,1)S(1)}, u32[]{:S(2)}, u32[]{:S(2)}) collective-permute-start(bf16[2096,128]{1,0:T(8,128)(2,1)S(1)} %get-tuple-element.13.refs_0_), channel_id=1, source_target_pairs={{0,32},{32,0},{64,96},{96,64},{128,160},{160,128},{192,224},{224,1... | collective-permute-start | bytes 1609736 | tf_op jit(solution)/shard_map/ppermute | solution.py:337
  61.4 8.9 %collective-permute-start.8 = (bf16[3120,128]{1,0:T(8,128)(2,1)S(1)}, bf16[3120,128]{1,0:T(8,128)(2,1)S(1)}, u32[]{:S(2)}, u32[]{:S(2)}) collective-permute-start(bf16[3120,128]{1,0:T(8,128)(2,1)S(1)} %pad_maximum_fusion), channel_id=1, source_target_pairs={{0,32},{32,0},{64,96},{96,64},{128,160},{160,128},{192,224},{224,1... | collective-permute-start | bytes 2396168 | tf_op jit(solution)/shard_map/ppermute | solution.py:341

commit v6 on v5

--- a/solution.py
+++ b/solution.py
@@ -109,6 +109,13 @@
     out_ref[:, : lines * chunks, :] = wide[...].reshape(n_owner, lines * chunks, LANES).astype(BF16)
 
 
+def list_kernel(blocks, pairs_ref, out_ref):
+    first, second = pairs_ref[0:1, :], pairs_ref[1:2, :]
+    rows, wide = iota((blocks, LANES), 0), iota((LANES, LANES), 0)
+    table = mm_nt(ones_where(rows == first), ones_where(wide == second))
+    out_ref[...] = table + mm_nt(ones_where(rows == second - blocks), ones_where(wide == first + blocks))
+
+
 def receive_kernel(n_owner, cap, feat, in_ref, here_ref, there_ref, both_ref, first_ref, wide):
     chunks = feat // LANES
     per_peer = UNITS * cap
@@ -153,8 +160,7 @@
         both_ref[pl.ds(n * size + feat, PAY_META), :] = numbers
         if n == 0:
             first_ref[pl.ds(feat, PAY_META), :] = numbers
-    lists = jnp.concatenate([here_ref[...], there_ref[...]], axis=0)
-    both_ref[pl.ds(UNITS * size, PAY_META), :] = lists.astype(BF16)
+    both_ref[pl.ds(UNITS * size, PAY_META), :] = (here_ref[...] + there_ref[...]).astype(BF16)
 
 
 def rows_of(ref, start, feat):
@@ -184,8 +190,8 @@
 
 
 def bias_of(penalty, marks):
-    picked = ones_where(iota((penalty.shape[0], marks.shape[1]), 0) == marks)
-    return mm_tn(picked, penalty).astype(BF16)
+    picked = ones_where(iota((LANES, marks.shape[1]), 0) == marks)
+    return lax.dot_general(picked, penalty, (((0,), (1,)), ((), ())), preferred_element_type=F32).astype(BF16)
 
 
 def slot_table(best, numbers, blocks):
@@ -205,18 +211,7 @@
 
 def first_score_kernel(blocks, feat, own_ref, twin_ref, back_ref, next_ref, left_ref, right_ref, out_ref, bias_ref):
     size = feat + PAY_META
-    lists = [r[pl.ds(UNITS * size, PAY_META), :].astype(F32) for r in (own_ref, twin_ref)]
-    count = PAY_META // 2
-
-    def list_row(i):
-        return jnp.concatenate([n[2 * b + i : 2 * b + i + 1, :] for n in lists for b in range(count)], axis=1).astype(I32)
-
-    first, second = list_row(0), list_row(1)
-    total = 2 * count * LANES
-    first_rows = iota((blocks, total), 0)
-    wide_rows = iota((3 * blocks, total), 0)
-    paired = mm_nt(ones_where(wide_rows == second), ones_where(first_rows == first))
-    paired += mm_nt(ones_where(wide_rows == first + blocks), ones_where(first_rows == second - blocks))
+    paired = own_ref[pl.ds(UNITS * size, PAY_META), :].astype(F32) + twin_ref[pl.ds(UNITS * size, PAY_META), :].astype(F32)
     penalty = jnp.where(paired > 0.5, 0.0, -4.0).astype(BF16)
     across = [(left_ref, 0), (right_ref, 0), (left_ref, size), (right_ref, size)]
     marks = stack_numbers(across, feat)[0:1, :]
@@ -315,12 +310,19 @@
         return lax.ppermute(x, "owner", [(i, partner(i) % n_owner) for i in range(n_owner)])
 
     entries = pairs.reshape(-1, 2)
-    here = jnp.pad(entries.T, ((0, 0), (0, LANES - entries.shape[0])), constant_values=-1).astype(F32)
-    blank = jnp.full((6, LANES), -1.0, F32)
-    there = along_y(jnp.concatenate([here, blank], axis=0), lambda y: y ^ 1)
-    here = jnp.concatenate([here, there[:2]], axis=0)
-    there = along_y(jnp.concatenate([here, blank[:4]], axis=0), lambda y: y ^ 2)
-    here = jnp.concatenate([here, there[:4]], axis=0)
+    listed = jnp.pad(entries.T, ((0, 0), (0, LANES - entries.shape[0])), constant_values=-1)
+    here = pl.pallas_call(
+        lambda *refs: list_kernel(n_group, *refs),
+        out_shape=jax.ShapeDtypeStruct((n_group, LANES), F32),
+        in_specs=[vmem()],
+        out_specs=vmem(),
+        compiler_params=PARAMS,
+        name="list_table",
+    )(listed)
+    there = along_y(here, lambda y: y ^ 1)
+    here = here + there
+    there = along_y(here, lambda y: y ^ 2)
+    here = here + there
     there = along_y(here, lambda y: y ^ 4)
     both, first = pl.pallas_call(
         lambda *refs: receive_kernel(n_owner, cap, feat, *refs),

time: 86.4 us -> 86.1 us (level)
  no operation moved by 1% of the time
where the time goes in v6:
time: 86.1 us; the launch traced here: 85.7 us
  starting transfers between devices  53.6 us (62%)
  blocking collectives  13.9 us (16%)
  Pallas kernels  10.2 us (12%)
  waiting for transfers between devices  7.07 us (8%)
    ppermute x5, starting transfers between devices, along_y(): lax.ppermute(x, 'group', [(i, 2 * (partner(i // 2) % (n_group // 2)) + i...  21.7 us
    all_to_all x1, blocking collectives, on_device(): lax.all_to_all(table, 'group', split_axis=0, concat_axis=0, tiled=True)  13.9 us
    all_to_all x1, starting transfers between devices, on_device(): lax.all_to_all(outgoing, 'owner', split_axis=0, concat_axis=0, tiled=True)  13.7 us
    ppermute x2, starting transfers between devices, along_owner(): lax.ppermute(x, 'owner', [(i, partner(i) % n_owner) for i in range(n_owne...  6.89 us
    ppermute x1, starting transfers between devices, on_device(): lax.ppermute(jnp.concatenate([back[:2 * size], following], axis=0), 'grou...  6.04 us
    ppermute x1, starting transfers between devices, on_device(): twin = lax.ppermute(both, 'group', swap)  5.25 us
    pallas_call x1, Pallas kernels, on_device(): pl.pallas_call(lambda *refs: send_kernel(n_owner, n_group, cap, 6, pieces...  4.9 us
    ppermute x5, waiting for transfers between devices, along_y(): lax.ppermute(x, 'group', [(i, 2 * (partner(i // 2) % (n_group // 2)) + i...  3.86 us
  transfers between devices with their start and end apart: 10, of which 4 were waited for; matrix products, arithmetic and copies ran while one was open for 0% of the time, Pallas kernels for 3%

profile of v6, /device:TPU:1, one launch (start us, length us, event | category | flops | bytes accessed | tf_op | source)
XLA Modules:
  0.0 85.7 jit_solution(2801479009981073279)
XLA Ops:
  0.0 4.9 %send_rows.1 = bf16[32,104,128]{2,1,0:T(8,128)(2,1)} custom-call(s32[1,2048]{1,0:T(1,128)} %bitcast.7, s32[1,32]{1,0:T(1,128)} %bitcast.10, s32[1,2048]{1,0:T(1,128)} %bitcast.8, bf16[2048,1024]{1,0:T(8,128)(2,1)} %refs_3_.1), custom_call_target="tpu_custom_call" | custom-call | tf_op jit(solution)/shard_map/send_rows/pallas_call | solution.py:282
  4.9 0.0 copy-start
  4.9 13.7 %all-to-all-start = ((bf16[32,104,128]{2,1,0:T(8,128)(2,1)}), bf16[32,104,128]{2,1,0:T(8,128)(2,1)S(1)}, u32[]{:S(2)}, u32[]{:S(2)}) async-start(bf16[32,104,128]{2,1,0:T(8,128)(2,1)} %send_rows.1), calls=%async_computation | async-start | bytes 1703936 | tf_op jit(solution)/shard_map/all_to_all | solution.py:303
  18.7 0.1 list_table.1
  18.8 3.2 %collective-permute-start = (f32[16,128]{1,0:T(8,128)S(1)}, f32[16,128]{1,0:T(8,128)S(1)}, u32[]{:S(2)}, u32[]{:S(2)}) collective-permute-start(f32[16,128]{1,0:T(8,128)S(1)} %list_table.1), channel_id=1, source_target_pairs={{0,64},{32,96},{64,0},{96,32},{128,192},{160,224},{192,128},{224,1... | collective-permute-start | bytes 24584 | tf_op jit(solution)/shard_map/ppermute | solution.py:307
  22.0 1.5 %collective-permute-done = f32[16,128]{1,0:T(8,128)S(1)} collective-permute-done((f32[16,128]{1,0:T(8,128)S(1)}, f32[16,128]{1,0:T(8,128)S(1)}, u32[]{:S(2)}, u32[]{:S(2)}) %collective-permute-start) | collective-permute-done | bytes 8224 | tf_op jit(solution)/shard_map/ppermute | solution.py:307
  23.5 4.2 %collective-permute-start.1 = (f32[16,128]{1,0:T(8,128)S(1)}, f32[16,128]{1,0:T(8,128)S(1)}, u32[]{:S(2)}, u32[]{:S(2)}) collective-permute-start(f32[16,128]{1,0:T(8,128)S(1)} %add.8), channel_id=1, source_target_pairs={{0,128},{32,160},{64,192},{96,224},{128,0},{160,32},{192,64},{224,... | collective-permute-start | bytes 24584 | tf_op jit(solution)/shard_map/ppermute | solution.py:307
  27.7 1.4 %collective-permute-done.1 = f32[16,128]{1,0:T(8,128)S(1)} collective-permute-done((f32[16,128]{1,0:T(8,128)S(1)}, f32[16,128]{1,0:T(8,128)S(1)}, u32[]{:S(2)}, u32[]{:S(2)}) %collective-permute-start.1) | collective-permute-done | bytes 8224 | tf_op jit(solution)/shard_map/ppermute | solution.py:307
  29.1 7.4 %collective-permute-start.2 = (f32[16,128]{1,0:T(8,128)S(1)}, f32[16,128]{1,0:T(8,128)S(1)}, u32[]{:S(2)}, u32[]{:S(2)}) collective-permute-start(f32[16,128]{1,0:T(8,128)S(1)} %add.9.refs_1_), channel_id=1, source_target_pairs={{0,256},{32,288},{64,320},{96,352},{128,384},{160,416},{192,448},{... | collective-permute-start | bytes 24584 | tf_op jit(solution)/shard_map/ppermute | solution.py:307
  36.5 1.0 %collective-permute-done.2.refs_2_ = f32[16,128]{1,0:T(8,128)S(1)} collective-permute-done((f32[16,128]{1,0:T(8,128)S(1)}, f32[16,128]{1,0:T(8,128)S(1)}, u32[]{:S(2)}, u32[]{:S(2)}) %collective-permute-start.2) | collective-permute-done | bytes 8224 | tf_op jit(solution)/shard_map/ppermute | solution.py:307
  37.6 3.2 %all-to-all-done.refs_0_ = bf16[32,104,128]{2,1,0:T(8,128)(2,1)S(1)} async-done(((bf16[32,104,128]{2,1,0:T(8,128)(2,1)}), bf16[32,104,128]{2,1,0:T(8,128)(2,1)S(1)}, u32[]{:S(2)}, u32[]{:S(2)}) %all-to-all-start) | async-done | bytes 852000 | tf_op jit(solution)/shard_map/all_to_all | solution.py:303
  40.8 1.5 %unit_rows.1 = (bf16[2096,128]{1,0:T(8,128)(2,1)S(1)}, bf16[1040,128]{1,0:T(8,128)(2,1)S(1)}) custom-call(bf16[32,104,128]{2,1,0:T(8,128)(2,1)S(1)} %all-to-all-done.refs_0_, f32[16,128]{1,0:T(8,128)S(1)} %add.9.refs_1_, f32[16,128]{1,0:T(8,128)S(1)} %collective-permute-done.2.refs_2_), custom_call_target="tpu_custom_call" | custom-call | tf_op jit(solution)/shard_map/unit_rows/pallas_call | solution.py:327
  42.2 3.7 %collective-permute-start.5 = (bf16[2096,128]{1,0:T(8,128)(2,1)S(1)}, bf16[2096,128]{1,0:T(8,128)(2,1)S(1)}, u32[]{:S(2)}, u32[]{:S(2)}) collective-permute-start(bf16[2096,128]{1,0:T(8,128)(2,1)S(1)} %get-tuple-element.13.refs_0_), channel_id=1, source_target_pairs={{0,31},{1,2},{2,1},{3,4},{4,3},{5,6},{6,5},{7,8},{8,7},{9,10},{10,... | collective-permute-start | bytes 1609736 | tf_op jit(solution)/shard_map/ppermute | solution.py:310
  45.9 3.0 %collective-permute-start.6 = (bf16[2096,128]{1,0:T(8,128)(2,1)S(1)}, bf16[2096,128]{1,0:T(8,128)(2,1)S(1)}, u32[]{:S(2)}, u32[]{:S(2)}) collective-permute-start(bf16[2096,128]{1,0:T(8,128)(2,1)S(1)} %get-tuple-element.13.refs_0_), channel_id=1, source_target_pairs={{0,64},{32,96},{64,128},{96,160},{128,192},{160,224},{192,256},{22... | collective-permute-start | bytes 1609736 | tf_op jit(solution)/shard_map/ppermute | solution.py:307
  48.9 3.2 %collective-permute-start.7 = (bf16[2096,128]{1,0:T(8,128)(2,1)S(1)}, bf16[2096,128]{1,0:T(8,128)(2,1)S(1)}, u32[]{:S(2)}, u32[]{:S(2)}) collective-permute-start(bf16[2096,128]{1,0:T(8,128)(2,1)S(1)} %get-tuple-element.13.refs_0_), channel_id=1, source_target_pairs={{0,1},{1,0},{2,3},{3,2},{4,5},{5,4},{6,7},{7,6},{8,9},{9,8},{10,11... | collective-permute-start | bytes 1609736 | tf_op jit(solution)/shard_map/ppermute | solution.py:310
  52.2 3.8 %collective-permute-start.4 = (bf16[1040,128]{1,0:T(8,128)(2,1)S(1)}, bf16[1040,128]{1,0:T(8,128)(2,1)S(1)}, u32[]{:S(2)}, u32[]{:S(2)}) collective-permute-start(bf16[1040,128]{1,0:T(8,128)(2,1)S(1)} %get-tuple-element.14), channel_id=1, source_target_pairs={{0,448},{32,480},{64,0},{96,32},{128,64},{160,96},{192,128},{224,1... | collective-permute-start | bytes 798728 | tf_op jit(solution)/shard_map/ppermute | solution.py:307
  56.0 5.2 %collective-permute-start.3 = (bf16[2096,128]{1,0:T(8,128)(2,1)S(1)}, bf16[2096,128]{1,0:T(8,128)(2,1)S(1)}, u32[]{:S(2)}, u32[]{:S(2)}) collective-permute-start(bf16[2096,128]{1,0:T(8,128)(2,1)S(1)} %get-tuple-element.13.refs_0_), channel_id=1, source_target_pairs={{0,32},{32,0},{64,96},{96,64},{128,160},{160,128},{192,224},{224,1... | collective-permute-start | bytes 1609736 | tf_op jit(solution)/shard_map/ppermute | solution.py:339
  61.3 0.0 collective-permute-done.5.refs_5_.refs_3_
  61.3 0.1 pad_maximum_fusion
  61.4 6.0 %collective-permute-start.8 = (bf16[3120,128]{1,0:T(8,128)(2,1)S(1)}, bf16[3120,128]{1,0:T(8,128)(2,1)S(1)}, u32[]{:S(2)}, u32[]{:S(2)}) collective-permute-start(bf16[3120,128]{1,0:T(8,128)(2,1)S(1)} %pad_maximum_fusion), channel_id=1, source_target_pairs={{0,32},{32,0},{64,96},{96,64},{128,160},{160,128},{192,224},{224,1... | collective-permute-start | bytes 2396168 | tf_op jit(solution)/shard_map/ppermute | solution.py:343
  67.5 2.7 %score_rows.1 = (f32[16,128]{1,0:T(8,128)S(1)}, bf16[512,16]{1,0:T(8,128)(2,1)S(1)}) custom-call(bf16[2096,128]{1,0:T(8,128)(2,1)S(1)} %get-tuple-element.13.refs_0_, bf16[2096,128]{1,0:T(8,128)(2,1)S(1)} %collective-permute-done.3.refs_1_, bf16[2096,128]{1,0:T(8,128)(2,1)S(1)} %collective-permute-done.6.refs_2_.refs_4_, ...), custom_call_target="tpu_custom_call" | custom-call | flops 3000000000 | bytes 4000000 | tf_op jit(solution)/shard_map/score_rows/pallas_call | solution.py:344
  70.1 1.0 %score_rest.1 = f32[16,8,128]{2,1,0:T(8,128)S(1)} custom-call(f32[16,128]{1,0:T(8,128)S(1)} %get-tuple-element.19.refs_0_, bf16[512,16]{1,0:T(8,128)(2,1)S(1)} %get-tuple-element.20.refs_1_, bf16[2096,128]{1,0:T(8,128)(2,1)S(1)} %collective-permute-done.7.refs_4_.refs_2_, bf16[2096,128]{1,0:T(8,128)(2,1)S(1)} %collective-permute-done.5.refs_5_.refs_3_, ...), custom_call_target="tpu_custom_call" | custom-call | flops 500000000 | bytes 2000000 | tf_op jit(solution)/shard_map/score_rest/pallas_call | solution.py:356
  71.2 13.9 %all_to_all.10 = f32[16,8,128]{2,1,0:T(8,128)S(1)} all-to-all(f32[16,8,128]{2,1,0:T(8,128)S(1)} %score_rest.1), channel_id=1, replica_groups=mesh['group'=16,'owner'=32] {'group'}, dimensions={0} | all-to-all | bytes 131072 | tf_op jit(solution)/shard_map/all_to_all | solution.py:365
  85.1 0.5 slice_reduce_fusion
  (10 shorter events, 0.1 us)
Async XLA Ops:
  4.9 13.8 %copy-start = (s32[1,1,49,2]{2,3,1,0:T(2,128)S(1)}, s32[1,1,49,2]{2,3,1,0:T(2,128)}, u32[]{:S(2)}) copy-start(s32[1,1,49,2]{2,3,1,0:T(2,128)} %param.9) | copy-start | bytes 1180
  4.9 35.8 %all-to-all-start = ((bf16[32,104,128]{2,1,0:T(8,128)(2,1)}), bf16[32,104,128]{2,1,0:T(8,128)(2,1)S(1)}, u32[]{:S(2)}, u32[]{:S(2)}) async-start(bf16[32,104,128]{2,1,0:T(8,128)(2,1)} %send_rows.1), calls=%async_computation | async-start | bytes 1703936 | tf_op jit(solution)/shard_map/all_to_all | solution.py:303
  18.8 4.7 %collective-permute-start = (f32[16,128]{1,0:T(8,128)S(1)}, f32[16,128]{1,0:T(8,128)S(1)}, u32[]{:S(2)}, u32[]{:S(2)}) collective-permute-start(f32[16,128]{1,0:T(8,128)S(1)} %list_table.1), channel_id=1, source_target_pairs={{0,64},{32,96},{64,0},{96,32},{128,192},{160,224},{192,128},{224,1... | collective-permute-start | bytes 24584 | tf_op jit(solution)/shard_map/ppermute | solution.py:307
  23.5 5.6 %collective-permute-start.1 = (f32[16,128]{1,0:T(8,128)S(1)}, f32[16,128]{1,0:T(8,128)S(1)}, u32[]{:S(2)}, u32[]{:S(2)}) collective-permute-start(f32[16,128]{1,0:T(8,128)S(1)} %add.8), channel_id=1, source_target_pairs={{0,128},{32,160},{64,192},{96,224},{128,0},{160,32},{192,64},{224,... | collective-permute-start | bytes 24584 | tf_op jit(solution)/shard_map/ppermute | solution.py:307
  29.1 8.5 %collective-permute-start.2 = (f32[16,128]{1,0:T(8,128)S(1)}, f32[16,128]{1,0:T(8,128)S(1)}, u32[]{:S(2)}, u32[]{:S(2)}) collective-permute-start(f32[16,128]{1,0:T(8,128)S(1)} %add.9.refs_1_), channel_id=1, source_target_pairs={{0,256},{32,288},{64,320},{96,352},{128,384},{160,416},{192,448},{... | collective-permute-start | bytes 24584 | tf_op jit(solution)/shard_map/ppermute | solution.py:307
  42.2 19.0 %collective-permute-start.5 = (bf16[2096,128]{1,0:T(8,128)(2,1)S(1)}, bf16[2096,128]{1,0:T(8,128)(2,1)S(1)}, u32[]{:S(2)}, u32[]{:S(2)}) collective-permute-start(bf16[2096,128]{1,0:T(8,128)(2,1)S(1)} %get-tuple-element.13.refs_0_), channel_id=1, source_target_pairs={{0,31},{1,2},{2,1},{3,4},{4,3},{5,6},{6,5},{7,8},{8,7},{9,10},{10,... | collective-permute-start | bytes 1609736 | tf_op jit(solution)/shard_map/ppermute | solution.py:310
  45.9 15.4 %collective-permute-start.6 = (bf16[2096,128]{1,0:T(8,128)(2,1)S(1)}, bf16[2096,128]{1,0:T(8,128)(2,1)S(1)}, u32[]{:S(2)}, u32[]{:S(2)}) collective-permute-start(bf16[2096,128]{1,0:T(8,128)(2,1)S(1)} %get-tuple-element.13.refs_0_), channel_id=1, source_target_pairs={{0,64},{32,96},{64,128},{96,160},{128,192},{160,224},{192,256},{22... | collective-permute-start | bytes 1609736 | tf_op jit(solution)/shard_map/ppermute | solution.py:307
  48.9 12.3 %collective-permute-start.7 = (bf16[2096,128]{1,0:T(8,128)(2,1)S(1)}, bf16[2096,128]{1,0:T(8,128)(2,1)S(1)}, u32[]{:S(2)}, u32[]{:S(2)}) collective-permute-start(bf16[2096,128]{1,0:T(8,128)(2,1)S(1)} %get-tuple-element.13.refs_0_), channel_id=1, source_target_pairs={{0,1},{1,0},{2,3},{3,2},{4,5},{5,4},{6,7},{7,6},{8,9},{9,8},{10,11... | collective-permute-start | bytes 1609736 | tf_op jit(solution)/shard_map/ppermute | solution.py:310
  52.2 9.1 %collective-permute-start.4 = (bf16[1040,128]{1,0:T(8,128)(2,1)S(1)}, bf16[1040,128]{1,0:T(8,128)(2,1)S(1)}, u32[]{:S(2)}, u32[]{:S(2)}) collective-permute-start(bf16[1040,128]{1,0:T(8,128)(2,1)S(1)} %get-tuple-element.14), channel_id=1, source_target_pairs={{0,448},{32,480},{64,0},{96,32},{128,64},{160,96},{192,128},{224,1... | collective-permute-start | bytes 798728 | tf_op jit(solution)/shard_map/ppermute | solution.py:307
  56.0 11.5 %collective-permute-start.3 = (bf16[2096,128]{1,0:T(8,128)(2,1)S(1)}, bf16[2096,128]{1,0:T(8,128)(2,1)S(1)}, u32[]{:S(2)}, u32[]{:S(2)}) collective-permute-start(bf16[2096,128]{1,0:T(8,128)(2,1)S(1)} %get-tuple-element.13.refs_0_), channel_id=1, source_target_pairs={{0,32},{32,0},{64,96},{96,64},{128,160},{160,128},{192,224},{224,1... | collective-permute-start | bytes 1609736 | tf_op jit(solution)/shard_map/ppermute | solution.py:339
  61.4 8.7 %collective-permute-start.8 = (bf16[3120,128]{1,0:T(8,128)(2,1)S(1)}, bf16[3120,128]{1,0:T(8,128)(2,1)S(1)}, u32[]{:S(2)}, u32[]{:S(2)}) collective-permute-start(bf16[3120,128]{1,0:T(8,128)(2,1)S(1)} %pad_maximum_fusion), channel_id=1, source_target_pairs={{0,32},{32,0},{64,96},{96,64},{128,160},{160,128},{192,224},{224,1... | collective-permute-start | bytes 2396168 | tf_op jit(solution)/shard_map/ppermute | solution.py:343

commit v7 on v6

--- a/solution.py
+++ b/solution.py
@@ -93,7 +93,10 @@
     column = iota((2 * width, LANES), 0) & (width - 1)
     meta = mm(meta, ones_where(column == iota((2 * width, LANES), 1)))
     out_ref[:, lines * chunks :, :] = meta.reshape(n_owner, META, LANES).astype(BF16)
-    select = ones_where(iota((n_owner * lines, rows), 0) == goal)
+    middle = n_owner * lines // 2
+    line = (iota((n_owner * lines, 1), 0) - middle).astype(F32).astype(BF16)
+    goal = jnp.where(mine, goal - middle, middle).astype(F32).astype(BF16)
+    select = jnp.where(line == goal, jnp.ones((), BF16), jnp.zeros((), BF16))
     total = None
     for i, copy in enumerate(copies[:-1]):
         copy.wait()
@@ -220,14 +223,15 @@
     across_bias = bias_of(penalty, marks)
     bias_ref[...] = across_bias
     across_rows = stack_rows(across, feat)
-    inside = [(next_ref, 0), (back_ref, 0), (own_ref, 0), (twin_ref, 0), (own_ref, size), (twin_ref, size)]
+    inside = [(twin_ref, size), (next_ref, 0), (back_ref, size), (own_ref, 0), (own_ref, size), (twin_ref, size)]
     inside_bias = bias_of(penalty, stack_numbers(inside, feat)[0:1, :] + blocks)
     inside_rows = stack_rows(inside, feat)
-    row, lane = iota((5 * BLOCK, 2 * BLOCK), 0), iota((5 * BLOCK, 2 * BLOCK), 1)
+    row, lane = iota((4 * BLOCK, 2 * BLOCK), 0), iota((4 * BLOCK, 2 * BLOCK), 1)
+    same = jnp.logical_and(row - 3 * BLOCK == lane, lane < BLOCK)
     groups = [
-        ([(own_ref, 0), (twin_ref, 0)], 4, 1, 6, row == lane + BLOCK),
-        ([(own_ref, size), (twin_ref, size)], 2, 0, 3, None),
-        ([(back_ref, 0), (next_ref, 0)], 4, 2, 6, None),
+        ([(own_ref, 0), (twin_ref, 0)], 4, 0, 2, None),
+        ([(own_ref, size), (twin_ref, size)], 2, 1, 5, same),
+        ([(back_ref, 0), (next_ref, 0)], 4, 4, 6, None),
     ]
     best, numbers = [], []
     for places, count, low, high, equal in groups:
@@ -277,7 +281,7 @@
     chunks = feat // LANES
     cap = 3 * rows // (2 * n_owner * n_group)
     lines = UNITS * cap
-    pieces = 4
+    pieces = 2
     size = feat + PAY_META
     outgoing = pl.pallas_call(
         lambda *refs: send_kernel(n_owner, n_group, cap, 6, pieces, *refs),

time: 86.1 us -> 85.5 us (level)
  no operation moved by 1% of the time
where the time goes in v7:
time: 85.5 us; the launch traced here: 85 us
  starting transfers between devices  53.6 us (63%)
  blocking collectives  14 us (16%)
  Pallas kernels  9.59 us (11%)
  waiting for transfers between devices  7.07 us (8%)
    ppermute x5, starting transfers between devices, along_y(): lax.ppermute(x, 'group', [(i, 2 * (partner(i // 2) % (n_group // 2)) + i...  21.7 us
    all_to_all x1, blocking collectives, on_device(): lax.all_to_all(table, 'group', split_axis=0, concat_axis=0, tiled=True)  14 us
    all_to_all x1, starting transfers between devices, on_device(): lax.all_to_all(outgoing, 'owner', split_axis=0, concat_axis=0, tiled=True)  13.7 us
    ppermute x2, starting transfers between devices, along_owner(): lax.ppermute(x, 'owner', [(i, partner(i) % n_owner) for i in range(n_owne...  6.91 us
    ppermute x1, starting transfers between devices, on_device(): lax.ppermute(jnp.concatenate([back[:2 * size], following], axis=0), 'grou...  6.04 us
    ppermute x1, starting transfers between devices, on_device(): twin = lax.ppermute(both, 'group', swap)  5.25 us
    pallas_call x1, Pallas kernels, on_device(): pl.pallas_call(lambda *refs: send_kernel(n_owner, n_group, cap, 6, pieces...  4.64 us
    ppermute x5, waiting for transfers between devices, along_y(): lax.ppermute(x, 'group', [(i, 2 * (partner(i // 2) % (n_group // 2)) + i...  3.88 us
  transfers between devices with their start and end apart: 10, of which 4 were waited for; matrix products, arithmetic and copies ran while one was open for 0% of the time, Pallas kernels for 3%

profile of v7, /device:TPU:1, one launch (start us, length us, event | category | flops | bytes accessed | tf_op | source)
XLA Modules:
  0.0 85.0 jit_solution(5727906095553162398)
XLA Ops:
  0.0 4.6 %send_rows.1 = bf16[32,104,128]{2,1,0:T(8,128)(2,1)} custom-call(s32[1,2048]{1,0:T(1,128)} %bitcast.7, s32[1,32]{1,0:T(1,128)} %bitcast.10, s32[1,2048]{1,0:T(1,128)} %bitcast.8, bf16[2048,1024]{1,0:T(8,128)(2,1)} %refs_3_.1), custom_call_target="tpu_custom_call" | custom-call | tf_op jit(solution)/shard_map/send_rows/pallas_call | solution.py:286
  4.6 0.0 copy-start
  4.7 13.7 %all-to-all-start = ((bf16[32,104,128]{2,1,0:T(8,128)(2,1)}), bf16[32,104,128]{2,1,0:T(8,128)(2,1)S(1)}, u32[]{:S(2)}, u32[]{:S(2)}) async-start(bf16[32,104,128]{2,1,0:T(8,128)(2,1)} %send_rows.1), calls=%async_computation | async-start | bytes 1703936 | tf_op jit(solution)/shard_map/all_to_all | solution.py:307
  18.4 0.1 list_table.1
  18.6 3.2 %collective-permute-start = (f32[16,128]{1,0:T(8,128)S(1)}, f32[16,128]{1,0:T(8,128)S(1)}, u32[]{:S(2)}, u32[]{:S(2)}) collective-permute-start(f32[16,128]{1,0:T(8,128)S(1)} %list_table.1), channel_id=1, source_target_pairs={{0,64},{32,96},{64,0},{96,32},{128,192},{160,224},{192,128},{224,1... | collective-permute-start | bytes 24584 | tf_op jit(solution)/shard_map/ppermute | solution.py:311
  21.8 1.5 %collective-permute-done = f32[16,128]{1,0:T(8,128)S(1)} collective-permute-done((f32[16,128]{1,0:T(8,128)S(1)}, f32[16,128]{1,0:T(8,128)S(1)}, u32[]{:S(2)}, u32[]{:S(2)}) %collective-permute-start) | collective-permute-done | bytes 8224 | tf_op jit(solution)/shard_map/ppermute | solution.py:311
  23.3 4.2 %collective-permute-start.1 = (f32[16,128]{1,0:T(8,128)S(1)}, f32[16,128]{1,0:T(8,128)S(1)}, u32[]{:S(2)}, u32[]{:S(2)}) collective-permute-start(f32[16,128]{1,0:T(8,128)S(1)} %add.8), channel_id=1, source_target_pairs={{0,128},{32,160},{64,192},{96,224},{128,0},{160,32},{192,64},{224,... | collective-permute-start | bytes 24584 | tf_op jit(solution)/shard_map/ppermute | solution.py:311
  27.5 1.4 %collective-permute-done.1 = f32[16,128]{1,0:T(8,128)S(1)} collective-permute-done((f32[16,128]{1,0:T(8,128)S(1)}, f32[16,128]{1,0:T(8,128)S(1)}, u32[]{:S(2)}, u32[]{:S(2)}) %collective-permute-start.1) | collective-permute-done | bytes 8224 | tf_op jit(solution)/shard_map/ppermute | solution.py:311
  28.8 7.4 %collective-permute-start.2 = (f32[16,128]{1,0:T(8,128)S(1)}, f32[16,128]{1,0:T(8,128)S(1)}, u32[]{:S(2)}, u32[]{:S(2)}) collective-permute-start(f32[16,128]{1,0:T(8,128)S(1)} %add.9.refs_1_), channel_id=1, source_target_pairs={{0,256},{32,288},{64,320},{96,352},{128,384},{160,416},{192,448},{... | collective-permute-start | bytes 24584 | tf_op jit(solution)/shard_map/ppermute | solution.py:311
  36.3 1.0 %collective-permute-done.2.refs_2_ = f32[16,128]{1,0:T(8,128)S(1)} collective-permute-done((f32[16,128]{1,0:T(8,128)S(1)}, f32[16,128]{1,0:T(8,128)S(1)}, u32[]{:S(2)}, u32[]{:S(2)}) %collective-permute-start.2) | collective-permute-done | bytes 8224 | tf_op jit(solution)/shard_map/ppermute | solution.py:311
  37.3 3.2 %all-to-all-done.refs_0_ = bf16[32,104,128]{2,1,0:T(8,128)(2,1)S(1)} async-done(((bf16[32,104,128]{2,1,0:T(8,128)(2,1)}), bf16[32,104,128]{2,1,0:T(8,128)(2,1)S(1)}, u32[]{:S(2)}, u32[]{:S(2)}) %all-to-all-start) | async-done | bytes 852000 | tf_op jit(solution)/shard_map/all_to_all | solution.py:307
  40.5 1.5 %unit_rows.1 = (bf16[2096,128]{1,0:T(8,128)(2,1)S(1)}, bf16[1040,128]{1,0:T(8,128)(2,1)S(1)}) custom-call(bf16[32,104,128]{2,1,0:T(8,128)(2,1)S(1)} %all-to-all-done.refs_0_, f32[16,128]{1,0:T(8,128)S(1)} %add.9.refs_1_, f32[16,128]{1,0:T(8,128)S(1)} %collective-permute-done.2.refs_2_), custom_call_target="tpu_custom_call" | custom-call | tf_op jit(solution)/shard_map/unit_rows/pallas_call | solution.py:331
  41.9 3.7 %collective-permute-start.5 = (bf16[2096,128]{1,0:T(8,128)(2,1)S(1)}, bf16[2096,128]{1,0:T(8,128)(2,1)S(1)}, u32[]{:S(2)}, u32[]{:S(2)}) collective-permute-start(bf16[2096,128]{1,0:T(8,128)(2,1)S(1)} %get-tuple-element.13.refs_0_), channel_id=1, source_target_pairs={{0,31},{1,2},{2,1},{3,4},{4,3},{5,6},{6,5},{7,8},{8,7},{9,10},{10,... | collective-permute-start | bytes 1609736 | tf_op jit(solution)/shard_map/ppermute | solution.py:314
  45.6 3.0 %collective-permute-start.6 = (bf16[2096,128]{1,0:T(8,128)(2,1)S(1)}, bf16[2096,128]{1,0:T(8,128)(2,1)S(1)}, u32[]{:S(2)}, u32[]{:S(2)}) collective-permute-start(bf16[2096,128]{1,0:T(8,128)(2,1)S(1)} %get-tuple-element.13.refs_0_), channel_id=1, source_target_pairs={{0,64},{32,96},{64,128},{96,160},{128,192},{160,224},{192,256},{22... | collective-permute-start | bytes 1609736 | tf_op jit(solution)/shard_map/ppermute | solution.py:311
  48.7 3.2 %collective-permute-start.7 = (bf16[2096,128]{1,0:T(8,128)(2,1)S(1)}, bf16[2096,128]{1,0:T(8,128)(2,1)S(1)}, u32[]{:S(2)}, u32[]{:S(2)}) collective-permute-start(bf16[2096,128]{1,0:T(8,128)(2,1)S(1)} %get-tuple-element.13.refs_0_), channel_id=1, source_target_pairs={{0,1},{1,0},{2,3},{3,2},{4,5},{5,4},{6,7},{7,6},{8,9},{9,8},{10,11... | collective-permute-start | bytes 1609736 | tf_op jit(solution)/shard_map/ppermute | solution.py:314
  51.9 3.8 %collective-permute-start.4 = (bf16[1040,128]{1,0:T(8,128)(2,1)S(1)}, bf16[1040,128]{1,0:T(8,128)(2,1)S(1)}, u32[]{:S(2)}, u32[]{:S(2)}) collective-permute-start(bf16[1040,128]{1,0:T(8,128)(2,1)S(1)} %get-tuple-element.14), channel_id=1, source_target_pairs={{0,448},{32,480},{64,0},{96,32},{128,64},{160,96},{192,128},{224,1... | collective-permute-start | bytes 798728 | tf_op jit(solution)/shard_map/ppermute | solution.py:311
  55.7 5.2 %collective-permute-start.3 = (bf16[2096,128]{1,0:T(8,128)(2,1)S(1)}, bf16[2096,128]{1,0:T(8,128)(2,1)S(1)}, u32[]{:S(2)}, u32[]{:S(2)}) collective-permute-start(bf16[2096,128]{1,0:T(8,128)(2,1)S(1)} %get-tuple-element.13.refs_0_), channel_id=1, source_target_pairs={{0,32},{32,0},{64,96},{96,64},{128,160},{160,128},{192,224},{224,1... | collective-permute-start | bytes 1609736 | tf_op jit(solution)/shard_map/ppermute | solution.py:343
  61.0 0.0 collective-permute-done.5.refs_5_.refs_3_
  61.1 0.1 pad_maximum_fusion
  61.1 6.0 %collective-permute-start.8 = (bf16[3120,128]{1,0:T(8,128)(2,1)S(1)}, bf16[3120,128]{1,0:T(8,128)(2,1)S(1)}, u32[]{:S(2)}, u32[]{:S(2)}) collective-permute-start(bf16[3120,128]{1,0:T(8,128)(2,1)S(1)} %pad_maximum_fusion), channel_id=1, source_target_pairs={{0,32},{32,0},{64,96},{96,64},{128,160},{160,128},{192,224},{224,1... | collective-permute-start | bytes 2396168 | tf_op jit(solution)/shard_map/ppermute | solution.py:347
  67.2 2.3 %score_rows.1 = (f32[16,128]{1,0:T(8,128)S(1)}, bf16[512,16]{1,0:T(8,128)(2,1)S(1)}) custom-call(bf16[2096,128]{1,0:T(8,128)(2,1)S(1)} %get-tuple-element.13.refs_0_, bf16[2096,128]{1,0:T(8,128)(2,1)S(1)} %collective-permute-done.3.refs_1_, bf16[2096,128]{1,0:T(8,128)(2,1)S(1)} %collective-permute-done.6.refs_2_.refs_4_, ...), custom_call_target="tpu_custom_call" | custom-call | flops 3000000000 | bytes 4000000 | tf_op jit(solution)/shard_map/score_rows/pallas_call | solution.py:348
  69.5 1.0 %score_rest.1 = f32[16,8,128]{2,1,0:T(8,128)S(1)} custom-call(f32[16,128]{1,0:T(8,128)S(1)} %get-tuple-element.19.refs_0_, bf16[512,16]{1,0:T(8,128)(2,1)S(1)} %get-tuple-element.20.refs_1_, bf16[2096,128]{1,0:T(8,128)(2,1)S(1)} %collective-permute-done.7.refs_4_.refs_2_, bf16[2096,128]{1,0:T(8,128)(2,1)S(1)} %collective-permute-done.5.refs_5_.refs_3_, ...), custom_call_target="tpu_custom_call" | custom-call | flops 500000000 | bytes 2000000 | tf_op jit(solution)/shard_map/score_rest/pallas_call | solution.py:360
  70.5 14.0 %all_to_all.10 = f32[16,8,128]{2,1,0:T(8,128)S(1)} all-to-all(f32[16,8,128]{2,1,0:T(8,128)S(1)} %score_rest.1), channel_id=1, replica_groups=mesh['group'=16,'owner'=32] {'group'}, dimensions={0} | all-to-all | bytes 131072 | tf_op jit(solution)/shard_map/all_to_all | solution.py:369
  84.5 0.5 slice_reduce_fusion
  (10 shorter events, 0.1 us)
Async XLA Ops:
  4.6 13.7 %copy-start = (s32[1,1,49,2]{2,3,1,0:T(2,128)S(1)}, s32[1,1,49,2]{2,3,1,0:T(2,128)}, u32[]{:S(2)}) copy-start(s32[1,1,49,2]{2,3,1,0:T(2,128)} %param.9) | copy-start | bytes 1180
  4.7 35.8 %all-to-all-start = ((bf16[32,104,128]{2,1,0:T(8,128)(2,1)}), bf16[32,104,128]{2,1,0:T(8,128)(2,1)S(1)}, u32[]{:S(2)}, u32[]{:S(2)}) async-start(bf16[32,104,128]{2,1,0:T(8,128)(2,1)} %send_rows.1), calls=%async_computation | async-start | bytes 1703936 | tf_op jit(solution)/shard_map/all_to_all | solution.py:307
  18.6 4.7 %collective-permute-start = (f32[16,128]{1,0:T(8,128)S(1)}, f32[16,128]{1,0:T(8,128)S(1)}, u32[]{:S(2)}, u32[]{:S(2)}) collective-permute-start(f32[16,128]{1,0:T(8,128)S(1)} %list_table.1), channel_id=1, source_target_pairs={{0,64},{32,96},{64,0},{96,32},{128,192},{160,224},{192,128},{224,1... | collective-permute-start | bytes 24584 | tf_op jit(solution)/shard_map/ppermute | solution.py:311
  23.3 5.6 %collective-permute-start.1 = (f32[16,128]{1,0:T(8,128)S(1)}, f32[16,128]{1,0:T(8,128)S(1)}, u32[]{:S(2)}, u32[]{:S(2)}) collective-permute-start(f32[16,128]{1,0:T(8,128)S(1)} %add.8), channel_id=1, source_target_pairs={{0,128},{32,160},{64,192},{96,224},{128,0},{160,32},{192,64},{224,... | collective-permute-start | bytes 24584 | tf_op jit(solution)/shard_map/ppermute | solution.py:311
  28.8 8.5 %collective-permute-start.2 = (f32[16,128]{1,0:T(8,128)S(1)}, f32[16,128]{1,0:T(8,128)S(1)}, u32[]{:S(2)}, u32[]{:S(2)}) collective-permute-start(f32[16,128]{1,0:T(8,128)S(1)} %add.9.refs_1_), channel_id=1, source_target_pairs={{0,256},{32,288},{64,320},{96,352},{128,384},{160,416},{192,448},{... | collective-permute-start | bytes 24584 | tf_op jit(solution)/shard_map/ppermute | solution.py:311
  41.9 19.0 %collective-permute-start.5 = (bf16[2096,128]{1,0:T(8,128)(2,1)S(1)}, bf16[2096,128]{1,0:T(8,128)(2,1)S(1)}, u32[]{:S(2)}, u32[]{:S(2)}) collective-permute-start(bf16[2096,128]{1,0:T(8,128)(2,1)S(1)} %get-tuple-element.13.refs_0_), channel_id=1, source_target_pairs={{0,31},{1,2},{2,1},{3,4},{4,3},{5,6},{6,5},{7,8},{8,7},{9,10},{10,... | collective-permute-start | bytes 1609736 | tf_op jit(solution)/shard_map/ppermute | solution.py:314
  45.6 15.4 %collective-permute-start.6 = (bf16[2096,128]{1,0:T(8,128)(2,1)S(1)}, bf16[2096,128]{1,0:T(8,128)(2,1)S(1)}, u32[]{:S(2)}, u32[]{:S(2)}) collective-permute-start(bf16[2096,128]{1,0:T(8,128)(2,1)S(1)} %get-tuple-element.13.refs_0_), channel_id=1, source_target_pairs={{0,64},{32,96},{64,128},{96,160},{128,192},{160,224},{192,256},{22... | collective-permute-start | bytes 1609736 | tf_op jit(solution)/shard_map/ppermute | solution.py:311
  48.7 12.4 %collective-permute-start.7 = (bf16[2096,128]{1,0:T(8,128)(2,1)S(1)}, bf16[2096,128]{1,0:T(8,128)(2,1)S(1)}, u32[]{:S(2)}, u32[]{:S(2)}) collective-permute-start(bf16[2096,128]{1,0:T(8,128)(2,1)S(1)} %get-tuple-element.13.refs_0_), channel_id=1, source_target_pairs={{0,1},{1,0},{2,3},{3,2},{4,5},{5,4},{6,7},{7,6},{8,9},{9,8},{10,11... | collective-permute-start | bytes 1609736 | tf_op jit(solution)/shard_map/ppermute | solution.py:314
  51.9 9.1 %collective-permute-start.4 = (bf16[1040,128]{1,0:T(8,128)(2,1)S(1)}, bf16[1040,128]{1,0:T(8,128)(2,1)S(1)}, u32[]{:S(2)}, u32[]{:S(2)}) collective-permute-start(bf16[1040,128]{1,0:T(8,128)(2,1)S(1)} %get-tuple-element.14), channel_id=1, source_target_pairs={{0,448},{32,480},{64,0},{96,32},{128,64},{160,96},{192,128},{224,1... | collective-permute-start | bytes 798728 | tf_op jit(solution)/shard_map/ppermute | solution.py:311
  55.7 11.5 %collective-permute-start.3 = (bf16[2096,128]{1,0:T(8,128)(2,1)S(1)}, bf16[2096,128]{1,0:T(8,128)(2,1)S(1)}, u32[]{:S(2)}, u32[]{:S(2)}) collective-permute-start(bf16[2096,128]{1,0:T(8,128)(2,1)S(1)} %get-tuple-element.13.refs_0_), channel_id=1, source_target_pairs={{0,32},{32,0},{64,96},{96,64},{128,160},{160,128},{192,224},{224,1... | collective-permute-start | bytes 1609736 | tf_op jit(solution)/shard_map/ppermute | solution.py:343
  61.1 8.4 %collective-permute-start.8 = (bf16[3120,128]{1,0:T(8,128)(2,1)S(1)}, bf16[3120,128]{1,0:T(8,128)(2,1)S(1)}, u32[]{:S(2)}, u32[]{:S(2)}) collective-permute-start(bf16[3120,128]{1,0:T(8,128)(2,1)S(1)} %pad_maximum_fusion), channel_id=1, source_target_pairs={{0,32},{32,0},{64,96},{96,64},{128,160},{160,128},{192,224},{224,1... | collective-permute-start | bytes 2396168 | tf_op jit(solution)/shard_map/ppermute | solution.py:347

commit v8 on v7

--- a/solution.py
+++ b/solution.py
@@ -212,9 +212,9 @@
     return jnp.where(filled > 0.5, result, -2.0)
 
 
-def first_score_kernel(blocks, feat, own_ref, twin_ref, back_ref, next_ref, left_ref, right_ref, out_ref, bias_ref):
+def first_score_kernel(blocks, feat, own_ref, next_ref, twin_ref, far_ref, back_ref, right_ref, left_ref, out_ref, bias_ref):
     size = feat + PAY_META
-    paired = own_ref[pl.ds(UNITS * size, PAY_META), :].astype(F32) + twin_ref[pl.ds(UNITS * size, PAY_META), :].astype(F32)
+    paired = own_ref[pl.ds(UNITS * size, PAY_META), :].astype(F32) + far_ref[pl.ds(UNITS * size, PAY_META), :].astype(F32)
     penalty = jnp.where(paired > 0.5, 0.0, -4.0).astype(BF16)
     across = [(left_ref, 0), (right_ref, 0), (left_ref, size), (right_ref, size)]
     marks = stack_numbers(across, feat)[0:1, :]
@@ -223,14 +223,14 @@
     across_bias = bias_of(penalty, marks)
     bias_ref[...] = across_bias
     across_rows = stack_rows(across, feat)
-    inside = [(twin_ref, size), (next_ref, 0), (back_ref, size), (own_ref, 0), (own_ref, size), (twin_ref, size)]
+    inside = [(far_ref, size), (next_ref, 0), (back_ref, size), (own_ref, 0), (own_ref, size), (far_ref, size)]
     inside_bias = bias_of(penalty, stack_numbers(inside, feat)[0:1, :] + blocks)
     inside_rows = stack_rows(inside, feat)
     row, lane = iota((4 * BLOCK, 2 * BLOCK), 0), iota((4 * BLOCK, 2 * BLOCK), 1)
     same = jnp.logical_and(row - 3 * BLOCK == lane, lane < BLOCK)
     groups = [
         ([(own_ref, 0), (twin_ref, 0)], 4, 0, 2, None),
-        ([(own_ref, size), (twin_ref, size)], 2, 1, 5, same),
+        ([(own_ref, size), (far_ref, size)], 2, 1, 5, same),
         ([(back_ref, 0), (next_ref, 0)], 4, 4, 6, None),
     ]
     best, numbers = [], []
@@ -244,12 +244,12 @@
     out_ref[...] = slot_table(jnp.concatenate(best, axis=1), jnp.concatenate(numbers, axis=1), blocks)
 
 
-def second_score_kernel(blocks, feat, table_ref, bias_ref, left_ref, right_ref, back_ref, late_ref, out_ref):
+def second_score_kernel(blocks, feat, table_ref, bias_ref, left_ref, right_ref, back_ref, far_ref, late_ref, out_ref):
     size = feat + PAY_META
     across_rows = stack_rows([(left_ref, 0), (right_ref, 0), (left_ref, size), (right_ref, size)], feat)
     across_bias = bias_ref[...]
     best, numbers = [], []
-    for places, count in (([(back_ref, size), (late_ref, size)], 2), ([(late_ref, 0), (late_ref, 2 * size)], 4)):
+    for places, count in (([(back_ref, size), (late_ref, 0)], 2), ([(far_ref, 0), (late_ref, size)], 4)):
         outer = slice(0, count * BLOCK)
         best.append(best_of(across_rows[outer], across_bias[outer], places, feat, blocks))
         numbers.append(stack_numbers(places, feat))
@@ -340,32 +340,32 @@
         compiler_params=PARAMS,
         name="unit_rows",
     )(arrived, here, there)
-    twin = lax.ppermute(both, "group", swap)
-    following, back = along_y(first, lambda y: y - 1), along_y(both, lambda y: y + 1)
+    back, following = along_y(both, lambda y: y + 1), along_y(first, lambda y: y - 1)
     left, right = along_owner(both, lambda o: o ^ 1), along_owner(both, lambda o: o + 2 * (o & 1) - 1)
-    following, right, back, left = lax.optimization_barrier((following, right, back, left))
-    late = lax.ppermute(jnp.concatenate([back[: 2 * size], following], axis=0), "group", swap)
+    twin = lax.ppermute(both[:size], "group", swap)
+    wing = lax.ppermute(jnp.concatenate([back[:size], both[size : 2 * size + PAY_META]], axis=0), "group", swap)
+    late = lax.ppermute(jnp.concatenate([back[size : 2 * size], following[:size]], axis=0), "group", swap)
     table, bias = pl.pallas_call(
         lambda *refs: first_score_kernel(n_group, feat, *refs),
         out_shape=[
             jax.ShapeDtypeStruct((n_group, BLOCK), F32),
             jax.ShapeDtypeStruct((4 * BLOCK, n_group), BF16),
         ],
-        in_specs=[vmem()] * 6,
+        in_specs=[vmem()] * 7,
         out_specs=[vmem()] * 2,
         compiler_params=PARAMS,
         cost_estimate=cost(3 * 10**9, 4 * 10**6),
         name="score_rows",
-    )(both, twin, back, following, left, right)
+    )(both, following, twin, wing, back, right, left)
     table = pl.pallas_call(
         lambda *refs: second_score_kernel(n_group, feat, *refs),
         out_shape=jax.ShapeDtypeStruct((n_group, 8, BLOCK), F32),
-        in_specs=[vmem()] * 6,
+        in_specs=[vmem()] * 7,
         out_specs=vmem(),
         compiler_params=PARAMS,
         cost_estimate=cost(5 * 10**8, 2 * 10**6),
         name="score_rest",
-    )(table, bias, left, right, back, late)
+    )(table, bias, left, right, back, wing, late)
     shares = lax.all_to_all(table, "group", split_axis=0, concat_axis=0, tiled=True)
     return jnp.max(shares[:, :1], axis=0)
 

time: 85.5 us -> 85.1 us (level)
  starting transfers between devices: 53.6 us -> 51.9 us
  blocking collectives: 14 us -> 15.1 us
    ppermute x2 -> x3, starting transfers between devices: 11.3 us -> 9.6 us  [the longest x1 5.25 us: on_device(): twin = lax.ppermute(both[:size], 'group', swap)]
    all_to_all x1, blocking collectives: 14 us -> 15.1 us  [on_device(): lax.all_to_all(table, 'group', split_axis=0, concat_axis=0, tiled=True)]
  transfers between devices with their start and end apart: 10 -> 11, of which waited for: 4 -> 4; matrix products, arithmetic and copies ran while one was open for 0% -> 0% of each run, Pallas kernels for 3% -> 3%
where the time goes in v8:
time: 85.1 us; the launch traced here: 84.6 us
  starting transfers between devices  51.9 us (61%)
  blocking collectives  15.1 us (18%)
  Pallas kernels  9.59 us (11%)
  waiting for transfers between devices  7.07 us (8%)
    ppermute x5, starting transfers between devices, along_y(): lax.ppermute(x, 'group', [(i, 2 * (partner(i // 2) % (n_group // 2)) + i...  21.9 us
    all_to_all x1, blocking collectives, on_device(): lax.all_to_all(table, 'group', split_axis=0, concat_axis=0, tiled=True)  15.1 us
    all_to_all x1, starting transfers between devices, on_device(): lax.all_to_all(outgoing, 'owner', split_axis=0, concat_axis=0, tiled=True)  13.7 us
    ppermute x2, starting transfers between devices, along_owner(): lax.ppermute(x, 'owner', [(i, partner(i) % n_owner) for i in range(n_owne...  6.71 us
    ppermute x1, starting transfers between devices, on_device(): twin = lax.ppermute(both[:size], 'group', swap)  5.25 us
    pallas_call x1, Pallas kernels, on_device(): pl.pallas_call(lambda *refs: send_kernel(n_owner, n_group, cap, 6, pieces...  4.63 us
    ppermute x5, waiting for transfers between devices, along_y(): lax.ppermute(x, 'group', [(i, 2 * (partner(i // 2) % (n_group // 2)) + i...  3.88 us
    all_to_all x1, waiting for transfers between devices, on_device(): lax.all_to_all(outgoing, 'owner', split_axis=0, concat_axis=0, tiled=True)  3.18 us
  transfers between devices with their start and end apart: 11, of which 4 were waited for; matrix products, arithmetic and copies ran while one was open for 0% of the time, Pallas kernels for 3%

profile of v8, /device:TPU:1, one launch (start us, length us, event | category | flops | bytes accessed | tf_op | source)
XLA Modules:
  0.0 84.6 jit_solution(9444667328240157314)
XLA Ops:
  0.0 4.6 %send_rows.1 = bf16[32,104,128]{2,1,0:T(8,128)(2,1)} custom-call(s32[1,2048]{1,0:T(1,128)} %bitcast.7, s32[1,32]{1,0:T(1,128)} %bitcast.10, s32[1,2048]{1,0:T(1,128)} %bitcast.8, bf16[2048,1024]{1,0:T(8,128)(2,1)} %refs_3_.1), custom_call_target="tpu_custom_call" | custom-call | tf_op jit(solution)/shard_map/send_rows/pallas_call | solution.py:286
  4.6 0.0 copy-start
  4.6 13.7 %all-to-all-start = ((bf16[32,104,128]{2,1,0:T(8,128)(2,1)}), bf16[32,104,128]{2,1,0:T(8,128)(2,1)S(1)}, u32[]{:S(2)}, u32[]{:S(2)}) async-start(bf16[32,104,128]{2,1,0:T(8,128)(2,1)} %send_rows.1), calls=%async_computation | async-start | bytes 1703936 | tf_op jit(solution)/shard_map/all_to_all | solution.py:307
  18.4 0.1 list_table.1
  18.5 3.2 %collective-permute-start = (f32[16,128]{1,0:T(8,128)S(1)}, f32[16,128]{1,0:T(8,128)S(1)}, u32[]{:S(2)}, u32[]{:S(2)}) collective-permute-start(f32[16,128]{1,0:T(8,128)S(1)} %list_table.1), channel_id=1, source_target_pairs={{0,64},{32,96},{64,0},{96,32},{128,192},{160,224},{192,128},{224,1... | collective-permute-start | bytes 24584 | tf_op jit(solution)/shard_map/ppermute | solution.py:311
  21.8 1.5 %collective-permute-done = f32[16,128]{1,0:T(8,128)S(1)} collective-permute-done((f32[16,128]{1,0:T(8,128)S(1)}, f32[16,128]{1,0:T(8,128)S(1)}, u32[]{:S(2)}, u32[]{:S(2)}) %collective-permute-start) | collective-permute-done | bytes 8224 | tf_op jit(solution)/shard_map/ppermute | solution.py:311
  23.2 4.2 %collective-permute-start.1 = (f32[16,128]{1,0:T(8,128)S(1)}, f32[16,128]{1,0:T(8,128)S(1)}, u32[]{:S(2)}, u32[]{:S(2)}) collective-permute-start(f32[16,128]{1,0:T(8,128)S(1)} %add.8), channel_id=1, source_target_pairs={{0,128},{32,160},{64,192},{96,224},{128,0},{160,32},{192,64},{224,... | collective-permute-start | bytes 24584 | tf_op jit(solution)/shard_map/ppermute | solution.py:311
  27.4 1.4 %collective-permute-done.1 = f32[16,128]{1,0:T(8,128)S(1)} collective-permute-done((f32[16,128]{1,0:T(8,128)S(1)}, f32[16,128]{1,0:T(8,128)S(1)}, u32[]{:S(2)}, u32[]{:S(2)}) %collective-permute-start.1) | collective-permute-done | bytes 8224 | tf_op jit(solution)/shard_map/ppermute | solution.py:311
  28.8 7.4 %collective-permute-start.2 = (f32[16,128]{1,0:T(8,128)S(1)}, f32[16,128]{1,0:T(8,128)S(1)}, u32[]{:S(2)}, u32[]{:S(2)}) collective-permute-start(f32[16,128]{1,0:T(8,128)S(1)} %add.9.refs_1_), channel_id=1, source_target_pairs={{0,256},{32,288},{64,320},{96,352},{128,384},{160,416},{192,448},{... | collective-permute-start | bytes 24584 | tf_op jit(solution)/shard_map/ppermute | solution.py:311
  36.3 1.0 %collective-permute-done.2.refs_2_ = f32[16,128]{1,0:T(8,128)S(1)} collective-permute-done((f32[16,128]{1,0:T(8,128)S(1)}, f32[16,128]{1,0:T(8,128)S(1)}, u32[]{:S(2)}, u32[]{:S(2)}) %collective-permute-start.2) | collective-permute-done | bytes 8224 | tf_op jit(solution)/shard_map/ppermute | solution.py:311
  37.3 3.2 %all-to-all-done.refs_0_ = bf16[32,104,128]{2,1,0:T(8,128)(2,1)S(1)} async-done(((bf16[32,104,128]{2,1,0:T(8,128)(2,1)}), bf16[32,104,128]{2,1,0:T(8,128)(2,1)S(1)}, u32[]{:S(2)}, u32[]{:S(2)}) %all-to-all-start) | async-done | bytes 852000 | tf_op jit(solution)/shard_map/all_to_all | solution.py:307
  40.5 1.5 %unit_rows.1 = (bf16[2096,128]{1,0:T(8,128)(2,1)S(1)}, bf16[1040,128]{1,0:T(8,128)(2,1)S(1)}) custom-call(bf16[32,104,128]{2,1,0:T(8,128)(2,1)S(1)} %all-to-all-done.refs_0_, f32[16,128]{1,0:T(8,128)S(1)} %add.9.refs_1_, f32[16,128]{1,0:T(8,128)S(1)} %collective-permute-done.2.refs_2_), custom_call_target="tpu_custom_call" | custom-call | tf_op jit(solution)/shard_map/unit_rows/pallas_call | solution.py:331
  41.9 3.2 %collective-permute-start.5 = (bf16[2096,128]{1,0:T(8,128)(2,1)S(1)}, bf16[2096,128]{1,0:T(8,128)(2,1)S(1)}, u32[]{:S(2)}, u32[]{:S(2)}) collective-permute-start(bf16[2096,128]{1,0:T(8,128)(2,1)S(1)} %get-tuple-element.9.refs_0_), channel_id=1, source_target_pairs={{0,64},{32,96},{64,128},{96,160},{128,192},{160,224},{192,256},{22... | collective-permute-start | bytes 1609736 | tf_op jit(solution)/shard_map/ppermute | solution.py:311
  45.2 3.5 %collective-permute-start.7 = (bf16[2096,128]{1,0:T(8,128)(2,1)S(1)}, bf16[2096,128]{1,0:T(8,128)(2,1)S(1)}, u32[]{:S(2)}, u32[]{:S(2)}) collective-permute-start(bf16[2096,128]{1,0:T(8,128)(2,1)S(1)} %get-tuple-element.9.refs_0_), channel_id=1, source_target_pairs={{0,31},{1,2},{2,1},{3,4},{4,3},{5,6},{6,5},{7,8},{8,7},{9,10},{10,... | collective-permute-start | bytes 1609736 | tf_op jit(solution)/shard_map/ppermute | solution.py:314
  48.7 3.2 %collective-permute-start.8 = (bf16[2096,128]{1,0:T(8,128)(2,1)S(1)}, bf16[2096,128]{1,0:T(8,128)(2,1)S(1)}, u32[]{:S(2)}, u32[]{:S(2)}) collective-permute-start(bf16[2096,128]{1,0:T(8,128)(2,1)S(1)} %get-tuple-element.9.refs_0_), channel_id=1, source_target_pairs={{0,1},{1,0},{2,3},{3,2},{4,5},{5,4},{6,7},{7,6},{8,9},{9,8},{10,11... | collective-permute-start | bytes 1609736 | tf_op jit(solution)/shard_map/ppermute | solution.py:314
  51.9 3.8 %collective-permute-start.3 = (bf16[1040,128]{1,0:T(8,128)(2,1)S(1)}, bf16[1040,128]{1,0:T(8,128)(2,1)S(1)}, u32[]{:S(2)}, u32[]{:S(2)}) collective-permute-start(bf16[1040,128]{1,0:T(8,128)(2,1)S(1)} %get-tuple-element.10), channel_id=1, source_target_pairs={{0,448},{32,480},{64,0},{96,32},{128,64},{160,96},{192,128},{224,1... | collective-permute-start | bytes 798728 | tf_op jit(solution)/shard_map/ppermute | solution.py:311
  55.8 5.2 %collective-permute-start.4 = (bf16[1040,128]{1,0:T(8,128)(2,1)S(1)}, bf16[1040,128]{1,0:T(8,128)(2,1)S(1)}, u32[]{:S(2)}, u32[]{:S(2)}) collective-permute-start(bf16[1040,128]{1,0:T(8,128)(2,1)S(1)} %slice.15), channel_id=1, source_target_pairs={{0,32},{32,0},{64,96},{96,64},{128,160},{160,128},{192,224},{224,1... | collective-permute-start | bytes 798728 | tf_op jit(solution)/shard_map/ppermute | solution.py:345
  61.1 1.9 %collective-permute-start.6 = (bf16[2096,128]{1,0:T(8,128)(2,1)S(1)}, bf16[2096,128]{1,0:T(8,128)(2,1)S(1)}, u32[]{:S(2)}, u32[]{:S(2)}) collective-permute-start(bf16[2096,128]{1,0:T(8,128)(2,1)S(1)} %pad_maximum_fusion), channel_id=1, source_target_pairs={{0,32},{32,0},{64,96},{96,64},{128,160},{160,128},{192,224},{224,1... | collective-permute-start | bytes 1609736 | tf_op jit(solution)/shard_map/ppermute | solution.py:346
  63.1 0.0 collective-permute-done.3.refs_1_
  63.1 2.4 %collective-permute-start.9 = (bf16[2080,128]{1,0:T(8,128)(2,1)S(1)}, bf16[2080,128]{1,0:T(8,128)(2,1)S(1)}, u32[]{:S(2)}, u32[]{:S(2)}) collective-permute-start(bf16[2080,128]{1,0:T(8,128)(2,1)S(1)} %pad_maximum_fusion.1), channel_id=1, source_target_pairs={{0,32},{32,0},{64,96},{96,64},{128,160},{160,128},{192,224},{224,1... | collective-permute-start | bytes 1597448 | tf_op jit(solution)/shard_map/ppermute | solution.py:347
  65.6 2.3 %score_rows.1 = (f32[16,128]{1,0:T(8,128)S(1)}, bf16[512,16]{1,0:T(8,128)(2,1)S(1)}) custom-call(bf16[2096,128]{1,0:T(8,128)(2,1)S(1)} %get-tuple-element.9.refs_0_, bf16[1040,128]{1,0:T(8,128)(2,1)S(1)} %collective-permute-done.3.refs_1_, bf16[1040,128]{1,0:T(8,128)(2,1)S(1)} %collective-permute-done.4.refs_2_, ...), custom_call_target="tpu_custom_call" | custom-call | flops 3000000000 | bytes 4000000 | tf_op jit(solution)/shard_map/score_rows/pallas_call | solution.py:348
  67.9 1.0 %score_rest.1 = f32[16,8,128]{2,1,0:T(8,128)S(1)} custom-call(f32[16,128]{1,0:T(8,128)S(1)} %get-tuple-element.11.refs_0_, bf16[512,16]{1,0:T(8,128)(2,1)S(1)} %get-tuple-element.12.refs_1_, bf16[2096,128]{1,0:T(8,128)(2,1)S(1)} %collective-permute-done.8.refs_6_.refs_2_, bf16[2096,128]{1,0:T(8,128)(2,1)S(1)} %collective-permute-done.7.refs_5_.refs_3_, ...), custom_call_target="tpu_custom_call" | custom-call | flops 500000000 | bytes 2000000 | tf_op jit(solution)/shard_map/score_rest/pallas_call | solution.py:360
  69.0 15.1 %all_to_all.10 = f32[16,8,128]{2,1,0:T(8,128)S(1)} all-to-all(f32[16,8,128]{2,1,0:T(8,128)S(1)} %score_rest.1), channel_id=1, replica_groups=mesh['group'=16,'owner'=32] {'group'}, dimensions={0} | all-to-all | bytes 131072 | tf_op jit(solution)/shard_map/all_to_all | solution.py:369
  84.0 0.5 slice_reduce_fusion
  (15 shorter events, 0.2 us)
Async XLA Ops:
  4.6 13.7 %copy-start = (s32[1,1,49,2]{2,3,1,0:T(2,128)S(1)}, s32[1,1,49,2]{2,3,1,0:T(2,128)}, u32[]{:S(2)}) copy-start(s32[1,1,49,2]{2,3,1,0:T(2,128)} %param.9) | copy-start | bytes 1180
  4.6 35.8 %all-to-all-start = ((bf16[32,104,128]{2,1,0:T(8,128)(2,1)}), bf16[32,104,128]{2,1,0:T(8,128)(2,1)S(1)}, u32[]{:S(2)}, u32[]{:S(2)}) async-start(bf16[32,104,128]{2,1,0:T(8,128)(2,1)} %send_rows.1), calls=%async_computation | async-start | bytes 1703936 | tf_op jit(solution)/shard_map/all_to_all | solution.py:307
  18.5 4.7 %collective-permute-start = (f32[16,128]{1,0:T(8,128)S(1)}, f32[16,128]{1,0:T(8,128)S(1)}, u32[]{:S(2)}, u32[]{:S(2)}) collective-permute-start(f32[16,128]{1,0:T(8,128)S(1)} %list_table.1), channel_id=1, source_target_pairs={{0,64},{32,96},{64,0},{96,32},{128,192},{160,224},{192,128},{224,1... | collective-permute-start | bytes 24584 | tf_op jit(solution)/shard_map/ppermute | solution.py:311
  23.2 5.6 %collective-permute-start.1 = (f32[16,128]{1,0:T(8,128)S(1)}, f32[16,128]{1,0:T(8,128)S(1)}, u32[]{:S(2)}, u32[]{:S(2)}) collective-permute-start(f32[16,128]{1,0:T(8,128)S(1)} %add.8), channel_id=1, source_target_pairs={{0,128},{32,160},{64,192},{96,224},{128,0},{160,32},{192,64},{224,... | collective-permute-start | bytes 24584 | tf_op jit(solution)/shard_map/ppermute | solution.py:311
  28.8 8.5 %collective-permute-start.2 = (f32[16,128]{1,0:T(8,128)S(1)}, f32[16,128]{1,0:T(8,128)S(1)}, u32[]{:S(2)}, u32[]{:S(2)}) collective-permute-start(f32[16,128]{1,0:T(8,128)S(1)} %add.9.refs_1_), channel_id=1, source_target_pairs={{0,256},{32,288},{64,320},{96,352},{128,384},{160,416},{192,448},{... | collective-permute-start | bytes 24584 | tf_op jit(solution)/shard_map/ppermute | solution.py:311
  41.9 19.1 %collective-permute-start.5 = (bf16[2096,128]{1,0:T(8,128)(2,1)S(1)}, bf16[2096,128]{1,0:T(8,128)(2,1)S(1)}, u32[]{:S(2)}, u32[]{:S(2)}) collective-permute-start(bf16[2096,128]{1,0:T(8,128)(2,1)S(1)} %get-tuple-element.9.refs_0_), channel_id=1, source_target_pairs={{0,64},{32,96},{64,128},{96,160},{128,192},{160,224},{192,256},{22... | collective-permute-start | bytes 1609736 | tf_op jit(solution)/shard_map/ppermute | solution.py:311
  45.2 20.3 %collective-permute-start.7 = (bf16[2096,128]{1,0:T(8,128)(2,1)S(1)}, bf16[2096,128]{1,0:T(8,128)(2,1)S(1)}, u32[]{:S(2)}, u32[]{:S(2)}) collective-permute-start(bf16[2096,128]{1,0:T(8,128)(2,1)S(1)} %get-tuple-element.9.refs_0_), channel_id=1, source_target_pairs={{0,31},{1,2},{2,1},{3,4},{4,3},{5,6},{6,5},{7,8},{8,7},{9,10},{10,... | collective-permute-start | bytes 1609736 | tf_op jit(solution)/shard_map/ppermute | solution.py:314
  48.7 16.9 %collective-permute-start.8 = (bf16[2096,128]{1,0:T(8,128)(2,1)S(1)}, bf16[2096,128]{1,0:T(8,128)(2,1)S(1)}, u32[]{:S(2)}, u32[]{:S(2)}) collective-permute-start(bf16[2096,128]{1,0:T(8,128)(2,1)S(1)} %get-tuple-element.9.refs_0_), channel_id=1, source_target_pairs={{0,1},{1,0},{2,3},{3,2},{4,5},{5,4},{6,7},{7,6},{8,9},{9,8},{10,11... | collective-permute-start | bytes 1609736 | tf_op jit(solution)/shard_map/ppermute | solution.py:314
  51.9 11.1 %collective-permute-start.3 = (bf16[1040,128]{1,0:T(8,128)(2,1)S(1)}, bf16[1040,128]{1,0:T(8,128)(2,1)S(1)}, u32[]{:S(2)}, u32[]{:S(2)}) collective-permute-start(bf16[1040,128]{1,0:T(8,128)(2,1)S(1)} %get-tuple-element.10), channel_id=1, source_target_pairs={{0,448},{32,480},{64,0},{96,32},{128,64},{160,96},{192,128},{224,1... | collective-permute-start | bytes 798728 | tf_op jit(solution)/shard_map/ppermute | solution.py:311
  55.8 9.8 %collective-permute-start.4 = (bf16[1040,128]{1,0:T(8,128)(2,1)S(1)}, bf16[1040,128]{1,0:T(8,128)(2,1)S(1)}, u32[]{:S(2)}, u32[]{:S(2)}) collective-permute-start(bf16[1040,128]{1,0:T(8,128)(2,1)S(1)} %slice.15), channel_id=1, source_target_pairs={{0,32},{32,0},{64,96},{96,64},{128,160},{160,128},{192,224},{224,1... | collective-permute-start | bytes 798728 | tf_op jit(solution)/shard_map/ppermute | solution.py:345
  61.1 4.5 %collective-permute-start.6 = (bf16[2096,128]{1,0:T(8,128)(2,1)S(1)}, bf16[2096,128]{1,0:T(8,128)(2,1)S(1)}, u32[]{:S(2)}, u32[]{:S(2)}) collective-permute-start(bf16[2096,128]{1,0:T(8,128)(2,1)S(1)} %pad_maximum_fusion), channel_id=1, source_target_pairs={{0,32},{32,0},{64,96},{96,64},{128,160},{160,128},{192,224},{224,1... | collective-permute-start | bytes 1609736 | tf_op jit(solution)/shard_map/ppermute | solution.py:346
  63.1 4.8 %collective-permute-start.9 = (bf16[2080,128]{1,0:T(8,128)(2,1)S(1)}, bf16[2080,128]{1,0:T(8,128)(2,1)S(1)}, u32[]{:S(2)}, u32[]{:S(2)}) collective-permute-start(bf16[2080,128]{1,0:T(8,128)(2,1)S(1)} %pad_maximum_fusion.1), channel_id=1, source_target_pairs={{0,32},{32,0},{64,96},{96,64},{128,160},{160,128},{192,224},{224,1... | collective-permute-start | bytes 1597448 | tf_op jit(solution)/shard_map/ppermute | solution.py:347

commit v9 on v8

--- a/solution.py
+++ b/solution.py
@@ -233,11 +233,12 @@
         ([(own_ref, size), (far_ref, size)], 2, 1, 5, same),
         ([(back_ref, 0), (next_ref, 0)], 4, 4, 6, None),
     ]
+    wide = best_of(across_rows, across_bias, groups[0][0] + groups[2][0], feat, blocks)
+    near = best_of(across_rows[: 2 * BLOCK], across_bias[: 2 * BLOCK], groups[1][0], feat, blocks)
+    outer = [wide[:, : 2 * BLOCK], near, wide[:, 2 * BLOCK :]]
     best, numbers = [], []
-    for places, count, low, high, equal in groups:
+    for one, (places, _, low, high, equal) in zip(outer, groups):
         part = slice(low * BLOCK, high * BLOCK)
-        outer = slice(0, count * BLOCK)
-        one = best_of(across_rows[outer], across_bias[outer], places, feat, blocks)
         two = best_of(inside_rows[part], inside_bias[part], places, feat, blocks, equal)
         best.append(jnp.maximum(one, two))
         numbers.append(stack_numbers(places, feat))
@@ -367,7 +368,7 @@
         name="score_rest",
     )(table, bias, left, right, back, wing, late)
     shares = lax.all_to_all(table, "group", split_axis=0, concat_axis=0, tiled=True)
-    return jnp.max(shares[:, :1], axis=0)
+    return jnp.max(shares, axis=(0, 1)).reshape(1, LANES)
 
 
 def solution(mesh):

time: 85.1 us -> 85.1 us (level)
  no operation moved by 1% of the time
where the time goes in v9:
time: 85.1 us; the launch traced here: 84.6 us
  starting transfers between devices  51.9 us (61%)
  blocking collectives  15.1 us (18%)
  Pallas kernels  9.62 us (11%)
  waiting for transfers between devices  7.07 us (8%)
    ppermute x5, starting transfers between devices, along_y(): lax.ppermute(x, 'group', [(i, 2 * (partner(i // 2) % (n_group // 2)) + i...  21.9 us
    all_to_all x1, blocking collectives, on_device(): lax.all_to_all(table, 'group', split_axis=0, concat_axis=0, tiled=True)  15.1 us
    all_to_all x1, starting transfers between devices, on_device(): lax.all_to_all(outgoing, 'owner', split_axis=0, concat_axis=0, tiled=True)  13.7 us
    ppermute x2, starting transfers between devices, along_owner(): lax.ppermute(x, 'owner', [(i, partner(i) % n_owner) for i in range(n_owne...  6.71 us
    ppermute x1, starting transfers between devices, on_device(): twin = lax.ppermute(both[:size], 'group', swap)  5.25 us
    pallas_call x1, Pallas kernels, on_device(): pl.pallas_call(lambda *refs: send_kernel(n_owner, n_group, cap, 6, pieces...  4.63 us
    ppermute x5, waiting for transfers between devices, along_y(): lax.ppermute(x, 'group', [(i, 2 * (partner(i // 2) % (n_group // 2)) + i...  3.88 us
    all_to_all x1, waiting for transfers between devices, on_device(): lax.all_to_all(outgoing, 'owner', split_axis=0, concat_axis=0, tiled=True)  3.18 us
  transfers between devices with their start and end apart: 11, of which 4 were waited for; matrix products, arithmetic and copies ran while one was open for 0% of the time, Pallas kernels for 3%

profile of v9, /device:TPU:1, one launch (start us, length us, event | category | flops | bytes accessed | tf_op | source)
XLA Modules:
  0.0 84.6 jit_solution(7069038609149651515)
XLA Ops:
  0.0 4.6 %send_rows.1 = bf16[32,104,128]{2,1,0:T(8,128)(2,1)} custom-call(s32[1,2048]{1,0:T(1,128)} %bitcast.7, s32[1,32]{1,0:T(1,128)} %bitcast.10, s32[1,2048]{1,0:T(1,128)} %bitcast.8, bf16[2048,1024]{1,0:T(8,128)(2,1)} %refs_3_.1), custom_call_target="tpu_custom_call" | custom-call | tf_op jit(solution)/shard_map/send_rows/pallas_call | solution.py:287
  4.6 0.0 copy-start
  4.6 13.7 %all-to-all-start = ((bf16[32,104,128]{2,1,0:T(8,128)(2,1)}), bf16[32,104,128]{2,1,0:T(8,128)(2,1)S(1)}, u32[]{:S(2)}, u32[]{:S(2)}) async-start(bf16[32,104,128]{2,1,0:T(8,128)(2,1)} %send_rows.1), calls=%async_computation | async-start | bytes 1703936 | tf_op jit(solution)/shard_map/all_to_all | solution.py:308
  18.4 0.1 list_table.1
  18.5 3.2 %collective-permute-start = (f32[16,128]{1,0:T(8,128)S(1)}, f32[16,128]{1,0:T(8,128)S(1)}, u32[]{:S(2)}, u32[]{:S(2)}) collective-permute-start(f32[16,128]{1,0:T(8,128)S(1)} %list_table.1), channel_id=1, source_target_pairs={{0,64},{32,96},{64,0},{96,32},{128,192},{160,224},{192,128},{224,1... | collective-permute-start | bytes 24584 | tf_op jit(solution)/shard_map/ppermute | solution.py:312
  21.8 1.5 %collective-permute-done = f32[16,128]{1,0:T(8,128)S(1)} collective-permute-done((f32[16,128]{1,0:T(8,128)S(1)}, f32[16,128]{1,0:T(8,128)S(1)}, u32[]{:S(2)}, u32[]{:S(2)}) %collective-permute-start) | collective-permute-done | bytes 8224 | tf_op jit(solution)/shard_map/ppermute | solution.py:312
  23.2 4.2 %collective-permute-start.1 = (f32[16,128]{1,0:T(8,128)S(1)}, f32[16,128]{1,0:T(8,128)S(1)}, u32[]{:S(2)}, u32[]{:S(2)}) collective-permute-start(f32[16,128]{1,0:T(8,128)S(1)} %add.8), channel_id=1, source_target_pairs={{0,128},{32,160},{64,192},{96,224},{128,0},{160,32},{192,64},{224,... | collective-permute-start | bytes 24584 | tf_op jit(solution)/shard_map/ppermute | solution.py:312
  27.4 1.4 %collective-permute-done.1 = f32[16,128]{1,0:T(8,128)S(1)} collective-permute-done((f32[16,128]{1,0:T(8,128)S(1)}, f32[16,128]{1,0:T(8,128)S(1)}, u32[]{:S(2)}, u32[]{:S(2)}) %collective-permute-start.1) | collective-permute-done | bytes 8224 | tf_op jit(solution)/shard_map/ppermute | solution.py:312
  28.8 7.4 %collective-permute-start.2 = (f32[16,128]{1,0:T(8,128)S(1)}, f32[16,128]{1,0:T(8,128)S(1)}, u32[]{:S(2)}, u32[]{:S(2)}) collective-permute-start(f32[16,128]{1,0:T(8,128)S(1)} %add.9.refs_1_), channel_id=1, source_target_pairs={{0,256},{32,288},{64,320},{96,352},{128,384},{160,416},{192,448},{... | collective-permute-start | bytes 24584 | tf_op jit(solution)/shard_map/ppermute | solution.py:312
  36.3 1.0 %collective-permute-done.2.refs_2_ = f32[16,128]{1,0:T(8,128)S(1)} collective-permute-done((f32[16,128]{1,0:T(8,128)S(1)}, f32[16,128]{1,0:T(8,128)S(1)}, u32[]{:S(2)}, u32[]{:S(2)}) %collective-permute-start.2) | collective-permute-done | bytes 8224 | tf_op jit(solution)/shard_map/ppermute | solution.py:312
  37.3 3.2 %all-to-all-done.refs_0_ = bf16[32,104,128]{2,1,0:T(8,128)(2,1)S(1)} async-done(((bf16[32,104,128]{2,1,0:T(8,128)(2,1)}), bf16[32,104,128]{2,1,0:T(8,128)(2,1)S(1)}, u32[]{:S(2)}, u32[]{:S(2)}) %all-to-all-start) | async-done | bytes 852000 | tf_op jit(solution)/shard_map/all_to_all | solution.py:308
  40.5 1.5 %unit_rows.1 = (bf16[2096,128]{1,0:T(8,128)(2,1)S(1)}, bf16[1040,128]{1,0:T(8,128)(2,1)S(1)}) custom-call(bf16[32,104,128]{2,1,0:T(8,128)(2,1)S(1)} %all-to-all-done.refs_0_, f32[16,128]{1,0:T(8,128)S(1)} %add.9.refs_1_, f32[16,128]{1,0:T(8,128)S(1)} %collective-permute-done.2.refs_2_), custom_call_target="tpu_custom_call" | custom-call | tf_op jit(solution)/shard_map/unit_rows/pallas_call | solution.py:332
  41.9 3.2 %collective-permute-start.5 = (bf16[2096,128]{1,0:T(8,128)(2,1)S(1)}, bf16[2096,128]{1,0:T(8,128)(2,1)S(1)}, u32[]{:S(2)}, u32[]{:S(2)}) collective-permute-start(bf16[2096,128]{1,0:T(8,128)(2,1)S(1)} %get-tuple-element.9.refs_0_), channel_id=1, source_target_pairs={{0,64},{32,96},{64,128},{96,160},{128,192},{160,224},{192,256},{22... | collective-permute-start | bytes 1609736 | tf_op jit(solution)/shard_map/ppermute | solution.py:312
  45.2 3.5 %collective-permute-start.7 = (bf16[2096,128]{1,0:T(8,128)(2,1)S(1)}, bf16[2096,128]{1,0:T(8,128)(2,1)S(1)}, u32[]{:S(2)}, u32[]{:S(2)}) collective-permute-start(bf16[2096,128]{1,0:T(8,128)(2,1)S(1)} %get-tuple-element.9.refs_0_), channel_id=1, source_target_pairs={{0,31},{1,2},{2,1},{3,4},{4,3},{5,6},{6,5},{7,8},{8,7},{9,10},{10,... | collective-permute-start | bytes 1609736 | tf_op jit(solution)/shard_map/ppermute | solution.py:315
  48.7 3.2 %collective-permute-start.8 = (bf16[2096,128]{1,0:T(8,128)(2,1)S(1)}, bf16[2096,128]{1,0:T(8,128)(2,1)S(1)}, u32[]{:S(2)}, u32[]{:S(2)}) collective-permute-start(bf16[2096,128]{1,0:T(8,128)(2,1)S(1)} %get-tuple-element.9.refs_0_), channel_id=1, source_target_pairs={{0,1},{1,0},{2,3},{3,2},{4,5},{5,4},{6,7},{7,6},{8,9},{9,8},{10,11... | collective-permute-start | bytes 1609736 | tf_op jit(solution)/shard_map/ppermute | solution.py:315
  51.9 3.8 %collective-permute-start.3 = (bf16[1040,128]{1,0:T(8,128)(2,1)S(1)}, bf16[1040,128]{1,0:T(8,128)(2,1)S(1)}, u32[]{:S(2)}, u32[]{:S(2)}) collective-permute-start(bf16[1040,128]{1,0:T(8,128)(2,1)S(1)} %get-tuple-element.10), channel_id=1, source_target_pairs={{0,448},{32,480},{64,0},{96,32},{128,64},{160,96},{192,128},{224,1... | collective-permute-start | bytes 798728 | tf_op jit(solution)/shard_map/ppermute | solution.py:312
  55.8 5.2 %collective-permute-start.4 = (bf16[1040,128]{1,0:T(8,128)(2,1)S(1)}, bf16[1040,128]{1,0:T(8,128)(2,1)S(1)}, u32[]{:S(2)}, u32[]{:S(2)}) collective-permute-start(bf16[1040,128]{1,0:T(8,128)(2,1)S(1)} %slice.12), channel_id=1, source_target_pairs={{0,32},{32,0},{64,96},{96,64},{128,160},{160,128},{192,224},{224,1... | collective-permute-start | bytes 798728 | tf_op jit(solution)/shard_map/ppermute | solution.py:346
  61.1 1.9 %collective-permute-start.6 = (bf16[2096,128]{1,0:T(8,128)(2,1)S(1)}, bf16[2096,128]{1,0:T(8,128)(2,1)S(1)}, u32[]{:S(2)}, u32[]{:S(2)}) collective-permute-start(bf16[2096,128]{1,0:T(8,128)(2,1)S(1)} %pad_maximum_fusion), channel_id=1, source_target_pairs={{0,32},{32,0},{64,96},{96,64},{128,160},{160,128},{192,224},{224,1... | collective-permute-start | bytes 1609736 | tf_op jit(solution)/shard_map/ppermute | solution.py:347
  63.1 0.0 collective-permute-done.3.refs_1_
  63.1 2.4 %collective-permute-start.9 = (bf16[2080,128]{1,0:T(8,128)(2,1)S(1)}, bf16[2080,128]{1,0:T(8,128)(2,1)S(1)}, u32[]{:S(2)}, u32[]{:S(2)}) collective-permute-start(bf16[2080,128]{1,0:T(8,128)(2,1)S(1)} %pad_maximum_fusion.1), channel_id=1, source_target_pairs={{0,32},{32,0},{64,96},{96,64},{128,160},{160,128},{192,224},{224,1... | collective-permute-start | bytes 1597448 | tf_op jit(solution)/shard_map/ppermute | solution.py:348
  65.6 2.4 %score_rows.1 = (f32[16,128]{1,0:T(8,128)S(1)}, bf16[512,16]{1,0:T(8,128)(2,1)S(1)}) custom-call(bf16[2096,128]{1,0:T(8,128)(2,1)S(1)} %get-tuple-element.9.refs_0_, bf16[1040,128]{1,0:T(8,128)(2,1)S(1)} %collective-permute-done.3.refs_1_, bf16[1040,128]{1,0:T(8,128)(2,1)S(1)} %collective-permute-done.4.refs_2_, ...), custom_call_target="tpu_custom_call" | custom-call | flops 3000000000 | bytes 4000000 | tf_op jit(solution)/shard_map/score_rows/pallas_call | solution.py:349
  68.0 1.0 %score_rest.1 = f32[16,8,128]{2,1,0:T(8,128)S(1)} custom-call(f32[16,128]{1,0:T(8,128)S(1)} %get-tuple-element.11.refs_0_, bf16[512,16]{1,0:T(8,128)(2,1)S(1)} %get-tuple-element.12.refs_1_, bf16[2096,128]{1,0:T(8,128)(2,1)S(1)} %collective-permute-done.8.refs_6_.refs_2_, bf16[2096,128]{1,0:T(8,128)(2,1)S(1)} %collective-permute-done.7.refs_5_.refs_3_, ...), custom_call_target="tpu_custom_call" | custom-call | flops 500000000 | bytes 2000000 | tf_op jit(solution)/shard_map/score_rest/pallas_call | solution.py:361
  69.0 15.1 %all_to_all.10 = f32[16,8,128]{2,1,0:T(8,128)S(1)} all-to-all(f32[16,8,128]{2,1,0:T(8,128)S(1)} %score_rest.1), channel_id=1, replica_groups=mesh['group'=16,'owner'=32] {'group'}, dimensions={0} | all-to-all | bytes 131072 | tf_op jit(solution)/shard_map/all_to_all | solution.py:370
  84.1 0.5 reduce_max.9
  (15 shorter events, 0.2 us)
Async XLA Ops:
  4.6 13.7 %copy-start = (s32[1,1,49,2]{2,3,1,0:T(2,128)S(1)}, s32[1,1,49,2]{2,3,1,0:T(2,128)}, u32[]{:S(2)}) copy-start(s32[1,1,49,2]{2,3,1,0:T(2,128)} %param.9) | copy-start | bytes 1180
  4.6 35.8 %all-to-all-start = ((bf16[32,104,128]{2,1,0:T(8,128)(2,1)}), bf16[32,104,128]{2,1,0:T(8,128)(2,1)S(1)}, u32[]{:S(2)}, u32[]{:S(2)}) async-start(bf16[32,104,128]{2,1,0:T(8,128)(2,1)} %send_rows.1), calls=%async_computation | async-start | bytes 1703936 | tf_op jit(solution)/shard_map/all_to_all | solution.py:308
  18.5 4.7 %collective-permute-start = (f32[16,128]{1,0:T(8,128)S(1)}, f32[16,128]{1,0:T(8,128)S(1)}, u32[]{:S(2)}, u32[]{:S(2)}) collective-permute-start(f32[16,128]{1,0:T(8,128)S(1)} %list_table.1), channel_id=1, source_target_pairs={{0,64},{32,96},{64,0},{96,32},{128,192},{160,224},{192,128},{224,1... | collective-permute-start | bytes 24584 | tf_op jit(solution)/shard_map/ppermute | solution.py:312
  23.2 5.6 %collective-permute-start.1 = (f32[16,128]{1,0:T(8,128)S(1)}, f32[16,128]{1,0:T(8,128)S(1)}, u32[]{:S(2)}, u32[]{:S(2)}) collective-permute-start(f32[16,128]{1,0:T(8,128)S(1)} %add.8), channel_id=1, source_target_pairs={{0,128},{32,160},{64,192},{96,224},{128,0},{160,32},{192,64},{224,... | collective-permute-start | bytes 24584 | tf_op jit(solution)/shard_map/ppermute | solution.py:312
  28.8 8.5 %collective-permute-start.2 = (f32[16,128]{1,0:T(8,128)S(1)}, f32[16,128]{1,0:T(8,128)S(1)}, u32[]{:S(2)}, u32[]{:S(2)}) collective-permute-start(f32[16,128]{1,0:T(8,128)S(1)} %add.9.refs_1_), channel_id=1, source_target_pairs={{0,256},{32,288},{64,320},{96,352},{128,384},{160,416},{192,448},{... | collective-permute-start | bytes 24584 | tf_op jit(solution)/shard_map/ppermute | solution.py:312
  41.9 19.1 %collective-permute-start.5 = (bf16[2096,128]{1,0:T(8,128)(2,1)S(1)}, bf16[2096,128]{1,0:T(8,128)(2,1)S(1)}, u32[]{:S(2)}, u32[]{:S(2)}) collective-permute-start(bf16[2096,128]{1,0:T(8,128)(2,1)S(1)} %get-tuple-element.9.refs_0_), channel_id=1, source_target_pairs={{0,64},{32,96},{64,128},{96,160},{128,192},{160,224},{192,256},{22... | collective-permute-start | bytes 1609736 | tf_op jit(solution)/shard_map/ppermute | solution.py:312
  45.2 20.3 %collective-permute-start.7 = (bf16[2096,128]{1,0:T(8,128)(2,1)S(1)}, bf16[2096,128]{1,0:T(8,128)(2,1)S(1)}, u32[]{:S(2)}, u32[]{:S(2)}) collective-permute-start(bf16[2096,128]{1,0:T(8,128)(2,1)S(1)} %get-tuple-element.9.refs_0_), channel_id=1, source_target_pairs={{0,31},{1,2},{2,1},{3,4},{4,3},{5,6},{6,5},{7,8},{8,7},{9,10},{10,... | collective-permute-start | bytes 1609736 | tf_op jit(solution)/shard_map/ppermute | solution.py:315
  48.7 16.9 %collective-permute-start.8 = (bf16[2096,128]{1,0:T(8,128)(2,1)S(1)}, bf16[2096,128]{1,0:T(8,128)(2,1)S(1)}, u32[]{:S(2)}, u32[]{:S(2)}) collective-permute-start(bf16[2096,128]{1,0:T(8,128)(2,1)S(1)} %get-tuple-element.9.refs_0_), channel_id=1, source_target_pairs={{0,1},{1,0},{2,3},{3,2},{4,5},{5,4},{6,7},{7,6},{8,9},{9,8},{10,11... | collective-permute-start | bytes 1609736 | tf_op jit(solution)/shard_map/ppermute | solution.py:315
  51.9 11.1 %collective-permute-start.3 = (bf16[1040,128]{1,0:T(8,128)(2,1)S(1)}, bf16[1040,128]{1,0:T(8,128)(2,1)S(1)}, u32[]{:S(2)}, u32[]{:S(2)}) collective-permute-start(bf16[1040,128]{1,0:T(8,128)(2,1)S(1)} %get-tuple-element.10), channel_id=1, source_target_pairs={{0,448},{32,480},{64,0},{96,32},{128,64},{160,96},{192,128},{224,1... | collective-permute-start | bytes 798728 | tf_op jit(solution)/shard_map/ppermute | solution.py:312
  55.8 9.8 %collective-permute-start.4 = (bf16[1040,128]{1,0:T(8,128)(2,1)S(1)}, bf16[1040,128]{1,0:T(8,128)(2,1)S(1)}, u32[]{:S(2)}, u32[]{:S(2)}) collective-permute-start(bf16[1040,128]{1,0:T(8,128)(2,1)S(1)} %slice.12), channel_id=1, source_target_pairs={{0,32},{32,0},{64,96},{96,64},{128,160},{160,128},{192,224},{224,1... | collective-permute-start | bytes 798728 | tf_op jit(solution)/shard_map/ppermute | solution.py:346
  61.1 4.5 %collective-permute-start.6 = (bf16[2096,128]{1,0:T(8,128)(2,1)S(1)}, bf16[2096,128]{1,0:T(8,128)(2,1)S(1)}, u32[]{:S(2)}, u32[]{:S(2)}) collective-permute-start(bf16[2096,128]{1,0:T(8,128)(2,1)S(1)} %pad_maximum_fusion), channel_id=1, source_target_pairs={{0,32},{32,0},{64,96},{96,64},{128,160},{160,128},{192,224},{224,1... | collective-permute-start | bytes 1609736 | tf_op jit(solution)/shard_map/ppermute | solution.py:347
  63.1 4.8 %collective-permute-start.9 = (bf16[2080,128]{1,0:T(8,128)(2,1)S(1)}, bf16[2080,128]{1,0:T(8,128)(2,1)S(1)}, u32[]{:S(2)}, u32[]{:S(2)}) collective-permute-start(bf16[2080,128]{1,0:T(8,128)(2,1)S(1)} %pad_maximum_fusion.1), channel_id=1, source_target_pairs={{0,32},{32,0},{64,96},{96,64},{128,160},{160,128},{192,224},{224,1... | collective-permute-start | bytes 1597448 | tf_op jit(solution)/shard_map/ppermute | solution.py:348
